TPU v7x, 32 devices: a whole 2x2x4 slice. The times are simulated.
32 devices in a mesh: ctx: 8 (over y, x, core), fsdp: 4 (over z).
Axes of the slice: x: 2, y: 2, z: 4, core: 2. Of those that a mesh axis runs over, the one named last changes fastest.
Arguments:
- tokens: bfloat16 [4096, 2048], P(('ctx', 'fsdp')), may hold values from -6 to 6
- cotangent: bfloat16 [4096, 2048], P(('ctx', 'fsdp')), may hold values from -6 to 6
- gain_attn: float32 [2048], replicated, may hold values from 0.25 to 1.75
- gain_ffn: float32 [2048], replicated, may hold values from 0.25 to 1.75
- query_key_value_weight: bfloat16 [2048, 4096], P('fsdp'), may hold values from -0.125 to 0.125
- w_out: bfloat16 [2048, 2048], P('fsdp'), may hold values from -1 to 1
- w_gate: bfloat16 [2048, 8192], P('fsdp'), may hold values from -0.125 to 0.125
- w_up: bfloat16 [2048, 8192], P('fsdp'), may hold values from -0.125 to 0.125
- w_down: bfloat16 [8192, 2048], P('fsdp'), may hold values from -0.0625 to 0.0625
- pair_block: int32 [8], replicated, may hold values from 0 to 7, each once
Outputs:
- result: bfloat16 [4096, 2048], P(('ctx', 'fsdp'))
- grad_input: float32 [4096, 2048], P(('ctx', 'fsdp'))
- grad_gain_attn: float32 [2048], P(('ctx', 'fsdp'))
- grad_gain_ffn: float32 [2048], P(('ctx', 'fsdp'))
- grad_qkv: float32 [2048, 4096], P(('fsdp', 'ctx'))
- grad_out: float32 [2048, 2048], P(('fsdp', 'ctx'))
- grad_gate: float32 [2048, 8192], P(('fsdp', 'ctx'))
- grad_up: float32 [2048, 8192], P(('fsdp', 'ctx'))
- grad_down: float32 [8192, 2048], P(('fsdp', 'ctx'))
Inputs may be any that keep to these rules, and one draw needn't show every extreme that they name: Ctx index c holds the blocks pair_block[c] and 15 - pair_block[c] of 64 tokens each of every sequence; every value appears once.
All inputs are finite; a program needn't handle non-finite values.
Results may differ from a plain program's by a relative error of at most 0.02.
Values may be sent and summed in bfloat16 or wider, within the bound.
A program may use at most 448 MiB of HBM per device.

v0:
```python
import math

import jax
import jax.numpy as jnp
from jax import lax
from jax.sharding import PartitionSpec as P

QUERY_HEADS = 16
KEY_VALUE_HEADS = 8
HEAD_SIZE = 128


norm_eps = 1e-05
rope_base = 1000000.0


def rms_norm(vectors, gain_vec):
    return (
        vectors
        * lax.rsqrt(jnp.mean(vectors * vectors, axis=-1, keepdims=True) + norm_eps)
        * gain_vec
    )


def apply_rotation(vectors, where_pos):
    half_dim = vectors.shape[-1] // 2
    frequency = jnp.exp(
        jnp.arange(half_dim, dtype=jnp.float32) * (-2.0 * math.log(rope_base) / vectors.shape[-1])
    )
    angles = where_pos.astype(jnp.float32)[:, None] * frequency[None, :]
    cosine = jnp.cos(angles)[:, None, :]
    sine_val = jnp.sin(angles)[:, None, :]
    first_half = vectors[..., :half_dim]
    second_half = vectors[..., half_dim:]
    return jnp.concatenate(
        [
            first_half * cosine - second_half * sine_val,
            second_half * cosine + first_half * sine_val,
        ],
        axis=-1,
    )


def positions(pair_block, token_rows):
    n_ctx = lax.axis_size("ctx")
    half_rows = token_rows // 2
    row_index = jnp.arange(token_rows, dtype=jnp.int32)
    first_block = pair_block[:, None]
    which_block = jnp.where(
        row_index[None, :] < half_rows, first_block, 2 * n_ctx - 1 - first_block
    )
    pos_table = which_block * half_rows + (row_index % half_rows)[None, :]
    own_pos = lax.dynamic_slice(pos_table, (lax.axis_index("ctx"), 0), (1, token_rows)).reshape(
        token_rows
    )
    return (pos_table.reshape(-1), own_pos)


def to_groups(input_array, group_count):
    token_rows = input_array.shape[0]
    head_length = input_array.shape[-1] // (group_count * KEY_VALUE_HEADS)
    return (
        input_array.reshape(token_rows, KEY_VALUE_HEADS, group_count, head_length)
        .transpose(1, 2, 0, 3)
        .reshape(KEY_VALUE_HEADS, group_count * token_rows, head_length)
    )


def from_groups(input_array, group_count):
    head_length = input_array.shape[-1]
    token_rows = input_array.shape[1] // group_count
    return (
        input_array.reshape(KEY_VALUE_HEADS, group_count, token_rows, head_length)
        .transpose(2, 0, 1, 3)
        .reshape(token_rows, KEY_VALUE_HEADS * group_count * head_length)
    )


def split_keys(every_key, every_value, key_pos):
    total_keys = every_key.shape[0]
    block_length = min(1024, total_keys)
    block_count = total_keys // block_length
    return (
        every_key.reshape(block_count, block_length, KEY_VALUE_HEADS, HEAD_SIZE),
        every_value.reshape(block_count, block_length, KEY_VALUE_HEADS, HEAD_SIZE),
        key_pos.reshape(block_count, block_length),
    )


def contract_last(left, right):
    return lax.dot_general(
        left, right, (((1,), (1,)), ((), ())), preferred_element_type=jnp.float32
    )


def contract_first(left, right):
    return lax.dot_general(
        left, right, (((0,), (0,)), ((), ())), preferred_element_type=jnp.float32
    )


def local(
    tokens,
    cotangent,
    gain_attn,
    gain_ffn,
    query_key_value_weight,
    w_out,
    w_gate,
    w_up,
    w_down,
    pair_block,
):
    token_rows = tokens.shape[0]
    query_columns = QUERY_HEADS * HEAD_SIZE
    key_value_columns = KEY_VALUE_HEADS * HEAD_SIZE
    group_count = QUERY_HEADS // KEY_VALUE_HEADS
    score_scale = 1.0 / math.sqrt(HEAD_SIZE)
    ff_cols = w_gate.shape[1]
    key_pos, own_pos = positions(pair_block, token_rows)
    query_pos = jnp.tile(own_pos, group_count)
    inputs_f = tokens.astype(jnp.float32)
    qkv_full, out_full = (
        lax.all_gather(query_key_value_weight, "fsdp", axis=0, tiled=True),
        lax.all_gather(w_out, "fsdp", axis=0, tiled=True),
    )
    normed_one_b = rms_norm(inputs_f, gain_attn).astype(jnp.bfloat16)
    projected_rows = jnp.dot(normed_one_b, qkv_full, preferred_element_type=jnp.float32)
    query_raw = projected_rows[:, :query_columns].reshape(token_rows, QUERY_HEADS, HEAD_SIZE)
    unrotated_key = projected_rows[:, query_columns : query_columns + key_value_columns].reshape(
        token_rows, KEY_VALUE_HEADS, HEAD_SIZE
    )
    query_b = (
        apply_rotation(query_raw, own_pos).astype(jnp.bfloat16).reshape(token_rows, query_columns)
    )
    keys_b = (
        apply_rotation(unrotated_key, own_pos)
        .astype(jnp.bfloat16)
        .reshape(token_rows, key_value_columns)
    )
    values_b = projected_rows[:, query_columns + key_value_columns :].astype(jnp.bfloat16)
    every_key, every_value = (
        lax.all_gather(keys_b, "ctx", axis=0, tiled=True),
        lax.all_gather(values_b, "ctx", axis=0, tiled=True),
    )
    query_grp = to_groups(query_b, group_count)
    key_blocks, value_blocks, pos_blocks = split_keys(every_key, every_value, key_pos)

    def forward_step(carry, block_in):
        run_max, run_total, weighted = carry
        key_block, value_block, block_pos = block_in
        causal = block_pos[None, None, :] <= query_pos[None, :, None]
        scores = (
            jnp.einsum("hqd,khd->hqk", query_grp, key_block, preferred_element_type=jnp.float32)
            * score_scale
        )
        scores = jnp.where(causal, scores, -1e30)
        new_max = jnp.maximum(run_max, jnp.max(scores, axis=-1))
        exp_scores = jnp.where(causal, jnp.exp(scores - new_max[..., None]), 0.0)
        fading = jnp.exp(run_max - new_max)
        run_total = run_total * fading + jnp.sum(exp_scores, axis=-1)
        weighted = weighted * fading[..., None] + jnp.einsum(
            "hqk,khd->hqd",
            exp_scores.astype(jnp.bfloat16),
            value_block,
            preferred_element_type=jnp.float32,
        )
        return ((new_max, run_total, weighted), None)

    initial_maximum = jnp.full((KEY_VALUE_HEADS, group_count * token_rows), -1e30, jnp.float32)
    initial_total = jnp.zeros((KEY_VALUE_HEADS, group_count * token_rows), jnp.float32)
    initial_weighted = jnp.zeros(
        (KEY_VALUE_HEADS, group_count * token_rows, HEAD_SIZE), jnp.float32
    )
    final_carry, ignored = lax.scan(
        forward_step,
        (initial_maximum, initial_total, initial_weighted),
        (key_blocks, value_blocks, pos_blocks),
    )
    run_max, run_total, weighted = final_carry
    log_total = run_max + jnp.log(run_total)
    attn_grp = weighted / run_total[..., None]
    attended_b = from_groups(attn_grp.astype(jnp.bfloat16), group_count)
    mid_rows = inputs_f + jnp.dot(attended_b, out_full, preferred_element_type=jnp.float32)
    gate_full, up_full, down_full = (
        lax.all_gather(w_gate, "fsdp", axis=0, tiled=True),
        lax.all_gather(w_up, "fsdp", axis=0, tiled=True),
        lax.all_gather(w_down, "fsdp", axis=0, tiled=True),
    )
    normed_two_b = rms_norm(mid_rows, gain_ffn).astype(jnp.bfloat16)
    gate_val = jnp.dot(normed_two_b, gate_full, preferred_element_type=jnp.float32)
    up_val = jnp.dot(normed_two_b, up_full, preferred_element_type=jnp.float32)
    hidden_b = (jax.nn.silu(gate_val) * up_val).astype(jnp.bfloat16)
    output_f = mid_rows + jnp.dot(hidden_b, down_full, preferred_element_type=jnp.float32)
    result = output_f.astype(jnp.bfloat16)
    normed_one_x, attended_x, normed_two_x, hidden_x = (
        lax.all_to_all(normed_one_b, "fsdp", split_axis=1, concat_axis=0, tiled=True),
        lax.all_to_all(attended_b, "fsdp", split_axis=1, concat_axis=0, tiled=True),
        lax.all_to_all(normed_two_b, "fsdp", split_axis=1, concat_axis=0, tiled=True),
        lax.all_to_all(hidden_b, "fsdp", split_axis=1, concat_axis=0, tiled=True),
    )
    grad_out_f = cotangent.astype(jnp.float32)
    gate_back, up_back, down_back = (
        lax.all_gather(w_gate, "fsdp", axis=0, tiled=True),
        lax.all_gather(w_up, "fsdp", axis=0, tiled=True),
        lax.all_gather(w_down, "fsdp", axis=0, tiled=True),
    )
    grad_hidden = contract_last(cotangent, down_back)
    ignored, ffn_back = jax.vjp(
        lambda gate_in, up_in: jax.nn.silu(gate_in) * up_in, gate_val, up_val
    )
    grad_gate_f, grad_up_f = ffn_back(grad_hidden)
    grad_gate_b = grad_gate_f.astype(jnp.bfloat16)
    grad_up_b = grad_up_f.astype(jnp.bfloat16)
    grad_normed_two = contract_last(grad_gate_b, gate_back) + contract_last(grad_up_b, up_back)
    ignored, norm_two_back = jax.vjp(rms_norm, mid_rows, gain_ffn)
    grad_mid_part, gain_ffn_part = norm_two_back(grad_normed_two)
    grad_mid = grad_out_f + grad_mid_part
    gate_up_b = jnp.concatenate([grad_gate_b, grad_up_b], axis=1)
    qkv_back, out_back = (
        lax.all_gather(query_key_value_weight, "fsdp", axis=0, tiled=True),
        lax.all_gather(w_out, "fsdp", axis=0, tiled=True),
    )
    grad_proj_b = grad_mid.astype(jnp.bfloat16)
    grad_att_b = contract_last(grad_proj_b, out_back).astype(jnp.bfloat16)
    grad_att_grp = to_groups(grad_att_b, group_count)
    delta_rows = jnp.sum(grad_att_grp.astype(jnp.float32) * attn_grp, axis=-1)

    def backward_step(grad_query, block_in):
        key_block, value_block, block_pos = block_in
        causal = block_pos[None, None, :] <= query_pos[None, :, None]
        scores = (
            jnp.einsum("hqd,khd->hqk", query_grp, key_block, preferred_element_type=jnp.float32)
            * score_scale
        )
        probs = jnp.where(causal, jnp.exp(scores - log_total[..., None]), 0.0)
        grad_values = jnp.einsum(
            "hqk,hqd->khd",
            probs.astype(jnp.bfloat16),
            grad_att_grp,
            preferred_element_type=jnp.float32,
        )
        grad_probs = jnp.einsum(
            "hqd,khd->hqk", grad_att_grp, value_block, preferred_element_type=jnp.float32
        )
        grad_scores = (probs * (grad_probs - delta_rows[..., None])).astype(jnp.bfloat16)
        grad_query = grad_query + score_scale * jnp.einsum(
            "hqk,khd->hqd", grad_scores, key_block, preferred_element_type=jnp.float32
        )
        grad_keys = score_scale * jnp.einsum(
            "hqk,hqd->khd", grad_scores, query_grp, preferred_element_type=jnp.float32
        )
        return (grad_query, (grad_keys, grad_values))

    grad_query_grp, key_grads = lax.scan(
        backward_step,
        jnp.zeros((KEY_VALUE_HEADS, group_count * token_rows, HEAD_SIZE), jnp.float32),
        (key_blocks, value_blocks, pos_blocks),
    )
    total_keys = key_pos.shape[0]
    grad_keys_all = key_grads[0].reshape(total_keys, key_value_columns)
    grad_values_all = key_grads[1].reshape(total_keys, key_value_columns)
    key_sums, summed_values = (
        lax.psum_scatter(
            grad_keys_all.astype(jnp.bfloat16), "ctx", scatter_dimension=0, tiled=True
        ).astype(jnp.float32),
        lax.psum_scatter(
            grad_values_all.astype(jnp.bfloat16), "ctx", scatter_dimension=0, tiled=True
        ).astype(jnp.float32),
    )
    grad_query_rows = from_groups(grad_query_grp, group_count).reshape(
        token_rows, QUERY_HEADS, HEAD_SIZE
    )
    ignored, query_rope_back = jax.vjp(lambda vectors: apply_rotation(vectors, own_pos), query_raw)
    ignored, key_rotation_backward = jax.vjp(
        lambda vectors: apply_rotation(vectors, own_pos), unrotated_key
    )
    grad_query_raw = query_rope_back(grad_query_rows)[0]
    unrotated_key_gradient = key_rotation_backward(
        key_sums.reshape(token_rows, KEY_VALUE_HEADS, HEAD_SIZE)
    )[0]
    grad_projected_b = jnp.concatenate(
        [
            grad_query_raw.reshape(token_rows, query_columns),
            unrotated_key_gradient.reshape(token_rows, key_value_columns),
            summed_values,
        ],
        axis=1,
    ).astype(jnp.bfloat16)
    grad_normed_one = contract_last(grad_projected_b, qkv_back)
    ignored, norm_one_back = jax.vjp(rms_norm, inputs_f, gain_attn)
    grad_in_part, gain_attn_part = norm_one_back(grad_normed_one)
    grad_input = grad_mid + grad_in_part
    cot_group, gate_up_group, projected_group, proj_group = (
        lax.all_gather(cotangent, "fsdp", axis=0, tiled=True),
        lax.all_gather(gate_up_b, "fsdp", axis=0, tiled=True),
        lax.all_gather(grad_projected_b, "fsdp", axis=0, tiled=True),
        lax.all_gather(grad_proj_b, "fsdp", axis=0, tiled=True),
    )
    qkv_part = contract_first(normed_one_x, projected_group)
    out_part = contract_first(attended_x, proj_group)
    gate_up_part = contract_first(normed_two_x, gate_up_group)
    gate_part = gate_up_part[:, :ff_cols]
    up_part = gate_up_part[:, ff_cols:]
    down_part = contract_first(hidden_x, cot_group)
    grad_qkv, grad_out, grad_down = (
        lax.psum_scatter(
            qkv_part.astype(jnp.bfloat16), "ctx", scatter_dimension=0, tiled=True
        ).astype(jnp.float32),
        lax.psum_scatter(
            out_part.astype(jnp.bfloat16), "ctx", scatter_dimension=0, tiled=True
        ).astype(jnp.float32),
        lax.psum_scatter(
            down_part.astype(jnp.bfloat16), "ctx", scatter_dimension=0, tiled=True
        ).astype(jnp.float32),
    )
    grad_gate, grad_up = (
        lax.psum_scatter(
            gate_part.astype(jnp.bfloat16), "ctx", scatter_dimension=0, tiled=True
        ).astype(jnp.float32),
        lax.psum_scatter(
            up_part.astype(jnp.bfloat16), "ctx", scatter_dimension=0, tiled=True
        ).astype(jnp.float32),
    )
    grad_gain_attn, grad_gain_ffn = (
        lax.psum_scatter(gain_attn_part, ("ctx", "fsdp"), scatter_dimension=0, tiled=True),
        lax.psum_scatter(gain_ffn_part, ("ctx", "fsdp"), scatter_dimension=0, tiled=True),
    )
    return (
        result,
        grad_input,
        grad_gain_attn,
        grad_gain_ffn,
        grad_qkv,
        grad_out,
        grad_gate,
        grad_up,
        grad_down,
    )


def solution(mesh):
    return jax.shard_map(
        local,
        mesh=mesh,
        in_specs=(
            P(("ctx", "fsdp"), None),
            P(("ctx", "fsdp"), None),
            P(),
            P(),
            P("fsdp", None),
            P("fsdp", None),
            P("fsdp", None),
            P("fsdp", None),
            P("fsdp", None),
            P(),
        ),
        out_specs=(
            P(("ctx", "fsdp"), None),
            P(("ctx", "fsdp"), None),
            P(("ctx", "fsdp")),
            P(("ctx", "fsdp")),
            P(("fsdp", "ctx"), None),
            P(("fsdp", "ctx"), None),
            P(("fsdp", "ctx"), None),
            P(("fsdp", "ctx"), None),
            P(("fsdp", "ctx"), None),
        ),
        check_vma=False,
    )
```

profile of v0, /device:TPU:5, one launch (start us, length us, event | category | flops | bytes accessed | tf_op | source)
XLA Modules:
  0.0 3228.2 jit_solution(3136313809291606934)
XLA Ops:
  9.0 288.9 %all-gather.12.cloned.1.call-done = bf16[2048,4096]{1,0:T(8,128)(2,1)} async-done(((bf16[512,4096]{1,0:T(8,128)(2,1)}), bf16[2048,4096]{1,0:T(8,128)(2,1)}) %all-gather.12.cloned.1.call-update) | async-done | bytes 16777232 | tf_op jit(solution)/shard_map/all_gather | solution.py:124
  316.1 19.1 all-gather.14.cloned.1.call-done
  342.5 23.3 all-gather.16.cloned.1.call-done
  373.1 143.8 %all-gather.18.cloned.1.call-done = bf16[2048,2048]{1,0:T(8,128)(2,1)} async-done(((bf16[512,2048]{1,0:T(8,128)(2,1)}), bf16[2048,2048]{1,0:T(8,128)(2,1)}) %all-gather.18.cloned.1.call-update) | async-done | bytes 8388624 | tf_op jit(solution)/shard_map/all_gather | solution.py:125
  521.8 556.1 %all-gather.20.cloned.1.call-done = bf16[2048,8192]{1,0:T(8,128)(2,1)} async-done(((bf16[512,8192]{1,0:T(8,128)(2,1)}), bf16[2048,8192]{1,0:T(8,128)(2,1)}) %all-gather.20.cloned.1.call-update) | async-done | bytes 33554448 | tf_op jit(solution)/shard_map/all_gather | solution.py:186
  1077.9 20.8 fusion.57
  1098.7 540.2 %all-gather.22.cloned.1.call-done = bf16[2048,8192]{1,0:T(8,128)(2,1)} async-done(((bf16[512,8192]{1,0:T(8,128)(2,1)}), bf16[2048,8192]{1,0:T(8,128)(2,1)}) %all-gather.22.cloned.1.call-update) | async-done | bytes 33554448 | tf_op jit(solution)/shard_map/all_gather | solution.py:187
  1639.0 20.7 fusion.58
  1659.7 540.5 %all-gather.24.cloned.1.call-done = bf16[8192,2048]{1,0:T(8,128)(2,1)} async-done(((bf16[2048,2048]{1,0:T(8,128)(2,1)}), bf16[8192,2048]{1,0:T(8,128)(2,1)}) %all-gather.24.cloned.1.call-update) | async-done | bytes 33554448 | tf_op jit(solution)/shard_map/all_gather | solution.py:188
  2200.1 20.4 multiply_convert_fusion.2
  2237.4 17.5 multiply_reduce_fusion
  2301.9 20.5 reduce-scatter.22.cloned.1.call-done
  2330.5 36.8 %reduce-scatter.24.cloned.1.call-done = bf16[128,1024]{1,0:T(8,128)(2,1)} async-done(((bf16[1024,1024]{1,0:T(8,128)(2,1)}), bf16[128,1024]{1,0:T(8,128)(2,1)}) %reduce-scatter.24.cloned.1.call-update) | async-done | bytes 262160 | tf_op jit(solution)/shard_map/reduce_scatter | solution.py:267
  2379.0 27.6 all-to-all-done.1
  2412.3 33.1 %all-gather.28.cloned.1.call-done = bf16[512,2048]{1,0:T(8,128)(2,1)} async-done(((bf16[128,2048]{1,0:T(8,128)(2,1)}), bf16[512,2048]{1,0:T(8,128)(2,1)}) %all-gather.28.cloned.1.call-update) | async-done | bytes 2097168 | tf_op jit(solution)/shard_map/all_gather | solution.py:298
  2449.8 55.9 %all-gather.32.cloned.1.call-done = bf16[512,2048]{1,0:T(8,128)(2,1)} async-done(((bf16[128,2048]{1,0:T(8,128)(2,1)}), bf16[512,2048]{1,0:T(8,128)(2,1)}) %all-gather.32.cloned.1.call-update) | async-done | bytes 2097168 | tf_op jit(solution)/shard_map/all_gather | solution.py:295
  2520.3 28.0 all-to-all-done
  2552.1 56.5 %all-gather.26.cloned.1.call-done = bf16[512,4096]{1,0:T(8,128)(2,1)} async-done(((bf16[128,4096]{1,0:T(8,128)(2,1)}), bf16[512,4096]{1,0:T(8,128)(2,1)}) %all-gather.26.cloned.1.call-update) | async-done | bytes 4194320 | tf_op jit(solution)/shard_map/all_gather | solution.py:297
  2615.4 280.3 %all-gather.30.cloned.1.call-done = bf16[512,16384]{1,0:T(8,128)(2,1)} async-done(((bf16[128,16384]{1,0:T(8,128)(2,1)}), bf16[512,16384]{1,0:T(8,128)(2,1)}) %all-gather.30.cloned.1.call-update) | async-done | bytes 16777232 | tf_op jit(solution)/shard_map/all_gather | solution.py:296
  2895.6 18.1 convolution_convert_fusion
  2956.6 37.1 %all-reduce.6 = (f32[2048]{0:T(1024)S(1)}, f32[2048]{0:T(1024)S(1)}) all-reduce(f32[2048]{0:T(1024)S(1)} %get-tuple-element.62, f32[2048]{0:T(1024)S(1)} %get-tuple-element.60), channel_id=4, replica_groups=mesh['ctx'=8,'fsdp'=4] {'ctx','fsdp'}, use_global_device_ids=true, to_apply=%region_10.11.clone | all-reduce | flops 4096 | bytes 32768
  3016.9 51.8 %reduce-scatter.12.cloned.1.call-done = bf16[64,4096]{1,0:T(8,128)(2,1)} async-done(((bf16[512,4096]{1,0:T(8,128)(2,1)}), bf16[64,4096]{1,0:T(8,128)(2,1)}) %reduce-scatter.12.cloned.1.call-update) | async-done | bytes 524304 | tf_op jit(solution)/shard_map/reduce_scatter | solution.py:307
  3070.8 72.9 %reduce-scatter.16.cloned.1.call-done = bf16[64,8192]{1,0:T(8,128)(2,1)} async-done(((bf16[512,8192]{1,0:T(8,128)(2,1)}), bf16[64,8192]{1,0:T(8,128)(2,1)}) %reduce-scatter.16.cloned.1.call-update) | async-done | bytes 1048592 | tf_op jit(solution)/shard_map/reduce_scatter | solution.py:318
  3146.4 71.9 %reduce-scatter.18.cloned.1.call-done = bf16[64,8192]{1,0:T(8,128)(2,1)} async-done(((bf16[512,8192]{1,0:T(8,128)(2,1)}), bf16[64,8192]{1,0:T(8,128)(2,1)}) %reduce-scatter.18.cloned.1.call-update) | async-done | bytes 1048592 | tf_op jit(solution)/shard_map/reduce_scatter | solution.py:321
  (189 shorter events, 231.1 us)
Async XLA Ops:
  7.2 290.6 %all-gather.12.cloned.1.call-start = ((), (), s32[]{:S(2)}) async-start(), calls=%async_computation.11 | async-start | bytes 20971520 | tf_op jit(solution)/shard_map/all_gather | solution.py:124
  7.9 327.3 %all-gather.14.cloned.1.call-start = ((), (), s32[]{:S(2)}) async-start(), calls=%async_computation.12 | async-start | bytes 2359296 | tf_op jit(solution)/shard_map/all_gather | solution.py:143
  308.8 57.1 %all-gather.16.cloned.1.call-start = ((), (), s32[]{:S(2)}) async-start(), calls=%async_computation.13 | async-start | bytes 2359296 | tf_op jit(solution)/shard_map/all_gather | solution.py:144
  310.6 206.2 %all-gather.18.cloned.1.call-start = ((), (), s32[]{:S(2)}) async-start(), calls=%async_computation.14 | async-start | bytes 10485760 | tf_op jit(solution)/shard_map/all_gather | solution.py:125
  311.2 766.7 %all-gather.20.cloned.1.call-start = ((), (), s32[]{:S(2)}) async-start(), calls=%async_computation.15 | async-start | bytes 41943040 | tf_op jit(solution)/shard_map/all_gather | solution.py:186
  311.8 1327.1 %all-gather.22.cloned.1.call-start = ((), (), s32[]{:S(2)}) async-start(), calls=%async_computation.16 | async-start | bytes 41943040 | tf_op jit(solution)/shard_map/all_gather | solution.py:187
  312.4 1887.8 %all-gather.24.cloned.1.call-start = ((), (), s32[]{:S(2)}) async-start(), calls=%async_computation.17 | async-start | bytes 41943040 | tf_op jit(solution)/shard_map/all_gather | solution.py:188
  313.1 2009.2 %reduce-scatter.22.cloned.1.call-start = ((), (), s32[]{:S(2)}) async-start(), calls=%async_computation.27 | async-start | bytes 2359296
  521.6 577.2 %copy-start.28 = (f32[128]{0:T(128)}, f32[128]{0:T(128)S(1)}, u32[]{:S(2)}) copy-start(f32[128]{0:T(128)S(1)} %get-tuple-element.106) | copy-start | bytes 1540
  521.8 1117.2 %copy-start.6 = (bf16[128,2048]{1,0:T(8,128)(2,1)}, bf16[128,2048]{1,0:T(8,128)(2,1)S(1)}, u32[]{:S(2)}) copy-start(bf16[128,2048]{1,0:T(8,128)(2,1)S(1)} %multiply_convert_fusion.4) | copy-start | bytes 1572868
  2283.1 84.2 %reduce-scatter.24.cloned.1.call-start = ((), (), s32[]{:S(2)}) async-start(), calls=%async_computation.28 | async-start | bytes 2359296 | tf_op jit(solution)/shard_map/reduce_scatter | solution.py:267
  2293.9 151.5 %all-gather.28.cloned.1.call-start = ((), (), s32[]{:S(2)}) async-start(), calls=%async_computation.20 | async-start | bytes 2621440 | tf_op jit(solution)/shard_map/all_gather | solution.py:298
  2294.5 211.2 %all-gather.32.cloned.1.call-start = ((), (), s32[]{:S(2)}) async-start(), calls=%async_computation.25 | async-start | bytes 2621440 | tf_op jit(solution)/shard_map/all_gather | solution.py:295
  2295.2 313.4 %all-gather.26.cloned.1.call-start = ((), (), s32[]{:S(2)}) async-start(), calls=%async_computation.18 | async-start | bytes 5242880 | tf_op jit(solution)/shard_map/all_gather | solution.py:297
  2369.0 526.7 %all-gather.30.cloned.1.call-start = ((), (), s32[]{:S(2)}) async-start(), calls=%async_computation.22 | async-start | bytes 20971520 | tf_op jit(solution)/shard_map/all_gather | solution.py:296
  2373.0 33.5 %all-to-all-start.1 = ((bf16[128,4,512]{0,2,1:T(8,128)(2,1)}), bf16[128,4,512]{0,2,1:T(8,128)(2,1)}, u32[]{:S(2)}, u32[]{:S(2)}) async-start(bf16[128,4,512]{0,2,1:T(8,128)(2,1)} %bitcast.134), calls=%async_computation.2 | async-start | bytes 1048576 | tf_op jit(solution)/shard_map/all_to_all | solution.py:198
  2406.6 99.1 %all-to-all-start.3 = ((bf16[128,4,2048]{2,0,1:T(8,128)(2,1)}), bf16[128,4,2048]{2,0,1:T(8,128)(2,1)S(1)}, u32[]{:S(2)}, u32[]{:S(2)}) async-start(bf16[128,4,2048]{2,0,1:T(8,128)(2,1)} %bitcast.131), calls=%async_computation.7 | async-start | bytes 4194304 | tf_op jit(solution)/shard_map/all_to_all | solution.py:200
  2410.2 587.5 %reduce-scatter.14.cloned.1.call-start = ((), (), s32[]{:S(2)}) async-start(), calls=%async_computation.21 | async-start | bytes 2359296 | tf_op jit(solution)/shard_map/reduce_scatter | solution.py:310
  2449.8 564.4 %reduce-scatter.20.cloned.1.call-start = ((), (), s32[]{:S(2)}) async-start(), calls=%async_computation.26 | async-start | bytes 9437184 | tf_op jit(solution)/shard_map/reduce_scatter | solution.py:313
  2516.0 32.4 %all-to-all-start = ((bf16[128,4,512]{2,0,1:T(8,128)(2,1)}), bf16[128,4,512]{2,0,1:T(8,128)(2,1)S(1)}, u32[]{:S(2)}, u32[]{:S(2)}) async-start(bf16[128,4,512]{2,0,1:T(8,128)(2,1)} %bitcast.126), calls=%async_computation | async-start | bytes 1048576 | tf_op jit(solution)/shard_map/all_to_all | solution.py:197
  2548.3 67.0 %all-to-all-start.2 = ((bf16[128,4,512]{2,0,1:T(8,128)(2,1)}), bf16[128,4,512]{2,0,1:T(8,128)(2,1)S(1)}, u32[]{:S(2)}, u32[]{:S(2)}) async-start(bf16[128,4,512]{2,0,1:T(8,128)(2,1)} %bitcast.125), calls=%async_computation.4 | async-start | bytes 1048576 | tf_op jit(solution)/shard_map/all_to_all | solution.py:199
  2551.8 516.9 %reduce-scatter.12.cloned.1.call-start = ((), (), s32[]{:S(2)}) async-start(), calls=%async_computation.19 | async-start | bytes 4718592 | tf_op jit(solution)/shard_map/reduce_scatter | solution.py:307
  2615.3 528.4 %reduce-scatter.16.cloned.1.call-start = ((), (), s32[]{:S(2)}) async-start(), calls=%async_computation.23 | async-start | bytes 9437184 | tf_op jit(solution)/shard_map/reduce_scatter | solution.py:318
  2925.5 292.7 %reduce-scatter.18.cloned.1.call-start = ((), (), s32[]{:S(2)}) async-start(), calls=%async_computation.24 | async-start | bytes 9437184 | tf_op jit(solution)/shard_map/reduce_scatter | solution.py:321
  (31 other events, 2030.3 us)
Sparse Core Ops, SparseCore 0:
  9.6 288.1 all-gather.11
  308.9 26.2 all-gather.13
  337.7 28.1 all-gather.15
  367.3 149.5 all-gather.17
  518.2 559.6 all-gather.19
  1079.3 559.5 all-gather.21
  1640.5 559.5 all-gather.23
  2283.2 39.1 reduce-scatter.21
  2326.0 41.2 reduce-scatter.23
  2369.3 76.0 all-gather.27
  2447.0 58.6 all-gather.31
  2507.7 100.8 all-gather.25
  2610.2 285.4 all-gather.29
  2899.4 39.1 reduce-scatter.13
  2942.3 71.8 reduce-scatter.19
  3017.3 51.3 reduce-scatter.11
  3072.4 71.2 reduce-scatter.15
  3147.0 71.2 reduce-scatter.17
where the time goes:
time: 3240 us; the launch traced here: 3230 us
  waiting for transfers between devices  2870 us (89%)
  matrix products  215 us (7%)
  local copies, waits for them, and re-layouts  48.2 us (1%)
  blocking collectives  37.1 us (1%)
    all_gather x1, waiting for transfers between devices, local(): lax.all_gather(w_gate, 'fsdp', axis=0, tiled=True)  556 us
    all_gather x1, waiting for transfers between devices, local(): lax.all_gather(w_down, 'fsdp', axis=0, tiled=True)  540 us
    all_gather x1, waiting for transfers between devices, local(): lax.all_gather(w_up, 'fsdp', axis=0, tiled=True)  540 us
    all_gather x1, waiting for transfers between devices, local(): lax.all_gather(query_key_value_weight, 'fsdp', axis=0, tiled=True)  289 us
    all_gather x1, waiting for transfers between devices, local(): lax.all_gather(gate_up_b, 'fsdp', axis=0, tiled=True)  280 us
    all_gather x1, waiting for transfers between devices, local(): lax.all_gather(w_out, 'fsdp', axis=0, tiled=True)  144 us
    dot_general x5, matrix products, contract_last(): lax.dot_general(left, right, (((1,), (1,)), ((), ())), preferred_element_...  75.7 us
    reduce_scatter x1, waiting for transfers between devices, local(): lax.psum_scatter(gate_part.astype(jnp.bfloat16), 'ctx', scatter_dimension...  72.9 us
  transfers between devices with their start and end apart: 22, of which 19 were waited for; matrix products, arithmetic and copies ran while one was open for 6% of the time, Pallas kernels for 0%

commit v1 on v0

--- a/solution.py
+++ b/solution.py
@@ -99,7 +99,7 @@
     )
 
 
-def local(
+def local_general(
     tokens,
     cotangent,
     gain_attn,
@@ -339,7 +339,250 @@
     )
 
 
+def rotate_heads(vectors, cosine, sine_val, sign):
+    half_dim = HEAD_SIZE // 2
+    first_half = vectors[..., :half_dim]
+    second_half = vectors[..., half_dim:]
+    return jnp.concatenate(
+        [
+            first_half * cosine - sign * second_half * sine_val,
+            second_half * cosine + sign * first_half * sine_val,
+        ],
+        axis=-1,
+    )
+
+
+def local_heads(
+    tokens,
+    cotangent,
+    gain_attn,
+    gain_ffn,
+    query_key_value_weight,
+    w_out,
+    w_gate,
+    w_up,
+    w_down,
+    pair_block,
+):
+    f32, bf16 = jnp.float32, jnp.bfloat16
+    n_ctx, n_fsdp = lax.axis_size("ctx"), lax.axis_size("fsdp")
+    ctx, fsdp = lax.axis_index("ctx"), lax.axis_index("fsdp")
+    token_rows, width = tokens.shape
+    group_count = QUERY_HEADS // KEY_VALUE_HEADS
+    head_columns = group_count * HEAD_SIZE
+    query_columns = QUERY_HEADS * HEAD_SIZE
+    key_columns = KEY_VALUE_HEADS * HEAD_SIZE
+    score_scale = 1.0 / math.sqrt(HEAD_SIZE)
+    depth = query_key_value_weight.shape[0]
+    hidden_cols = w_down.shape[0]
+    share = depth // head_columns
+    head = lax.rem(ctx + share * fsdp, n_ctx)
+    plane_of = lambda c, f: ((c + share * f) % n_ctx) // share
+
+    key_pos, own_pos = positions(pair_block, token_rows)
+
+    def head_columns_of(matrix, h):
+        return jnp.concatenate(
+            [
+                lax.dynamic_slice_in_dim(matrix, h * head_columns, head_columns, 1),
+                lax.dynamic_slice_in_dim(matrix, query_columns + h * HEAD_SIZE, HEAD_SIZE, 1),
+                lax.dynamic_slice_in_dim(
+                    matrix, query_columns + key_columns + h * HEAD_SIZE, HEAD_SIZE, 1
+                ),
+            ],
+            axis=1,
+        )
+
+    sends = jnp.stack(
+        [
+            head_columns_of(query_key_value_weight, lax.rem(ctx + share * f, n_ctx))
+            for f in range(n_fsdp)
+        ]
+    )
+    w_head = lax.all_to_all(sends, "fsdp", split_axis=0, concat_axis=0, tiled=True).reshape(
+        width, head_columns + 2 * HEAD_SIZE
+    )
+    out_block = lax.dynamic_slice_in_dim(
+        w_out, lax.rem(ctx, share) * head_columns, head_columns, 0
+    )
+    out_pairs = [
+        (c * n_fsdp + plane_of(c, f), c * n_fsdp + f) for c in range(n_ctx) for f in range(n_fsdp)
+    ]
+    out_head = lax.ppermute(out_block, ("ctx", "fsdp"), out_pairs)
+
+    def hidden_columns(matrix):
+        mine = lax.dynamic_index_in_dim(
+            matrix.reshape(depth, n_fsdp, n_ctx, hidden_cols // n_ctx), ctx, 2, keepdims=False
+        )
+        turned = lax.all_to_all(
+            mine.transpose(1, 0, 2), "fsdp", split_axis=0, concat_axis=0, tiled=True
+        ).reshape(width, hidden_cols // n_ctx)
+        return lax.all_gather(turned, "ctx", axis=1, tiled=True)
+
+    gate_w = hidden_columns(w_gate)
+    up_w = hidden_columns(w_up)
+    cot_group = lax.all_gather(cotangent, "fsdp", axis=0, tiled=True)
+
+    inputs_f = tokens.astype(f32)
+    normed_one_b = rms_norm(inputs_f, gain_attn).astype(bf16)
+    normed_one_seq = lax.all_gather(normed_one_b, "ctx", axis=0, tiled=True)
+    projected = jnp.dot(normed_one_seq, w_head, preferred_element_type=f32)
+    frequency = jnp.exp(
+        jnp.arange(HEAD_SIZE // 2, dtype=f32) * (-2.0 * math.log(rope_base) / HEAD_SIZE)
+    )
+    angles = key_pos.astype(f32)[:, None] * frequency[None, :]
+    cosine, sine_val = jnp.cos(angles), jnp.sin(angles)
+    heads = [
+        rotate_heads(projected[:, i * HEAD_SIZE : (i + 1) * HEAD_SIZE], cosine, sine_val, 1.0)
+        for i in range(group_count + 1)
+    ]
+    queries = jnp.stack(heads[:group_count]).astype(bf16)
+    keys = heads[group_count].astype(bf16)
+    values = projected[:, head_columns + HEAD_SIZE :].astype(bf16)
+    causal = key_pos[None, :] <= key_pos[:, None]
+    scores = jnp.einsum("gqd,kd->gqk", queries, keys, preferred_element_type=f32) * score_scale
+    scores = jnp.where(causal, scores, -1e30)
+    shifted = jnp.exp(scores - jnp.max(scores, axis=-1, keepdims=True))
+    probs = shifted / jnp.sum(shifted, axis=-1, keepdims=True)
+    probs_low = probs.astype(bf16)
+    attended = jnp.einsum("gqk,kd->qgd", probs_low, values, preferred_element_type=f32)
+    attended_b = attended.astype(bf16).reshape(-1, head_columns)
+    out_part = jnp.dot(attended_b, out_head, preferred_element_type=f32)
+    mid = inputs_f + lax.psum_scatter(
+        out_part.astype(bf16), "ctx", scatter_dimension=0, tiled=True
+    ).astype(f32)
+
+    mid_scale = lax.rsqrt(jnp.mean(mid * mid, axis=-1, keepdims=True) + norm_eps)
+    normed_two_b = (mid * mid_scale * gain_ffn).astype(bf16)
+    normed_two_group = lax.all_gather(normed_two_b, "fsdp", axis=0, tiled=True)
+    gate = jnp.dot(normed_two_group, gate_w, preferred_element_type=f32)
+    up = jnp.dot(normed_two_group, up_w, preferred_element_type=f32)
+    sig = jax.nn.sigmoid(gate)
+    silu = gate * sig
+    hidden_b = (silu * up).astype(bf16)
+    down_part = jnp.dot(hidden_b, w_down, preferred_element_type=f32)
+    grad_hidden = contract_last(cot_group, w_down)
+    grad_gate_b = (grad_hidden * up * sig * (1.0 + gate * (1.0 - sig))).astype(bf16)
+    grad_up_b = (grad_hidden * silu).astype(bf16)
+    normed_part = contract_last(grad_gate_b, gate_w) + contract_last(grad_up_b, up_w)
+    result = (
+        mid
+        + lax.psum_scatter(
+            down_part.astype(bf16), "fsdp", scatter_dimension=0, tiled=True
+        ).astype(f32)
+    ).astype(bf16)
+    grad_normed_two = lax.psum_scatter(
+        normed_part.astype(bf16), "fsdp", scatter_dimension=0, tiled=True
+    ).astype(f32)
+    u = grad_normed_two * gain_ffn
+    grad_mid = (
+        cotangent.astype(f32)
+        + mid_scale * u
+        - mid * mid_scale**3 * jnp.mean(u * mid, axis=-1, keepdims=True)
+    )
+
+    grad_down_part = contract_first(hidden_b, cot_group)
+    grad_gate_part = contract_first(normed_two_group, grad_gate_b)
+    grad_up_part = contract_first(normed_two_group, grad_up_b)
+    grad_down = lax.psum_scatter(
+        grad_down_part.astype(bf16), "ctx", scatter_dimension=0, tiled=True
+    ).astype(f32)
+
+    def spread(part):
+        blocks = part.astype(bf16).reshape(n_fsdp, n_ctx, depth // n_ctx, hidden_cols)
+        blocks = blocks.transpose(1, 0, 2, 3).reshape(width, hidden_cols)
+        mine = lax.psum_scatter(blocks, "ctx", scatter_dimension=0, tiled=True)
+        mine = mine.reshape(n_fsdp, depth // n_ctx, hidden_cols)
+        return lax.all_to_all(mine, "fsdp", split_axis=0, concat_axis=2, tiled=True).reshape(
+            depth // n_ctx, n_fsdp * hidden_cols
+        )
+
+    grad_gate, grad_up = spread(grad_gate_part).astype(f32), spread(grad_up_part).astype(f32)
+
+    grad_proj_b = grad_mid.astype(bf16)
+    grad_proj_seq = lax.all_gather(grad_proj_b, "ctx", axis=0, tiled=True)
+    grad_att = contract_last(grad_proj_seq, out_head).astype(bf16)
+    grad_att = grad_att.reshape(-1, group_count, HEAD_SIZE).transpose(1, 0, 2)
+    grad_out_part = contract_first(attended_b, grad_proj_seq)
+    grad_values = jnp.einsum("gqk,gqd->kd", probs_low, grad_att, preferred_element_type=f32)
+    grad_probs = jnp.einsum("gqd,kd->gqk", grad_att, values, preferred_element_type=f32)
+    delta = jnp.sum(grad_probs * probs, axis=-1, keepdims=True)
+    grad_scores = (probs * (grad_probs - delta)).astype(bf16)
+    grad_queries = score_scale * jnp.einsum(
+        "gqk,kd->gqd", grad_scores, keys, preferred_element_type=f32
+    )
+    grad_keys = score_scale * jnp.einsum(
+        "gqk,gqd->kd", grad_scores, queries, preferred_element_type=f32
+    )
+    grad_projected = jnp.concatenate(
+        [rotate_heads(grad_queries[g], cosine, sine_val, -1.0) for g in range(group_count)]
+        + [rotate_heads(grad_keys, cosine, sine_val, -1.0), grad_values],
+        axis=1,
+    ).astype(bf16)
+    normed_one_part = contract_last(grad_projected, w_head)
+    grad_normed_one = lax.psum_scatter(
+        normed_one_part.astype(bf16), "ctx", scatter_dimension=0, tiled=True
+    ).astype(f32)
+    in_scale = lax.rsqrt(jnp.mean(inputs_f * inputs_f, axis=-1, keepdims=True) + norm_eps)
+    u = grad_normed_one * gain_attn
+    grad_input = (
+        grad_mid
+        + in_scale * u
+        - inputs_f * in_scale**3 * jnp.mean(u * inputs_f, axis=-1, keepdims=True)
+    )
+
+    grad_head_part = contract_first(normed_one_seq, grad_projected).astype(bf16)
+    blocks = grad_head_part.reshape(n_fsdp, n_ctx, depth // n_ctx, -1).transpose(1, 0, 2, 3)
+    blocks = blocks.reshape(n_ctx * n_fsdp, depth // n_ctx, -1)
+    got = lax.all_to_all(blocks, ("ctx", "fsdp"), split_axis=0, concat_axis=0, tiled=True)
+    got = got.astype(f32)
+    sums = [
+        sum(got[((h - share * f) % n_ctx) * n_fsdp + f] for f in range(n_fsdp))
+        for h in range(KEY_VALUE_HEADS)
+    ]
+    grad_qkv = jnp.concatenate(
+        [s[:, :head_columns] for s in sums]
+        + [s[:, head_columns : head_columns + HEAD_SIZE] for s in sums]
+        + [s[:, head_columns + HEAD_SIZE :] for s in sums],
+        axis=1,
+    )
+    back_pairs = [(b, a) for a, b in out_pairs]
+    out_got = lax.ppermute(grad_out_part.astype(bf16), ("ctx", "fsdp"), back_pairs)
+    padded = lax.dynamic_update_slice_in_dim(
+        jnp.zeros((depth, width), bf16), out_got, lax.rem(ctx, share) * head_columns, 0
+    )
+    grad_out = lax.psum_scatter(padded, "ctx", scatter_dimension=0, tiled=True).astype(f32)
+
+    my_rows = ctx * (depth // n_ctx)
+    rows_of = lambda matrix: lax.dynamic_slice_in_dim(
+        matrix, my_rows, depth // n_ctx, 0
+    ).astype(f32)
+    attn_sum = jnp.sum(rows_of(query_key_value_weight) * grad_qkv, axis=1)
+    ffn_sum = jnp.sum(rows_of(w_gate) * grad_gate, axis=1) + jnp.sum(
+        rows_of(w_up) * grad_up, axis=1
+    )
+    gain_pairs = [
+        (c * n_fsdp + f, f * n_ctx + c) for c in range(n_ctx) for f in range(n_fsdp)
+    ]
+    moved = lax.ppermute(jnp.stack([attn_sum, ffn_sum]), ("ctx", "fsdp"), gain_pairs)
+    my_gain = (ctx * n_fsdp + fsdp) * (depth // n_ctx)
+    grad_gain_attn = moved[0] / lax.dynamic_slice_in_dim(gain_attn, my_gain, depth // n_ctx)
+    grad_gain_ffn = moved[1] / lax.dynamic_slice_in_dim(gain_ffn, my_gain, depth // n_ctx)
+    return (
+        result,
+        grad_input,
+        grad_gain_attn,
+        grad_gain_ffn,
+        grad_qkv,
+        grad_out,
+        grad_gate,
+        grad_up,
+        grad_down,
+    )
+
+
 def solution(mesh):
+    local = local_heads if mesh.shape["ctx"] == KEY_VALUE_HEADS else local_general
     return jax.shard_map(
         local,
         mesh=mesh,

time: 3240 us -> 908 us (0.28)
  waiting for transfers between devices: 2870 us -> 528 us
  matrix products: 215 us -> 143 us
    all_gather x11 -> x6, waiting for transfers between devices: 2540 us -> 155 us  [the longest x2 66.9 us: hidden_columns(): return lax.all_gather(turned, 'ctx', axis=1, tiled=True)]
    all_to_all x0 -> x2, blocking collectives: none -> 57.1 us  [hidden_columns(): lax.all_to_all(mine.transpose(1, 0, 2), 'fsdp', split_axis=0, concat_axis...]
    all_to_all x4, waiting for transfers between devices: 55.6 us -> 109 us  [the longest x1 63.2 us: local_heads(): lax.all_to_all(sends, 'fsdp', split_axis=0, concat_axis=0, tiled=True)]
    dot_general x11 -> x10, matrix products: 102 us -> 60.5 us  [the longest x1 10.7 us: local_heads(): up = jnp.dot(normed_two_group, up_w, preferred_element_type=f32)]
    unnamed x1 -> x0, blocking collectives: 37.1 us -> none
    dot_general x5, matrix products: 75.7 us -> 40.5 us  [contract_last(): lax.dot_general(left, right, (((1,), (1,)), ((), ())), preferred_element_...]
    ppermute x0 -> x3, waiting for transfers between devices: none -> 34.6 us  [the longest x1 29.5 us: local_heads(): lax.ppermute(grad_out_part.astype(bf16), ('ctx', 'fsdp'), back_pairs)]
    reduce_scatter x6 -> x8, waiting for transfers between devices: 248 us -> 229 us  [the longest x1 52.9 us: local_heads(): lax.psum_scatter(normed_one_part.astype(bf16), 'ctx', scatter_dimension=0...]
  transfers between devices with their start and end apart: 22 -> 21, of which waited for: 19 -> 15; matrix products, arithmetic and copies ran while one was open for 6% -> 22% of each run, Pallas kernels for 0% -> 0%
where the time goes in v1:
time: 908 us; the launch traced here: 895 us
  waiting for transfers between devices  528 us (58%)
  matrix products  143 us (16%)
  local copies, waits for them, and re-layouts  65.3 us (7%)
  blocking collectives  57.1 us (6%)
  other arithmetic  48.3 us (5%)
  starting transfers between devices  38.2 us (4%)
  between operations  15.1 us (2%)
    all_gather x2, waiting for transfers between devices, hidden_columns(): return lax.all_gather(turned, 'ctx', axis=1, tiled=True)  66.9 us
    all_to_all x1, waiting for transfers between devices, local_heads(): lax.all_to_all(sends, 'fsdp', split_axis=0, concat_axis=0, tiled=True)  63.2 us
    all_to_all x2, blocking collectives, hidden_columns(): lax.all_to_all(mine.transpose(1, 0, 2), 'fsdp', split_axis=0, concat_axis...  57.1 us
    reduce_scatter x1, waiting for transfers between devices, local_heads(): lax.psum_scatter(normed_one_part.astype(bf16), 'ctx', scatter_dimension=0...  52.9 us
    all_gather x1, waiting for transfers between devices, local_heads(): normed_two_group = lax.all_gather(normed_two_b, 'fsdp', axis=0, tiled=True)  48.8 us
    reduce_scatter x1, waiting for transfers between devices, local_heads(): lax.psum_scatter(down_part.astype(bf16), 'fsdp', scatter_dimension=0, til...  44.7 us
    reduce_scatter x2, waiting for transfers between devices, spread(): mine = lax.psum_scatter(blocks, 'ctx', scatter_dimension=0, tiled=True)  42.9 us
    reduce_scatter x1, waiting for transfers between devices, local_heads(): lax.psum_scatter(normed_part.astype(bf16), 'fsdp', scatter_dimension=0, t...  42.5 us
  transfers between devices with their start and end apart: 21, of which 15 were waited for; matrix products, arithmetic and copies ran while one was open for 22% of the time, Pallas kernels for 0%

profile of v1, /device:TPU:5, one launch (start us, length us, event | category | flops | bytes accessed | tf_op | source)
XLA Modules:
  0.0 895.4 jit_solution(15780134819397275049)
XLA Ops:
  27.6 63.2 %all-to-all-done = bf16[4,512,512]{2,1,0:T(8,128)(2,1)} async-done(((bf16[4,512,512]{2,1,0:T(8,128)(2,1)}), bf16[4,512,512]{2,1,0:T(8,128)(2,1)}, u32[]{:S(2)}, u32[]{:S(2)}) %all-to-all-start) | async-done | bytes 2097184 | tf_op jit(solution)/shard_map/all_to_all | solution.py:402
  117.9 11.7 %copy.42 = bf16[512,8192]{0,1:T(8,128)(2,1)} copy(bf16[512,8192]{1,0:T(8,128)(2,1)} %param.16) | data formatting | bytes 16777216 | tf_op args[6]
  129.5 12.1 %copy.44 = bf16[512,8192]{0,1:T(8,128)(2,1)} copy(bf16[512,8192]{1,0:T(8,128)(2,1)} %param.17) | data formatting | bytes 16777216 | tf_op args[7]
  144.7 29.2 %all_to_all.38 = bf16[4,512,256]{2,1,0:T(8,128)(2,1)} all-to-all(bf16[4,512,256]{2,1,0:T(8,128)(2,1)} %bitcast.170), channel_id=1, replica_groups=mesh['ctx'=8,'fsdp'=4] {'fsdp'}, dimensions={0} | all-to-all | bytes 2097152 | tf_op jit(solution)/shard_map/all_to_all | solution.py:417
  178.0 27.9 %all_to_all.39 = bf16[4,512,256]{2,1,0:T(8,128)(2,1)} all-to-all(bf16[4,512,256]{2,1,0:T(8,128)(2,1)S(1)} %bitcast.171), channel_id=1, replica_groups=mesh['ctx'=8,'fsdp'=4] {'fsdp'}, dimensions={0} | all-to-all | bytes 2097152 | tf_op jit(solution)/shard_map/all_to_all | solution.py:417
  206.8 21.8 %all-gather.13.cloned.1.call-done = bf16[2048,2048]{1,0:T(8,128)(2,1)} async-done(((bf16[2048,256]{1,0:T(8,128)(2,1)}), bf16[2048,2048]{1,0:T(8,128)(2,1)}) %all-gather.13.cloned.1.call-update) | async-done | bytes 8388624 | tf_op jit(solution)/shard_map/all_gather | solution.py:420
  228.6 48.8 %all-gather.9.cloned.1.call-done = bf16[512,2048]{1,0:T(8,128)(2,1)} async-done(((bf16[128,2048]{1,0:T(8,128)(2,1)}), bf16[512,2048]{1,0:T(8,128)(2,1)}) %all-gather.9.cloned.1.call-update) | async-done | bytes 2097168 | tf_op jit(solution)/shard_map/all_gather | solution.py:457
  277.4 10.7 %fusion.111 = f32[512,2048]{1,0:T(8,128)} fusion(bf16[512,2048]{1,0:T(8,128)(2,1)} %all-gather.9.cloned.1.call-done, bf16[2048,2048]{1,0:T(8,128)(2,1)} %all-gather.13.cloned.1.call-done), kind=kOutput, calls=%fused_computation.230 | convolution fusion | flops 4294967296 | bytes 14680064 | tf_op jit(solution)/shard_map/dot_general | solution.py:459
  288.1 45.1 %all-gather.11.cloned.1.call-done = bf16[2048,2048]{1,0:T(8,128)(2,1)} async-done(((bf16[2048,256]{1,0:T(8,128)(2,1)}), bf16[2048,2048]{1,0:T(8,128)(2,1)}) %all-gather.11.cloned.1.call-update) | async-done | bytes 8388624 | tf_op jit(solution)/shard_map/all_gather | solution.py:420
  333.2 9.4 %fusion.110 = f32[512,2048]{1,0:T(8,128)} fusion(bf16[512,2048]{1,0:T(8,128)(2,1)S(1)} %copy-done.29, bf16[2048,2048]{1,0:T(8,128)(2,1)} %all-gather.11.cloned.1.call-done), kind=kOutput, calls=%fused_computation.229 | convolution fusion | flops 4294967296 | bytes 14680064 | tf_op jit(solution)/shard_map/dot_general | solution.py:458
  342.6 38.8 %all-gather.15.cloned.1.call-done = bf16[512,2048]{1,0:T(8,128)(2,1)} async-done(((bf16[128,2048]{1,0:T(8,128)(2,1)}), bf16[512,2048]{1,0:T(8,128)(2,1)}) %all-gather.15.cloned.1.call-update) | async-done | bytes 2097168 | tf_op jit(solution)/shard_map/all_gather | solution.py:424
  381.4 13.6 %multiply_convert_fusion.1 = (bf16[512,2048]{1,0:T(8,128)(2,1)S(1)}, bf16[512,2048]{1,0:T(8,128)(2,1)S(1)}, bf16[512,2048]{1,0:T(8,128)(2,1)}) fusion(f32[512,2048]{1,0:T(8,128)} %fusion.110, f32[512,2048]{1,0:T(8,128)} %fusion.111, bf16[512,2048]{1,0:T(8,128)(2,1)} %all-gather.15.cloned.1.call-done, bf16[2048,2048]{1,0:T(8,128)(2,1)} %param.18), kind=kOutput, calls=%fused_computation.10 | convolution fusion | flops 4310695936 | bytes 25165824 | tf_op jit(solution)/shard_map/dot_general | solution.py:91
  403.5 9.3 %add_convert_fusion = bf16[512,2048]{1,0:T(8,128)(2,1)} fusion(f32[512,2048]{1,0:T(8,128)S(1)} %fusion.112, bf16[512,2048]{1,0:T(8,128)(2,1)S(1)} %get-tuple-element.9, bf16[2048,2048]{1,0:T(8,128)(2,1)} %all-gather.13.cloned.1.call-done), kind=kOutput, calls=%fused_computation.9 | convolution fusion | flops 4297064448 | bytes 16777216 | tf_op jit(solution)/shard_map/dot_general | solution.py:91
  412.9 42.5 %reduce-scatter.13.cloned.1.call-done = bf16[128,2048]{1,0:T(8,128)(2,1)} async-done(((bf16[512,2048]{1,0:T(8,128)(2,1)}), bf16[128,2048]{1,0:T(8,128)(2,1)}) %reduce-scatter.13.cloned.1.call-update) | async-done | bytes 524304 | tf_op jit(solution)/shard_map/reduce_scatter | solution.py:474
  467.9 10.1 %convolution_convert_fusion.1 = bf16[2048,2048]{1,0:T(8,128)(2,1)} fusion(bf16[512,2048]{1,0:T(8,128)(2,1)} %all-gather.9.cloned.1.call-done, bf16[512,2048]{1,0:T(8,128)(2,1)} %copy-done.35), kind=kOutput, calls=%fused_computation.6 | convolution fusion | flops 4299161600 | bytes 12582912 | tf_op jit(solution)/shard_map/dot_general | solution.py:97
  506.4 8.8 convolution_convert_fusion
  540.2 29.5 %collective-permute-done.2 = bf16[256,2048]{1,0:T(8,128)(2,1)S(1)} collective-permute-done((bf16[256,2048]{1,0:T(8,128)(2,1)S(1)}, bf16[256,2048]{1,0:T(8,128)(2,1)S(1)}, u32[]{:S(2)}, u32[]{:S(2)}) %collective-permute-start.2) | collective-permute-done | bytes 1048608 | tf_op jit(solution)/shard_map/ppermute | solution.py:550
  602.2 42.9 %reduce-scatter.17.cloned.1.call-done = bf16[256,2048]{1,0:T(8,128)(2,1)} async-done(((bf16[2048,2048]{1,0:T(8,128)(2,1)}), bf16[256,2048]{1,0:T(8,128)(2,1)}) %reduce-scatter.17.cloned.1.call-update) | async-done | bytes 1048592 | tf_op jit(solution)/shard_map/reduce_scatter | solution.py:494
  655.9 18.8 %all-to-all-done.4 = bf16[4,64,2048]{2,1,0:T(8,128)(2,1)S(1)} async-done(((bf16[4,64,2048]{2,1,0:T(8,128)(2,1)}), bf16[4,64,2048]{2,1,0:T(8,128)(2,1)S(1)}, u32[]{:S(2)}, u32[]{:S(2)}) %all-to-all-start.4) | async-done | bytes 1048608 | tf_op jit(solution)/shard_map/all_to_all | solution.py:496
  680.1 10.2 %convolution_convert_fusion.6 = bf16[512,2048]{1,0:T(8,128)(2,1)} fusion(bf16[512,2048]{1,0:T(8,128)(2,1)} %get-tuple-element.11, bf16[2048,2048]{1,0:T(8,128)(2,1)} %param.18), kind=kOutput, calls=%fused_computation.22 | convolution fusion | flops 4296015872 | bytes 12582912 | tf_op jit(solution)/shard_map/dot_general | solution.py:463
  701.2 26.8 %all-to-all-done.3 = bf16[32,64,512]{2,1,0:T(8,128)(2,1)S(1)} async-done(((bf16[32,64,512]{2,1,0:T(8,128)(2,1)}), bf16[32,64,512]{2,1,0:T(8,128)(2,1)S(1)}, u32[]{:S(2)}, u32[]{:S(2)}) %all-to-all-start.3) | async-done | bytes 2097184 | tf_op jit(solution)/shard_map/all_to_all | solution.py:537
  743.7 40.7 %reduce-scatter.21.cloned.1.call-done = bf16[64,2048]{1,0:T(8,128)(2,1)} async-done(((bf16[512,2048]{1,0:T(8,128)(2,1)}), bf16[64,2048]{1,0:T(8,128)(2,1)}) %reduce-scatter.21.cloned.1.call-update) | async-done | bytes 262160 | tf_op jit(solution)/shard_map/reduce_scatter | solution.py:554
  786.2 52.9 %reduce-scatter.15.cloned.1.call-done = bf16[128,2048]{1,0:T(8,128)(2,1)} async-done(((bf16[1024,2048]{1,0:T(8,128)(2,1)}), bf16[128,2048]{1,0:T(8,128)(2,1)}) %reduce-scatter.15.cloned.1.call-update) | async-done | bytes 524304 | tf_op jit(solution)/shard_map/reduce_scatter | solution.py:523
  840.4 44.7 %reduce-scatter.11.cloned.1.call-done = bf16[128,2048]{1,0:T(8,128)(2,1)} async-done(((bf16[512,2048]{1,0:T(8,128)(2,1)}), bf16[128,2048]{1,0:T(8,128)(2,1)}) %reduce-scatter.11.cloned.1.call-update) | async-done | bytes 524304 | tf_op jit(solution)/shard_map/reduce_scatter | solution.py:470
  (218 shorter events, 210.8 us)
Async XLA Ops:
  7.2 83.5 %all-gather.7.cloned.1.call-start = ((), (), s32[]{:S(2)}) async-start(), calls=%async_computation.14 | async-start | bytes 4718592 | tf_op jit(solution)/shard_map/all_gather | solution.py:428
  15.7 75.0 %all-to-all-start = ((bf16[4,512,512]{2,1,0:T(8,128)(2,1)}), bf16[4,512,512]{2,1,0:T(8,128)(2,1)}, u32[]{:S(2)}, u32[]{:S(2)}) async-start(bf16[4,512,512]{2,1,0:T(8,128)(2,1)} %pad_maximum_fusion), calls=%async_computation | async-start | bytes 4194304 | tf_op jit(solution)/shard_map/all_to_all | solution.py:402
  20.4 153.5 %reduce-scatter.9.cloned.1.call-start = ((), (), s32[]{:S(2)}) async-start(), calls=%async_computation.15 | async-start | bytes 4718592 | tf_op jit(solution)/shard_map/reduce_scatter | solution.py:451
  21.5 91.7 %collective-permute-start = (bf16[256,2048]{1,0:T(8,128)(2,1)}, bf16[256,2048]{1,0:T(8,128)(2,1)}, u32[]{:S(2)}, u32[]{:S(2)}) collective-permute-start(bf16[256,2048]{1,0:T(8,128)(2,1)} %constant_dynamic-slice_fusion.2), channel_id=1, source_target_pairs={{0,0},{1,1},{2,2},{3,3},{4,4},{5,5},{6,6},{7,7},{9,8},{10,9},{11,1... | collective-permute-start | bytes 3145736 | tf_op jit(solution)/shard_map/ppermute | solution.py:411
  117.8 110.8 %all-gather.13.cloned.1.call-start = ((), (), s32[]{:S(2)}) async-start(), calls=%async_computation.18 | async-start | bytes 9437184 | tf_op jit(solution)/shard_map/all_gather | solution.py:420
  173.9 103.4 %all-gather.9.cloned.1.call-start = ((), (), s32[]{:S(2)}) async-start(), calls=%async_computation.16 | async-start | bytes 2621440 | tf_op jit(solution)/shard_map/all_gather | solution.py:457
  177.4 155.8 %all-gather.11.cloned.1.call-start = ((), (), s32[]{:S(2)}) async-start(), calls=%async_computation.17 | async-start | bytes 9437184 | tf_op jit(solution)/shard_map/all_gather | solution.py:420
  205.9 175.5 %all-gather.15.cloned.1.call-start = ((), (), s32[]{:S(2)}) async-start(), calls=%async_computation.20 | async-start | bytes 2621440 | tf_op jit(solution)/shard_map/all_gather | solution.py:424
  206.5 248.9 %reduce-scatter.13.cloned.1.call-start = ((), (), s32[]{:S(2)}) async-start(), calls=%async_computation.21 | async-start | bytes 2621440 | tf_op jit(solution)/shard_map/reduce_scatter | solution.py:474
  412.8 102.5 %all-gather.17.cloned.1.call-start = ((), (), s32[]{:S(2)}) async-start(), calls=%async_computation.22 | async-start | bytes 4718592 | tf_op jit(solution)/shard_map/all_gather | solution.py:503
  459.1 139.6 %reduce-scatter.19.cloned.1.call-start = ((), (), s32[]{:S(2)}) async-start(), calls=%async_computation.25 | async-start | bytes 9437184 | tf_op jit(solution)/shard_map/reduce_scatter | solution.py:494
  486.3 158.8 %reduce-scatter.17.cloned.1.call-start = ((), (), s32[]{:S(2)}) async-start(), calls=%async_computation.24 | async-start | bytes 9437184 | tf_op jit(solution)/shard_map/reduce_scatter | solution.py:494
  504.6 235.7 %reduce-scatter.23.cloned.1.call-start = ((), (), s32[]{:S(2)}) async-start(), calls=%async_computation.27 | async-start | bytes 9437184 | tf_op jit(solution)/shard_map/reduce_scatter | solution.py:487
  515.2 269.2 %reduce-scatter.21.cloned.1.call-start = ((), (), s32[]{:S(2)}) async-start(), calls=%async_computation.26 | async-start | bytes 2359296 | tf_op jit(solution)/shard_map/reduce_scatter | solution.py:554
  519.9 49.8 %collective-permute-start.2 = (bf16[256,2048]{1,0:T(8,128)(2,1)S(1)}, bf16[256,2048]{1,0:T(8,128)(2,1)S(1)}, u32[]{:S(2)}, u32[]{:S(2)}) collective-permute-start(bf16[256,2048]{1,0:T(8,128)(2,1)S(1)} %convolution_convert_fusion.7), channel_id=1, source_target_pairs={{0,0},{1,1},{2,2},{3,3},{4,4},{5,5},{6,6},{7,7},{8,9},{9,10},{10,1... | collective-permute-start | bytes 3145736 | tf_op jit(solution)/shard_map/ppermute | solution.py:550
  571.5 267.6 %reduce-scatter.15.cloned.1.call-start = ((), (), s32[]{:S(2)}) async-start(), calls=%async_computation.23 | async-start | bytes 4718592 | tf_op jit(solution)/shard_map/reduce_scatter | solution.py:523
  598.7 46.5 %all-to-all-start.5 = ((bf16[4,64,2048]{2,1,0:T(8,128)(2,1)}), bf16[4,64,2048]{2,1,0:T(8,128)(2,1)S(1)}, u32[]{:S(2)}, u32[]{:S(2)}) async-start(bf16[4,64,2048]{2,1,0:T(8,128)(2,1)} %bitcast.175), calls=%async_computation.11 | async-start | bytes 2097152 | tf_op jit(solution)/shard_map/all_to_all | solution.py:496
  645.1 29.5 %all-to-all-start.4 = ((bf16[4,64,2048]{2,1,0:T(8,128)(2,1)}), bf16[4,64,2048]{2,1,0:T(8,128)(2,1)S(1)}, u32[]{:S(2)}, u32[]{:S(2)}) async-start(bf16[4,64,2048]{2,1,0:T(8,128)(2,1)} %bitcast.176), calls=%async_computation.9 | async-start | bytes 2097152 | tf_op jit(solution)/shard_map/all_to_all | solution.py:496
  675.7 52.3 %all-to-all-start.3 = ((bf16[32,64,512]{2,1,0:T(8,128)(2,1)}), bf16[32,64,512]{2,1,0:T(8,128)(2,1)S(1)}, u32[]{:S(2)}, u32[]{:S(2)}) async-start(bf16[32,64,512]{2,1,0:T(8,128)(2,1)} %bitcast.165), calls=%async_computation.7 | async-start | bytes 4194304 | tf_op jit(solution)/shard_map/all_to_all | solution.py:537
  679.9 205.2 %reduce-scatter.11.cloned.1.call-start = ((), (), s32[]{:S(2)}) async-start(), calls=%async_computation.19 | async-start | bytes 2621440 | tf_op jit(solution)/shard_map/reduce_scatter | solution.py:470
  729.0 156.1 %copy-start.25 = (f32[128]{0:T(128)S(1)}, f32[128]{0:T(128)}, u32[]{:S(2)}) copy-start(f32[128]{0:T(128)} %copy-done.24) | copy-start | bytes 1540
  729.0 156.1 %copy-start.26 = (f32[128]{0:T(128)S(1)}, f32[128]{0:T(128)}, u32[]{:S(2)}) copy-start(f32[128]{0:T(128)} %get-tuple-element.46) | copy-start | bytes 1540
  731.6 11.5 %collective-permute-start.1 = (f32[2,64]{1,0:T(2,128)S(1)}, f32[2,64]{1,0:T(2,128)S(1)}, u32[]{:S(2)}, u32[]{:S(2)}) collective-permute-start(f32[2,64]{1,0:T(2,128)S(1)} %pad_maximum_fusion.9), channel_id=1, source_target_pairs={{0,0},{1,8},{2,16},{3,24},{4,1},{5,9},{6,17},{7,25},{8,2},{9,10},{... | collective-permute-start | bytes 1544 | tf_op jit(solution)/shard_map/ppermute | solution.py:567
  734.6 154.0 %copy-start.1 = (bf16[512,2048]{1,0:T(8,128)(2,1)S(1)}, bf16[512,2048]{1,0:T(8,128)(2,1)}, u32[]{:S(2)}) copy-start(bf16[512,2048]{1,0:T(8,128)(2,1)} %param.15) | copy-start | bytes 6291460
  (35 other events, 432.9 us)
Sparse Core Ops, SparseCore 0:
  11.3 38.1 all-gather.6
  117.9 50.1 reduce-scatter.8
  174.0 54.4 all-gather.12
  230.6 46.6 all-gather.8
  279.2 53.9 all-gather.10
  334.7 46.6 all-gather.14
  412.9 42.4 reduce-scatter.12
  459.2 36.4 all-gather.16
  499.2 70.9 reduce-scatter.18
  573.8 71.2 reduce-scatter.16
  648.6 91.6 reduce-scatter.22
  743.8 40.5 reduce-scatter.20
  787.7 51.3 reduce-scatter.14
  841.3 43.7 reduce-scatter.10

commit v2 on v1

--- a/solution.py
+++ b/solution.py
@@ -3,6 +3,8 @@
 import jax
 import jax.numpy as jnp
 from jax import lax
+from jax.experimental import pallas as pl
+from jax.experimental.pallas import tpu as pltpu
 from jax.sharding import PartitionSpec as P
 
 QUERY_HEADS = 16
@@ -339,6 +341,487 @@
     )
 
 
+MESH = pl.DeviceIdType.MESH
+ACROSS_X, ACROSS_Y, ACROSS_CORE = 2, 4, 1
+
+
+class Links:
+    def __init__(self, sems, ctx, fsdp):
+        self.send_sem, self.recv_sem, self.local_sem = sems
+        self.ctx, self.fsdp = ctx, fsdp
+        self.remote = self.locals = 0
+
+    def to(self, src, dst, ctx, fsdp):
+        index, self.remote = self.remote, self.remote + 1
+        return pltpu.make_async_remote_copy(
+            src_ref=src,
+            dst_ref=dst,
+            send_sem=self.send_sem.at[index],
+            recv_sem=self.recv_sem.at[index],
+            device_id=(ctx, fsdp),
+            device_id_type=MESH,
+        )
+
+    def plane(self, src, dst, flip):
+        return self.to(src, dst, lax.bitwise_xor(self.ctx, flip), self.fsdp)
+
+    def column(self, src, dst, flip):
+        return self.to(src, dst, self.ctx, lax.bitwise_xor(self.fsdp, flip))
+
+    def here(self, src, dst):
+        index, self.locals = self.locals, self.locals + 1
+        return pltpu.make_async_copy(src, dst, self.local_sem.at[index])
+
+
+def greet(ctx, fsdp):
+    barrier = pltpu.get_barrier_semaphore()
+    partners = [(lax.bitwise_xor(ctx, flip), fsdp) for flip in (1, 2, 4)]
+    partners += [(ctx, lax.bitwise_xor(fsdp, flip)) for flip in (1, 2, 3)]
+    for partner in partners:
+        pl.semaphore_signal(barrier, inc=1, device_id=partner, device_id_type=MESH)
+    pl.semaphore_wait(barrier, len(partners))
+
+
+class PlaneGather:
+    def __init__(self, links, blocks, halves):
+        self.links, self.blocks, self.halves = links, blocks, halves
+        self.ctx = links.ctx
+        self.sent = []
+        self.cores = []
+
+    def _go(self, copies):
+        for copy in copies:
+            copy.start()
+        self.sent += copies
+        return copies
+
+    def _core(self, index):
+        refs = self.blocks(index)
+        self.cores += self._go([self.links.plane(r, r, ACROSS_CORE) for r in refs])
+
+    def begin(self):
+        refs = self.blocks(self.ctx)
+        self.from_x = self._go([self.links.plane(r, r, ACROSS_X) for r in refs])
+        self.from_y = self._go([self.links.plane(r, r, ACROSS_Y) for r in refs])
+        self._core(self.ctx)
+
+    def forward(self):
+        index = lax.bitwise_xor(self.ctx, ACROSS_X)
+        for copy in self.from_x:
+            copy.wait_recv()
+        refs = self.halves(index, 0)
+        self.corner = self._go([self.links.plane(r, r, ACROSS_Y) for r in refs])
+        self._core(index)
+        index = lax.bitwise_xor(self.ctx, ACROSS_Y)
+        for copy in self.from_y:
+            copy.wait_recv()
+        refs = self.halves(index, 1)
+        self.corner += self._go([self.links.plane(r, r, ACROSS_X) for r in refs])
+        self._core(index)
+
+    def finish(self):
+        for copy in self.corner:
+            copy.wait_recv()
+        self._core(lax.bitwise_xor(self.ctx, ACROSS_X | ACROSS_Y))
+        for copy in self.cores:
+            copy.wait_recv()
+
+    def drain(self):
+        for copy in self.sent:
+            copy.wait_send()
+
+
+class PlaneScatter:
+    def __init__(self, links, part, core_rx, half_rx, side_rx):
+        self.links, self.part = links, part
+        self.core_rx, self.half_rx, self.side_rx = core_rx, half_rx, side_rx
+        self.chip, self.core = links.ctx // 2, lax.rem(links.ctx, 2)
+        self.sent = []
+        self.from_core = {}
+
+    def order(self):
+        return [(flip, lax.bitwise_xor(self.chip, flip)) for flip in (3, 1, 2, 0)]
+
+    def _go(self, copy):
+        copy.start()
+        self.sent.append(copy)
+        return copy
+
+    def give(self, flip, chip):
+        self.from_core[flip] = self._go(
+            self.links.plane(
+                self.part.at[2 * chip + 1 - self.core], self.core_rx.at[chip], ACROSS_CORE
+            )
+        )
+
+    def _summed(self, flip):
+        chip = lax.bitwise_xor(self.chip, flip)
+        self.from_core[flip].wait_recv()
+        mine = self.part.at[2 * chip + self.core]
+        total = mine[...].astype(jnp.float32) + self.core_rx[chip].astype(jnp.float32)
+        return mine, total
+
+    def run(self):
+        half = self.half_rx.shape[1]
+        mine, total = self._summed(3)
+        mine[...] = total.astype(jnp.bfloat16)
+        top = self._go(
+            self.links.plane(mine.at[pl.ds(0, half)], self.half_rx.at[0], ACROSS_Y)
+        )
+        bottom = self._go(
+            self.links.plane(mine.at[pl.ds(half, half)], self.half_rx.at[1], ACROSS_X)
+        )
+        sides = []
+        for flip, copy, slot in ((1, top, 0), (2, bottom, 1)):
+            mine, total = self._summed(flip)
+            mine[...] = total.astype(jnp.bfloat16)
+            copy.wait_recv()
+            rows = pl.ds(slot * half, half)
+            mine[rows] = (
+                total[slot * half : (slot + 1) * half]
+                + self.half_rx[slot].astype(jnp.float32)
+            ).astype(jnp.bfloat16)
+            sides.append(
+                self._go(
+                    self.links.plane(
+                        mine, self.side_rx.at[slot], ACROSS_X if slot == 0 else ACROSS_Y
+                    )
+                )
+            )
+        mine, total = self._summed(0)
+        for slot, copy in enumerate(sides):
+            copy.wait_recv()
+            total = total + self.side_rx[slot].astype(jnp.float32)
+        return total
+
+    def drain(self):
+        for copy in self.sent:
+            copy.wait_send()
+
+
+def head_of(ctx, fsdp):
+    return lax.bitwise_xor(ctx, 4 * lax.rem(fsdp, 2))
+
+
+def out_plane(ctx, fsdp):
+    return lax.bitwise_xor(ctx // 2, 2 * lax.rem(fsdp, 2))
+
+
+def turn(vectors, cos_rows, sin_rows, sign):
+    return vectors * cos_rows + sign * pltpu.roll(vectors, HEAD_SIZE // 2, 1) * sin_rows
+
+
+def attention_kernel(
+    tokens_ref,
+    cot_ref,
+    gain_one_ref,
+    gain_two_ref,
+    qkv_w_ref,
+    out_w_ref,
+    gate_ref,
+    up_ref,
+    cos_ref,
+    sin_ref,
+    pos_col_ref,
+    pos_row_ref,
+    mid_ref,
+    normed_two_group,
+    cot_group,
+    gate_w,
+    up_w,
+    qkv_out,
+    attended_out,
+    normed_one_out,
+    w_head_out,
+    out_head_out,
+    normed,
+    w_head,
+    out_head,
+    qkv,
+    attended,
+    part,
+    core_rx,
+    half_rx,
+    side_rx,
+    normed_two,
+    send_sem,
+    recv_sem,
+    local_sem,
+):
+    f32, bf16 = jnp.float32, jnp.bfloat16
+    ctx, fsdp = lax.axis_index("ctx"), lax.axis_index("fsdp")
+    links = Links((send_sem, recv_sem, local_sem), ctx, fsdp)
+    rows, width = tokens_ref.shape
+    depth = qkv_w_ref.shape[0]
+    head_columns = out_head.shape[0]
+    n_ctx, n_fsdp = normed.shape[0], width // depth
+    seq_rows = n_ctx * rows
+    hidden = gate_w.shape[1]
+    strip = hidden // n_ctx
+    query_columns = QUERY_HEADS * HEAD_SIZE
+    key_columns = KEY_VALUE_HEADS * HEAD_SIZE
+    score_scale = 1.0 / math.sqrt(HEAD_SIZE)
+    finals = []
+
+    greet(ctx, fsdp)
+
+    my_rows = pl.ds(pl.multiple_of(fsdp * depth, depth), depth)
+
+    def head_parts(head):
+        starts = (
+            (head * head_columns, head_columns, 0),
+            (query_columns + head * HEAD_SIZE, HEAD_SIZE, head_columns),
+            (query_columns + key_columns + head * HEAD_SIZE, HEAD_SIZE, head_columns + HEAD_SIZE),
+        )
+        for start, size, place in starts:
+            yield (
+                qkv_w_ref.at[:, pl.ds(pl.multiple_of(start, HEAD_SIZE), size)],
+                w_head.at[my_rows, pl.ds(place, size)],
+            )
+
+    head_copies = []
+    for flip in (1, 2, 3):
+        for src, dst in head_parts(head_of(ctx, lax.bitwise_xor(fsdp, flip))):
+            head_copies.append(links.column(src, dst, flip))
+    own_head = [links.here(src, dst) for src, dst in head_parts(head_of(ctx, fsdp))]
+    for copy in head_copies + own_head:
+        copy.start()
+
+    inputs = tokens_ref[...].astype(f32)
+    scale = lax.rsqrt(jnp.mean(inputs * inputs, axis=-1, keepdims=True) + norm_eps)
+    normed[ctx] = (inputs * scale * gain_one_ref[...]).astype(bf16)
+    half = rows // 2
+    gather = PlaneGather(
+        links,
+        lambda j: [normed.at[j]],
+        lambda j, which: [normed.at[j, pl.ds(which * half, half)]],
+    )
+    gather.begin()
+    gather.forward()
+    gather.finish()
+    finals.append(links.here(normed, normed_one_out))
+    finals[-1].start()
+    for copy in own_head:
+        copy.wait()
+    for copy in head_copies:
+        copy.wait_recv()
+
+    out_block = out_w_ref.at[
+        pl.ds(pl.multiple_of(lax.rem(ctx, 2) * head_columns, head_columns), head_columns)
+    ]
+    out_sends = []
+    slot = links.remote
+    out_slot = links.column(out_block, out_head, 1)
+    out_home = links.here(out_block, out_head)
+    home = out_plane(ctx, fsdp) == fsdp
+    for target in range(n_fsdp):
+        wanted = (out_plane(ctx, jnp.int32(target)) == fsdp) & (fsdp != target)
+        copy = pltpu.make_async_remote_copy(
+            src_ref=out_block,
+            dst_ref=out_head,
+            send_sem=send_sem.at[links.remote],
+            recv_sem=recv_sem.at[slot],
+            device_id=(ctx, jnp.int32(target)),
+            device_id_type=MESH,
+        )
+        links.remote += 1
+        out_sends.append((wanted, copy))
+
+        @pl.when(wanted)
+        def _(copy=copy):
+            copy.start()
+
+    @pl.when(home)
+    def _():
+        out_home.start()
+
+    def strips(target, rows_of):
+        cols = pl.ds(pl.multiple_of(target * hidden + ctx * strip, strip), strip)
+        place = pl.ds(pl.multiple_of(ctx * strip, strip), strip)
+        for source, dest in ((gate_ref, gate_w), (up_ref, up_w)):
+            yield source.at[:, cols], dest.at[rows_of, place]
+
+    strip_copies = []
+    for flip in (1, 2, 3):
+        for src, dst in strips(lax.bitwise_xor(fsdp, flip), my_rows):
+            strip_copies.append(links.column(src, dst, flip))
+    own_strips = [links.here(src, dst) for src, dst in strips(fsdp, my_rows)]
+    for copy in strip_copies + own_strips:
+        copy.start()
+
+    block_rows = 2 * rows
+
+    def project(step, carry):
+        at = pl.multiple_of(step * block_rows, block_rows)
+        tile = normed[pl.ds(step * 2, 2)].reshape(block_rows, width)
+        out = jnp.dot(tile, w_head[...], preferred_element_type=f32)
+        cos_rows, sin_rows = cos_ref[pl.ds(at, block_rows)], sin_ref[pl.ds(at, block_rows)]
+        for column in range(0, head_columns + HEAD_SIZE, HEAD_SIZE):
+            turned = turn(out[:, column : column + HEAD_SIZE], cos_rows, sin_rows, 1.0)
+            qkv[pl.ds(at, block_rows), pl.ds(column, HEAD_SIZE)] = turned.astype(bf16)
+        column = head_columns + HEAD_SIZE
+        qkv[pl.ds(at, block_rows), pl.ds(column, HEAD_SIZE)] = out[:, column:].astype(bf16)
+        return carry
+
+    lax.fori_loop(0, seq_rows // block_rows, project, 0)
+
+    def attend(step, carry):
+        at = pl.multiple_of(step * block_rows, block_rows)
+        keys = qkv[:, pl.ds(head_columns, HEAD_SIZE)]
+        values = qkv[:, pl.ds(head_columns + HEAD_SIZE, HEAD_SIZE)]
+        causal = pos_row_ref[...] <= pos_col_ref[pl.ds(at, block_rows)]
+        for column in range(0, head_columns, HEAD_SIZE):
+            query = qkv[pl.ds(at, block_rows), pl.ds(column, HEAD_SIZE)]
+            scores = contract_last(query, keys) * score_scale
+            scores = jnp.where(causal, scores, -1e30)
+            shifted = jnp.exp(scores - jnp.max(scores, axis=-1, keepdims=True))
+            probs = shifted * (1.0 / jnp.sum(shifted, axis=-1, keepdims=True))
+            mixed = jnp.dot(probs.astype(bf16), values, preferred_element_type=f32)
+            attended[pl.ds(at, block_rows), pl.ds(column, HEAD_SIZE)] = mixed.astype(bf16)
+        return carry
+
+    lax.fori_loop(0, seq_rows // block_rows, attend, 0)
+
+    @pl.when(home)
+    def _():
+        out_home.wait()
+
+    @pl.when(jnp.logical_not(home))
+    def _():
+        out_slot.wait_recv()
+
+    for src, dst in (
+        (qkv, qkv_out),
+        (attended, attended_out),
+        (w_head, w_head_out),
+        (out_head, out_head_out),
+    ):
+        finals.append(links.here(src, dst))
+        finals[-1].start()
+
+    scatter = PlaneScatter(links, part, core_rx, half_rx, side_rx)
+    for flip, chip in scatter.order():
+        at = pl.multiple_of(chip * block_rows, block_rows)
+        out = jnp.dot(
+            attended[pl.ds(at, block_rows)], out_head[...], preferred_element_type=f32
+        )
+        part[pl.ds(chip * 2, 2)] = out.astype(bf16).reshape(2, rows, width)
+        scatter.give(flip, chip)
+    mid = tokens_ref[...].astype(f32) + scatter.run()
+    mid_ref[...] = mid
+    mid_scale = lax.rsqrt(jnp.mean(mid * mid, axis=-1, keepdims=True) + norm_eps)
+    normed_two[...] = (mid * mid_scale * gain_two_ref[...]).astype(bf16)
+
+    group_rows = pl.ds(pl.multiple_of(fsdp * rows, rows), rows)
+    group_copies = []
+    for source, dest in ((normed_two, normed_two_group), (cot_ref, cot_group)):
+        for flip in (1, 2, 3):
+            group_copies.append(links.column(source, dest.at[group_rows], flip))
+        finals.append(links.here(source, dest.at[group_rows]))
+        finals[-1].start()
+    for copy in group_copies:
+        copy.start()
+
+    for copy in own_strips:
+        copy.wait()
+    for copy in strip_copies:
+        copy.wait_recv()
+
+    def columns_of(j):
+        place = pl.ds(pl.multiple_of(j * strip, strip), strip)
+        return [gate_w.at[:, place], up_w.at[:, place]]
+
+    def halves_of(j, which):
+        place = pl.ds(pl.multiple_of(j * strip, strip), strip)
+        part_rows = pl.ds(which * (width // 2), width // 2)
+        return [gate_w.at[part_rows, place], up_w.at[part_rows, place]]
+
+    weights = PlaneGather(links, columns_of, halves_of)
+    weights.begin()
+    weights.forward()
+    weights.finish()
+
+    for copy in group_copies:
+        copy.wait_recv()
+    for copy in head_copies + strip_copies + group_copies:
+        copy.wait_send()
+    for wanted, copy in out_sends:
+
+        @pl.when(wanted)
+        def _(copy=copy):
+            copy.wait_send()
+
+    gather.drain()
+    scatter.drain()
+    weights.drain()
+    for copy in finals:
+        copy.wait()
+
+
+def attention_forward(
+    tokens, cotangent, gain_attn, gain_ffn, qkv_w, w_out, w_gate, w_up, cos, sin, key_pos
+):
+    f32, bf16 = jnp.float32, jnp.bfloat16
+    n_ctx, n_fsdp = lax.axis_size("ctx"), lax.axis_size("fsdp")
+    rows, width = tokens.shape
+    depth = qkv_w.shape[0]
+    hidden = w_gate.shape[1] // n_fsdp
+    seq_rows = n_ctx * rows
+    head_columns = QUERY_HEADS // KEY_VALUE_HEADS * HEAD_SIZE
+    all_columns = head_columns + 2 * HEAD_SIZE
+    vmem, hbm = pl.BlockSpec(memory_space=pltpu.VMEM), pl.BlockSpec(memory_space=pl.ANY)
+    shape = jax.ShapeDtypeStruct
+    return pl.pallas_call(
+        attention_kernel,
+        name="attention_forward",
+        out_shape=[
+            shape((rows, width), f32),
+            shape((n_fsdp * rows, width), bf16),
+            shape((n_fsdp * rows, width), bf16),
+            shape((width, hidden), bf16),
+            shape((width, hidden), bf16),
+            shape((seq_rows, all_columns), bf16),
+            shape((seq_rows, head_columns), bf16),
+            shape((n_ctx, rows, width), bf16),
+            shape((width, all_columns), bf16),
+            shape((head_columns, width), bf16),
+        ],
+        in_specs=[vmem] * 4 + [hbm] * 4 + [vmem] * 4,
+        out_specs=[vmem] + [hbm] * 9,
+        scratch_shapes=[
+            pltpu.VMEM((n_ctx, rows, width), bf16),
+            pltpu.VMEM((width, all_columns), bf16),
+            pltpu.VMEM((head_columns, width), bf16),
+            pltpu.VMEM((seq_rows, all_columns), bf16),
+            pltpu.VMEM((seq_rows, head_columns), bf16),
+            pltpu.VMEM((n_ctx, rows, width), bf16),
+            pltpu.VMEM((n_ctx // 2, rows, width), bf16),
+            pltpu.VMEM((2, rows // 2, width), bf16),
+            pltpu.VMEM((2, rows, width), bf16),
+            pltpu.VMEM((rows, width), bf16),
+            pltpu.SemaphoreType.DMA((80,)),
+            pltpu.SemaphoreType.DMA((80,)),
+            pltpu.SemaphoreType.DMA((24,)),
+        ],
+        compiler_params=pltpu.CompilerParams(
+            collective_id=1, has_side_effects=True, vmem_limit_bytes=58 * 2**20
+        ),
+    )(
+        tokens,
+        cotangent,
+        gain_attn[None],
+        gain_ffn[None],
+        qkv_w,
+        w_out,
+        w_gate,
+        w_up,
+        cos,
+        sin,
+        key_pos[:, None],
+        key_pos[None],
+    )
+
+
 def rotate_heads(vectors, cosine, sine_val, sign):
     half_dim = HEAD_SIZE // 2
     first_half = vectors[..., :half_dim]
@@ -375,86 +858,51 @@
     score_scale = 1.0 / math.sqrt(HEAD_SIZE)
     depth = query_key_value_weight.shape[0]
     hidden_cols = w_down.shape[0]
-    share = depth // head_columns
-    head = lax.rem(ctx + share * fsdp, n_ctx)
-    plane_of = lambda c, f: ((c + share * f) % n_ctx) // share
 
     key_pos, own_pos = positions(pair_block, token_rows)
 
-    def head_columns_of(matrix, h):
-        return jnp.concatenate(
-            [
-                lax.dynamic_slice_in_dim(matrix, h * head_columns, head_columns, 1),
-                lax.dynamic_slice_in_dim(matrix, query_columns + h * HEAD_SIZE, HEAD_SIZE, 1),
-                lax.dynamic_slice_in_dim(
-                    matrix, query_columns + key_columns + h * HEAD_SIZE, HEAD_SIZE, 1
-                ),
-            ],
-            axis=1,
-        )
-
-    sends = jnp.stack(
-        [
-            head_columns_of(query_key_value_weight, lax.rem(ctx + share * f, n_ctx))
-            for f in range(n_fsdp)
-        ]
-    )
-    w_head = lax.all_to_all(sends, "fsdp", split_axis=0, concat_axis=0, tiled=True).reshape(
-        width, head_columns + 2 * HEAD_SIZE
-    )
-    out_block = lax.dynamic_slice_in_dim(
-        w_out, lax.rem(ctx, share) * head_columns, head_columns, 0
-    )
-    out_pairs = [
-        (c * n_fsdp + plane_of(c, f), c * n_fsdp + f) for c in range(n_ctx) for f in range(n_fsdp)
-    ]
-    out_head = lax.ppermute(out_block, ("ctx", "fsdp"), out_pairs)
-
-    def hidden_columns(matrix):
-        mine = lax.dynamic_index_in_dim(
-            matrix.reshape(depth, n_fsdp, n_ctx, hidden_cols // n_ctx), ctx, 2, keepdims=False
-        )
-        turned = lax.all_to_all(
-            mine.transpose(1, 0, 2), "fsdp", split_axis=0, concat_axis=0, tiled=True
-        ).reshape(width, hidden_cols // n_ctx)
-        return lax.all_gather(turned, "ctx", axis=1, tiled=True)
-
-    gate_w = hidden_columns(w_gate)
-    up_w = hidden_columns(w_up)
-    cot_group = lax.all_gather(cotangent, "fsdp", axis=0, tiled=True)
-
-    inputs_f = tokens.astype(f32)
-    normed_one_b = rms_norm(inputs_f, gain_attn).astype(bf16)
-    normed_one_seq = lax.all_gather(normed_one_b, "ctx", axis=0, tiled=True)
-    projected = jnp.dot(normed_one_seq, w_head, preferred_element_type=f32)
     frequency = jnp.exp(
         jnp.arange(HEAD_SIZE // 2, dtype=f32) * (-2.0 * math.log(rope_base) / HEAD_SIZE)
     )
     angles = key_pos.astype(f32)[:, None] * frequency[None, :]
     cosine, sine_val = jnp.cos(angles), jnp.sin(angles)
-    heads = [
-        rotate_heads(projected[:, i * HEAD_SIZE : (i + 1) * HEAD_SIZE], cosine, sine_val, 1.0)
-        for i in range(group_count + 1)
-    ]
-    queries = jnp.stack(heads[:group_count]).astype(bf16)
-    keys = heads[group_count].astype(bf16)
-    values = projected[:, head_columns + HEAD_SIZE :].astype(bf16)
+    (
+        mid,
+        normed_two_group,
+        cot_group,
+        gate_w,
+        up_w,
+        qkv,
+        attended_b,
+        normed_one_seq,
+        w_head,
+        out_head,
+    ) = attention_forward(
+        tokens,
+        cotangent,
+        gain_attn,
+        gain_ffn,
+        query_key_value_weight,
+        w_out,
+        w_gate,
+        w_up,
+        jnp.concatenate([cosine, cosine], axis=1),
+        jnp.concatenate([-sine_val, sine_val], axis=1),
+        key_pos,
+    )
+    inputs_f = tokens.astype(f32)
+    normed_one_seq = normed_one_seq.reshape(-1, width)
+    queries = qkv[:, :head_columns].reshape(-1, group_count, HEAD_SIZE).transpose(1, 0, 2)
+    keys = qkv[:, head_columns : head_columns + HEAD_SIZE]
+    values = qkv[:, head_columns + HEAD_SIZE :]
     causal = key_pos[None, :] <= key_pos[:, None]
     scores = jnp.einsum("gqd,kd->gqk", queries, keys, preferred_element_type=f32) * score_scale
     scores = jnp.where(causal, scores, -1e30)
     shifted = jnp.exp(scores - jnp.max(scores, axis=-1, keepdims=True))
     probs = shifted / jnp.sum(shifted, axis=-1, keepdims=True)
     probs_low = probs.astype(bf16)
-    attended = jnp.einsum("gqk,kd->qgd", probs_low, values, preferred_element_type=f32)
-    attended_b = attended.astype(bf16).reshape(-1, head_columns)
-    out_part = jnp.dot(attended_b, out_head, preferred_element_type=f32)
-    mid = inputs_f + lax.psum_scatter(
-        out_part.astype(bf16), "ctx", scatter_dimension=0, tiled=True
-    ).astype(f32)
 
     mid_scale = lax.rsqrt(jnp.mean(mid * mid, axis=-1, keepdims=True) + norm_eps)
-    normed_two_b = (mid * mid_scale * gain_ffn).astype(bf16)
-    normed_two_group = lax.all_gather(normed_two_b, "fsdp", axis=0, tiled=True)
     gate = jnp.dot(normed_two_group, gate_w, preferred_element_type=f32)
     up = jnp.dot(normed_two_group, up_w, preferred_element_type=f32)
     sig = jax.nn.sigmoid(gate)
@@ -537,7 +985,7 @@
     got = lax.all_to_all(blocks, ("ctx", "fsdp"), split_axis=0, concat_axis=0, tiled=True)
     got = got.astype(f32)
     sums = [
-        sum(got[((h - share * f) % n_ctx) * n_fsdp + f] for f in range(n_fsdp))
+        sum(got[(h ^ (4 * (f % 2))) * n_fsdp + f] for f in range(n_fsdp))
         for h in range(KEY_VALUE_HEADS)
     ]
     grad_qkv = jnp.concatenate(
@@ -546,12 +994,14 @@
         + [s[:, head_columns + HEAD_SIZE :] for s in sums],
         axis=1,
     )
-    back_pairs = [(b, a) for a, b in out_pairs]
-    out_got = lax.ppermute(grad_out_part.astype(bf16), ("ctx", "fsdp"), back_pairs)
-    padded = lax.dynamic_update_slice_in_dim(
-        jnp.zeros((depth, width), bf16), out_got, lax.rem(ctx, share) * head_columns, 0
-    )
-    grad_out = lax.psum_scatter(padded, "ctx", scatter_dimension=0, tiled=True).astype(f32)
+    strip_rows = depth // n_ctx
+    placed = lax.dynamic_update_slice(
+        jnp.zeros((n_ctx, n_fsdp, strip_rows, width), bf16),
+        grad_out_part.astype(bf16).reshape(-1, 1, strip_rows, width),
+        (4 * lax.rem(ctx, 2), out_plane(ctx, fsdp), 0, 0),
+    ).reshape(n_ctx * n_fsdp, strip_rows, width)
+    out_got = lax.all_to_all(placed, ("ctx", "fsdp"), split_axis=0, concat_axis=0, tiled=True)
+    grad_out = jnp.sum(out_got.astype(f32), axis=0)
 
     my_rows = ctx * (depth // n_ctx)
     rows_of = lambda matrix: lax.dynamic_slice_in_dim(

time: 908 us -> 839 us (0.924)
  Pallas kernels: 0 us -> 221 us
  waiting for transfers between devices: 528 us -> 372 us
  blocking collectives: 57.1 us -> 0 us
  matrix products: 143 us -> 123 us
  local copies, waits for them, and re-layouts: 65.3 us -> 45.8 us
  starting transfers between devices: 38.2 us -> 20.9 us
  other arithmetic: 48.3 us -> 36.5 us
    pallas_call x0 -> x1, Pallas kernels: none -> 221 us  [attention_forward(): pl.pallas_call(attention_kernel, name='attention_forward', out_shape=[sha...]
    ppermute x1, waiting for transfers between devices: 0.01 us -> 181 us  [local_heads(): lax.ppermute(jnp.stack([attn_sum, ffn_sum]), ('ctx', 'fsdp'), gain_pairs)]
    all_gather x5 -> x0, waiting for transfers between devices: 155 us -> none  [the longest x2 66.9 us: hidden_columns(): return lax.all_gather(turned, 'ctx', axis=1, tiled=True)]
    all_to_all x1, waiting for transfers between devices: 63.2 us -> 0.01 us  [local_heads(): lax.all_to_all(placed, ('ctx', 'fsdp'), split_axis=0, concat_axis=0, tile...]
    all_to_all x2 -> x0, blocking collectives: 57.1 us -> none  [hidden_columns(): lax.all_to_all(mine.transpose(1, 0, 2), 'fsdp', split_axis=0, concat_axis...]
    reduce_scatter x1, waiting for transfers between devices: 52.9 us -> 0.01 us  [local_heads(): lax.psum_scatter(normed_one_part.astype(bf16), 'ctx', scatter_dimension=0...]
    reduce_scatter x2, waiting for transfers between devices: 42.9 us -> 95.5 us  [spread(): mine = lax.psum_scatter(blocks, 'ctx', scatter_dimension=0, tiled=True)]
    reduce_scatter x1, waiting for transfers between devices: 44.7 us -> 0.02 us  [local_heads(): lax.psum_scatter(down_part.astype(bf16), 'fsdp', scatter_dimension=0, til...]
  transfers between devices with their start and end apart: 21 -> 12, of which waited for: 15 -> 6; matrix products, arithmetic and copies ran while one was open for 22% -> 16% of each run, Pallas kernels for 0% -> 0%
where the time goes in v2:
time: 839 us; the launch traced here: 835 us
  waiting for transfers between devices  372 us (44%)
  Pallas kernels  221 us (26%)
  matrix products  123 us (15%)
  local copies, waits for them, and re-layouts  45.8 us (5%)
  other arithmetic  36.5 us (4%)
  starting transfers between devices  20.9 us (2%)
  between operations  15.5 us (2%)
    pallas_call x1, Pallas kernels, attention_forward(): pl.pallas_call(attention_kernel, name='attention_forward', out_shape=[sha...  221 us
    ppermute x1, waiting for transfers between devices, local_heads(): lax.ppermute(jnp.stack([attn_sum, ffn_sum]), ('ctx', 'fsdp'), gain_pairs)  181 us
    reduce_scatter x2, waiting for transfers between devices, spread(): mine = lax.psum_scatter(blocks, 'ctx', scatter_dimension=0, tiled=True)  95.5 us
    reduce_scatter x1, waiting for transfers between devices, local_heads(): lax.psum_scatter(normed_part.astype(bf16), 'fsdp', scatter_dimension=0, t...  43 us
    dot_general x5, matrix products, contract_last(): lax.dot_general(left, right, (((1,), (1,)), ((), ())), preferred_element_...  39.3 us
    all_to_all x1, waiting for transfers between devices, local_heads(): lax.all_to_all(blocks, ('ctx', 'fsdp'), split_axis=0, concat_axis=0, tile...  38.9 us
    dot_general x5, matrix products, contract_first(): lax.dot_general(left, right, (((0,), (0,)), ((), ())), preferred_element_...  34.4 us
  transfers between devices with their start and end apart: 12, of which 6 were waited for; matrix products, arithmetic and copies ran while one was open for 16% of the time, Pallas kernels for 0%

profile of v2, /device:TPU:5, one launch (start us, length us, event | category | flops | bytes accessed | tf_op | source)
XLA Modules:
  0.0 835.2 jit_solution(10331624009260492644)
XLA Ops:
  12.9 221.3 %attention_forward.1 = (f32[128,2048]{1,0:T(8,128)}, bf16[512,2048]{1,0:T(8,128)(2,1)}, bf16[512,2048]{1,0:T(8,128)(2,1)}, bf16[2048,2048]{1,0:T(8,128)(2,1)}, b...) custom-call(bf16[128,2048]{1,0:T(8,128)(2,1)} %tokens_ref.1, ...), custom_call_target="tpu_custom_call" | custom-call | tf_op jit(solution)/shard_map/attention_forward/pallas_call | solution.py:774
  234.2 10.7 %fusion.86 = f32[512,2048]{1,0:T(8,128)} fusion(bf16[512,2048]{1,0:T(8,128)(2,1)} %get-tuple-element.20, bf16[2048,2048]{1,0:T(8,128)(2,1)} %get-tuple-element.22), kind=kOutput, calls=%fused_computation.184 | convolution fusion | flops 4294967296 | bytes 14680064 | tf_op jit(solution)/shard_map/dot_general | solution.py:907
  244.9 6.1 fusion.85
  251.0 11.2 %multiply_convert_fusion.1 = (bf16[512,2048]{1,0:T(8,128)(2,1)}, bf16[512,2048]{1,0:T(8,128)(2,1)}, bf16[512,2048]{1,0:T(8,128)(2,1)}) fusion(f32[512,2048]{1,0:T(8,128)} %fusion.85, f32[512,2048]{1,0:T(8,128)} %fusion.86, bf16[512,2048]{1,0:T(8,128)(2,1)} %get-tuple-element.23, bf16[2048,2048]{1,0:T(8,128)(2,1)S(1)} %bitcast.191), kind=kOutput, calls=%fused_computation.16 | convolution fusion | flops 4310695936 | bytes 25165824 | tf_op jit(solution)/shard_map/dot_general | solution.py:93
  262.2 7.8 fusion.87
  270.0 9.5 %add_convert_fusion = bf16[512,2048]{1,0:T(8,128)(2,1)} fusion(f32[512,2048]{1,0:T(8,128)S(1)} %fusion.87, bf16[512,2048]{1,0:T(8,128)(2,1)S(1)} %copy-done.28, bf16[2048,2048]{1,0:T(8,128)(2,1)} %get-tuple-element.22), kind=kOutput, calls=%fused_computation.15 | convolution fusion | flops 4297064448 | bytes 16777216 | tf_op jit(solution)/shard_map/dot_general | solution.py:93
  279.6 43.0 %reduce-scatter.9.cloned.1.call-done = bf16[128,2048]{1,0:T(8,128)(2,1)} async-done(((bf16[512,2048]{1,0:T(8,128)(2,1)}), bf16[128,2048]{1,0:T(8,128)(2,1)}) %reduce-scatter.9.cloned.1.call-update) | async-done | bytes 524304 | tf_op jit(solution)/shard_map/reduce_scatter | solution.py:922
  326.8 10.1 %convolution_convert_fusion.1 = bf16[2048,2048]{1,0:T(8,128)(2,1)} fusion(bf16[512,2048]{1,0:T(8,128)(2,1)} %get-tuple-element.20, bf16[512,2048]{1,0:T(8,128)(2,1)} %get-tuple-element.33), kind=kOutput, calls=%fused_computation.7 | convolution fusion | flops 4299161600 | bytes 12582912 | tf_op jit(solution)/shard_map/dot_general | solution.py:99
  336.8 8.3 copy.97
  346.7 8.4 %convolution_convert_fusion.2 = bf16[2048,2048]{1,0:T(8,128)(2,1)} fusion(bf16[512,2048]{1,0:T(8,128)(2,1)S(1)} %copy-done.26, bf16[512,2048]{1,0:T(8,128)(2,1)} %get-tuple-element.34), kind=kOutput, calls=%fused_computation.8 | convolution fusion | flops 4299161600 | bytes 12582912 | tf_op jit(solution)/shard_map/dot_general | solution.py:99
  355.1 8.4 %copy.95 = bf16[4,8,64,2048]{3,2,0,1:T(8,128)(2,1)} copy(bf16[4,8,64,2048]{3,2,1,0:T(8,128)(2,1)} %bitcast.172) | data formatting | bytes 16777216 | tf_op jit(solution)/shard_map/reshape | solution.py:940
  365.1 8.5 %convolution_convert_fusion = bf16[2048,2048]{1,0:T(8,128)(2,1)} fusion(bf16[512,2048]{1,0:T(8,128)(2,1)} %get-tuple-element.35, bf16[512,2048]{1,0:T(8,128)(2,1)S(1)} %copy-done.24), kind=kOutput, calls=%fused_computation.6 | convolution fusion | flops 4299161600 | bytes 12582912 | tf_op jit(solution)/shard_map/dot_general | solution.py:99
  374.8 6.0 fusion.80
  385.3 4.9 multiply_reduce_fusion
  397.9 39.8 %reduce-scatter.15.cloned.1.call-done = bf16[256,2048]{1,0:T(8,128)(2,1)} async-done(((bf16[2048,2048]{1,0:T(8,128)(2,1)}), bf16[256,2048]{1,0:T(8,128)(2,1)}) %reduce-scatter.15.cloned.1.call-update) | async-done | bytes 1048592 | tf_op jit(solution)/shard_map/reduce_scatter | solution.py:942
  437.7 4.5 all-to-all-start.2
  456.6 55.8 %reduce-scatter.13.cloned.1.call-done = bf16[256,2048]{1,0:T(8,128)(2,1)} async-done(((bf16[2048,2048]{1,0:T(8,128)(2,1)}), bf16[256,2048]{1,0:T(8,128)(2,1)}) %reduce-scatter.13.cloned.1.call-update) | async-done | bytes 1048592 | tf_op jit(solution)/shard_map/reduce_scatter | solution.py:942
  516.6 5.8 fusion.15
  527.7 14.2 %all-to-all-done.1 = bf16[4,64,2048]{2,1,0:T(8,128)(2,1)S(1)} async-done(((bf16[4,64,2048]{2,1,0:T(8,128)(2,1)}), bf16[4,64,2048]{2,1,0:T(8,128)(2,1)S(1)}, u32[]{:S(2)}, u32[]{:S(2)}) %all-to-all-start.1) | async-done | bytes 1048608 | tf_op jit(solution)/shard_map/all_to_all | solution.py:944
  556.2 38.9 %all-to-all-done = bf16[32,64,512]{2,1,0:T(8,128)(2,1)S(1)} async-done(((bf16[32,64,512]{2,1,0:T(8,128)(2,1)}), bf16[32,64,512]{2,1,0:T(8,128)(2,1)S(1)}, u32[]{:S(2)}, u32[]{:S(2)}) %all-to-all-start) | async-done | bytes 2097184 | tf_op jit(solution)/shard_map/all_to_all | solution.py:985
  598.6 6.3 convolution_convert_fusion.3
  605.3 9.9 %convolution_convert_fusion.5 = bf16[512,2048]{1,0:T(8,128)(2,1)} fusion(bf16[512,2048]{1,0:T(8,128)(2,1)} %get-tuple-element.35, bf16[2048,2048]{1,0:T(8,128)(2,1)} %param.18), kind=kOutput, calls=%fused_computation.24 | convolution fusion | flops 4296015872 | bytes 12582912 | tf_op jit(solution)/shard_map/dot_general | solution.py:911
  635.9 180.7 %collective-permute-done = f32[2,64]{1,0:T(2,128)S(1)} collective-permute-done((f32[2,64]{1,0:T(2,128)S(1)}, f32[2,64]{1,0:T(2,128)S(1)}, u32[]{:S(2)}, u32[]{:S(2)}) %collective-permute-start) | collective-permute-done | bytes 544 | tf_op jit(solution)/shard_map/ppermute | solution.py:1017
  821.5 6.4 convert_reduce_fusion
  (172 shorter events, 93.4 us)
Async XLA Ops:
  7.2 315.4 %reduce-scatter.9.cloned.1.call-start = ((), (), s32[]{:S(2)}) async-start(), calls=%async_computation.11 | async-start | bytes 2621440 | tf_op jit(solution)/shard_map/reduce_scatter | solution.py:922
  234.2 16.8 %slice-start.2 = ((s8[8388608]{0:T(1024)(128)(4,1)}), s8[4194304]{0:T(1024)(128)(4,1)S(1)}, s32[]{:S(2)}) async-start(s8[8388608]{0:T(1024)(128)(4,1)} %bitcast.190), calls=%async_computation.19 | async-start | bytes 8388608
  270.0 52.6 %copy-start.1 = (f32[128,2048]{1,0:T(8,128)S(1)}, f32[128,2048]{1,0:T(8,128)}, u32[]{:S(2)}) copy-start(f32[128,2048]{1,0:T(8,128)} %get-tuple-element.19) | copy-start | bytes 3145732
  270.0 52.6 %copy-start.12 = (f32[2048]{0:T(1024)S(1)}, f32[2048]{0:T(1024)}, u32[]{:S(2)}) copy-start(f32[2048]{0:T(1024)} %param.13) | copy-start | bytes 24580
  270.0 54.0 %copy-start.5 = (bf16[128,2048]{1,0:T(8,128)(2,1)S(1)}, bf16[128,2048]{1,0:T(8,128)(2,1)}, u32[]{:S(2)}) copy-start(bf16[128,2048]{1,0:T(8,128)(2,1)} %cot_ref.1) | copy-start | bytes 1572868
  279.6 101.3 %all-gather.2.cloned.1.call-start = ((), (), s32[]{:S(2)}) async-start(), calls=%async_computation.12 | async-start | bytes 4718592 | tf_op jit(solution)/shard_map/all_gather | solution.py:951
  324.0 12.9 %copy-start.16 = (f32[128]{0:T(128)}, f32[128]{0:T(128)S(1)}, u32[]{:S(2)}) copy-start(f32[128]{0:T(128)S(1)} %get-tuple-element.68) | copy-start | bytes 1540
  326.3 111.4 %reduce-scatter.15.cloned.1.call-start = ((), (), s32[]{:S(2)}) async-start(), calls=%async_computation.15 | async-start | bytes 9437184 | tf_op jit(solution)/shard_map/reduce_scatter | solution.py:942
  345.2 167.2 %reduce-scatter.13.cloned.1.call-start = ((), (), s32[]{:S(2)}) async-start(), calls=%async_computation.14 | async-start | bytes 9437184 | tf_op jit(solution)/shard_map/reduce_scatter | solution.py:942
  363.6 269.5 %reduce-scatter.17.cloned.1.call-start = ((), (), s32[]{:S(2)}) async-start(), calls=%async_computation.16 | async-start | bytes 9437184 | tf_op jit(solution)/shard_map/reduce_scatter | solution.py:935
  437.7 74.6 %all-to-all-start.2 = ((bf16[4,64,2048]{2,1,0:T(8,128)(2,1)}), bf16[4,64,2048]{2,1,0:T(8,128)(2,1)S(1)}, u32[]{:S(2)}, u32[]{:S(2)}) async-start(bf16[4,64,2048]{2,1,0:T(8,128)(2,1)} %bitcast.183), calls=%async_computation.7 | async-start | bytes 2097152 | tf_op jit(solution)/shard_map/all_to_all | solution.py:944
  512.3 29.5 %all-to-all-start.1 = ((bf16[4,64,2048]{2,1,0:T(8,128)(2,1)}), bf16[4,64,2048]{2,1,0:T(8,128)(2,1)S(1)}, u32[]{:S(2)}, u32[]{:S(2)}) async-start(bf16[4,64,2048]{2,1,0:T(8,128)(2,1)} %bitcast.182), calls=%async_computation.5 | async-start | bytes 2097152 | tf_op jit(solution)/shard_map/all_to_all | solution.py:944
  542.8 52.3 %all-to-all-start = ((bf16[32,64,512]{2,1,0:T(8,128)(2,1)}), bf16[32,64,512]{2,1,0:T(8,128)(2,1)S(1)}, u32[]{:S(2)}, u32[]{:S(2)}) async-start(bf16[32,64,512]{2,1,0:T(8,128)(2,1)} %bitcast.178), calls=%async_computation.3 | async-start | bytes 4194304 | tf_op jit(solution)/shard_map/all_to_all | solution.py:985
  595.2 226.4 %all-to-all-start.3 = ((bf16[32,64,2048]{2,1,0:T(8,128)(2,1)}), bf16[32,64,2048]{2,1,0:T(8,128)(2,1)}, u32[]{:S(2)}, u32[]{:S(2)}) async-start(bf16[32,64,2048]{2,1,0:T(8,128)(2,1)} %bitcast.48), calls=%async_computation.8 | async-start | bytes 16777216 | tf_op jit(solution)/shard_map/all_to_all | solution.py:1003
  598.6 218.6 %reduce-scatter.11.cloned.1.call-start = ((), (), s32[]{:S(2)}) async-start(), calls=%async_computation.13 | async-start | bytes 4718592 | tf_op jit(solution)/shard_map/reduce_scatter | solution.py:971
  605.0 213.6 %reduce-scatter.7.cloned.1.call-start = ((), (), s32[]{:S(2)}) async-start(), calls=%async_computation.10 | async-start | bytes 2621440 | tf_op jit(solution)/shard_map/reduce_scatter | solution.py:918
  626.9 189.7 %copy-start.13 = (f32[2048]{0:T(1024)S(1)}, f32[2048]{0:T(1024)}, u32[]{:S(2)}) copy-start(f32[2048]{0:T(1024)} %param.12) | copy-start | bytes 24580
  626.9 190.3 %copy-start.4 = (bf16[128,2048]{1,0:T(8,128)(2,1)S(1)}, bf16[128,2048]{1,0:T(8,128)(2,1)}, u32[]{:S(2)}) copy-start(bf16[128,2048]{1,0:T(8,128)(2,1)} %tokens_ref.1) | copy-start | bytes 1572868
  627.2 191.4 %copy-start.6 = (bf16[128,2048]{1,0:T(8,128)(2,1)S(1)}, bf16[128,2048]{1,0:T(8,128)(2,1)}, u32[]{:S(2)}) copy-start(bf16[128,2048]{1,0:T(8,128)(2,1)} %cot_ref.1) | copy-start | bytes 1572868
  627.2 191.4 %copy-start.7 = (bf16[128,2048]{1,0:T(8,128)(2,1)S(1)}, bf16[128,2048]{1,0:T(8,128)(2,1)}, u32[]{:S(2)}) copy-start(bf16[128,2048]{1,0:T(8,128)(2,1)} %reduce-scatter.9.cloned.1.call-done) | copy-start | bytes 1572868
  627.2 191.4 %copy-start.17 = (f32[128]{0:T(128)S(1)}, f32[128]{0:T(128)}, u32[]{:S(2)}) copy-start(f32[128]{0:T(128)} %copy-done.16) | copy-start | bytes 1540
  627.2 191.4 %copy-start.19 = (f32[128]{0:T(128)S(1)}, f32[128]{0:T(128)}, u32[]{:S(2)}) copy-start(f32[128]{0:T(128)} %copy-done.18) | copy-start | bytes 1540
  627.2 191.4 %copy-start.21 = (f32[128]{0:T(128)S(1)}, f32[128]{0:T(128)}, u32[]{:S(2)}) copy-start(f32[128]{0:T(128)} %copy-done.20) | copy-start | bytes 1540
  629.8 186.8 %collective-permute-start = (f32[2,64]{1,0:T(2,128)S(1)}, f32[2,64]{1,0:T(2,128)S(1)}, u32[]{:S(2)}, u32[]{:S(2)}) collective-permute-start(f32[2,64]{1,0:T(2,128)S(1)} %pad_maximum_fusion.2), channel_id=1, source_target_pairs={{0,0},{1,8},{2,16},{3,24},{4,1},{5,9},{6,17},{7,25},{8,2},{9,10},{... | collective-permute-start | bytes 1544 | tf_op jit(solution)/shard_map/ppermute | solution.py:1017
  (21 other events, 114.7 us)
Sparse Core Ops, SparseCore 0:
  279.7 42.8 reduce-scatter.8
  326.4 36.4 all-gather.1
  366.7 70.9 reduce-scatter.14
  441.0 71.2 reduce-scatter.12
  516.0 102.2 reduce-scatter.16
  621.5 93.6 reduce-scatter.10
  717.6 58.9 reduce-scatter.6

commit v3 on v2

--- a/solution.py
+++ b/solution.py
@@ -343,6 +343,7 @@
 
 MESH = pl.DeviceIdType.MESH
 ACROSS_X, ACROSS_Y, ACROSS_CORE = 2, 4, 1
+BLOCK = 256
 
 
 class Links:
@@ -556,8 +557,9 @@
     head_columns = out_head.shape[0]
     n_ctx, n_fsdp = normed.shape[0], width // depth
     seq_rows = n_ctx * rows
-    hidden = gate_w.shape[1]
+    hidden = gate_w.shape[2]
     strip = hidden // n_ctx
+    depth_blocks = gate_ref.shape[0]
     query_columns = QUERY_HEADS * HEAD_SIZE
     key_columns = KEY_VALUE_HEADS * HEAD_SIZE
     score_scale = 1.0 / math.sqrt(HEAD_SIZE)
@@ -635,17 +637,19 @@
     def _():
         out_home.start()
 
-    def strips(target, rows_of):
+    block_rows_of = pl.ds(fsdp * depth_blocks, depth_blocks)
+
+    def strips(target):
         cols = pl.ds(pl.multiple_of(target * hidden + ctx * strip, strip), strip)
         place = pl.ds(pl.multiple_of(ctx * strip, strip), strip)
         for source, dest in ((gate_ref, gate_w), (up_ref, up_w)):
-            yield source.at[:, cols], dest.at[rows_of, place]
+            yield source.at[:, :, cols], dest.at[block_rows_of, :, place]
 
     strip_copies = []
     for flip in (1, 2, 3):
-        for src, dst in strips(lax.bitwise_xor(fsdp, flip), my_rows):
+        for src, dst in strips(lax.bitwise_xor(fsdp, flip)):
             strip_copies.append(links.column(src, dst, flip))
-    own_strips = [links.here(src, dst) for src, dst in strips(fsdp, my_rows)]
+    own_strips = [links.here(src, dst) for src, dst in strips(fsdp)]
     for copy in strip_copies + own_strips:
         copy.start()
 
@@ -729,12 +733,13 @@
 
     def columns_of(j):
         place = pl.ds(pl.multiple_of(j * strip, strip), strip)
-        return [gate_w.at[:, place], up_w.at[:, place]]
+        return [gate_w.at[:, :, place], up_w.at[:, :, place]]
 
     def halves_of(j, which):
         place = pl.ds(pl.multiple_of(j * strip, strip), strip)
-        part_rows = pl.ds(which * (width // 2), width // 2)
-        return [gate_w.at[part_rows, place], up_w.at[part_rows, place]]
+        blocks = gate_w.shape[0] // 2
+        some = pl.ds(which * blocks, blocks)
+        return [gate_w.at[some, :, place], up_w.at[some, :, place]]
 
     weights = PlaneGather(links, columns_of, halves_of)
     weights.begin()
@@ -778,8 +783,8 @@
             shape((rows, width), f32),
             shape((n_fsdp * rows, width), bf16),
             shape((n_fsdp * rows, width), bf16),
-            shape((width, hidden), bf16),
-            shape((width, hidden), bf16),
+            shape((width // BLOCK, BLOCK, hidden), bf16),
+            shape((width // BLOCK, BLOCK, hidden), bf16),
             shape((seq_rows, all_columns), bf16),
             shape((seq_rows, head_columns), bf16),
             shape((n_ctx, rows, width), bf16),
@@ -813,8 +818,8 @@
         gain_ffn[None],
         qkv_w,
         w_out,
-        w_gate,
-        w_up,
+        w_gate.reshape(depth // BLOCK, BLOCK, -1),
+        w_up.reshape(depth // BLOCK, BLOCK, -1),
         cos,
         sin,
         key_pos[:, None],
@@ -822,16 +827,700 @@
     )
 
 
-def rotate_heads(vectors, cosine, sine_val, sign):
-    half_dim = HEAD_SIZE // 2
-    first_half = vectors[..., :half_dim]
-    second_half = vectors[..., half_dim:]
-    return jnp.concatenate(
-        [
-            first_half * cosine - sign * second_half * sine_val,
-            second_half * cosine + sign * first_half * sine_val,
+class ChipScatter:
+    def __init__(self, links, part, halves, sides):
+        self.links, self.part, self.halves, self.sides = links, part, halves, sides
+        self.chip = links.ctx // 2
+        self.sent = []
+
+    def _go(self, copy):
+        copy.start()
+        self.sent.append(copy)
+        return copy
+
+    def begin(self):
+        corner = self.part(lax.bitwise_xor(self.chip, 3))
+        half = corner.shape[0] // 2
+        self.half = half
+        self.corner = [
+            self._go(self.links.plane(corner.at[pl.ds(0, half)], self.halves[0], ACROSS_Y)),
+            self._go(self.links.plane(corner.at[pl.ds(half, half)], self.halves[1], ACROSS_X)),
+        ]
+
+    def middle(self):
+        self.side = []
+        for slot, (flip, across) in enumerate(((1, ACROSS_X), (2, ACROSS_Y))):
+            mine = self.part(lax.bitwise_xor(self.chip, flip))
+            self.corner[slot].wait_recv()
+            rows = mine.at[pl.ds(slot * self.half, self.half)]
+            rows[...] = (
+                rows[...].astype(jnp.float32) + self.halves[slot][...].astype(jnp.float32)
+            ).astype(jnp.bfloat16)
+            self.side.append(self._go(self.links.plane(mine, self.sides[slot], across)))
+
+    def finish(self):
+        mine = self.part(self.chip)
+        for copy in self.side:
+            copy.wait_recv()
+        mine[...] = (
+            mine[...].astype(jnp.float32)
+            + self.sides[0][...].astype(jnp.float32)
+            + self.sides[1][...].astype(jnp.float32)
+        ).astype(jnp.bfloat16)
+        return mine
+
+    def drain(self):
+        for copy in self.sent:
+            copy.wait_send()
+
+
+def feed_forward_kernel(
+    mid_ref,
+    cot_ref,
+    gain_ref,
+    normed_ref,
+    cots_ref,
+    gate_hbm,
+    up_hbm,
+    down_hbm,
+    result_ref,
+    grad_mid_ref,
+    grad_proj_ref,
+    down_sum,
+    gate_sum,
+    up_part,
+    gate_v,
+    up_v,
+    down_v,
+    hidden,
+    grad_gate,
+    grad_up,
+    other_normed,
+    other_cots,
+    other_hidden,
+    other_gate,
+    other_up,
+    stage,
+    landed,
+    send_sem,
+    recv_sem,
+    local_sem,
+    load_sem,
+    free_sem,
+):
+    f32, bf16 = jnp.float32, jnp.bfloat16
+    ctx, fsdp = lax.axis_index("ctx"), lax.axis_index("fsdp")
+    links = Links((send_sem, recv_sem, local_sem), ctx, fsdp)
+    core = lax.rem(ctx, 2)
+    rows, width = mid_ref.shape
+    group_rows = normed_ref.shape[0]
+    blocks = gate_v.shape[0]
+    hidden_units = blocks * BLOCK
+    half_units = hidden_units // 2
+    n_fsdp = group_rows // rows
+
+    def loads(j):
+        cols = pl.ds(pl.multiple_of(j * BLOCK, BLOCK), BLOCK)
+        return (
+            pltpu.make_async_copy(
+                gate_hbm.at[:, :, cols], gate_v.at[:, :, cols], load_sem.at[0, j]
+            ),
+            pltpu.make_async_copy(up_hbm.at[:, :, cols], up_v.at[:, :, cols], load_sem.at[1, j]),
+            pltpu.make_async_copy(down_hbm.at[j], down_v.at[j], load_sem.at[2, j]),
+        )
+
+    for j in range(blocks):
+        for copy in loads(j):
+            copy.start()
+
+    greet(ctx, fsdp)
+
+    swaps = [
+        links.plane(normed_ref, other_normed, ACROSS_CORE),
+        links.plane(cots_ref, other_cots, ACROSS_CORE),
+    ]
+    for copy in swaps:
+        copy.start()
+
+    def activate(j, carry):
+        for copy in loads(j):
+            copy.wait()
+        cols = pl.ds(pl.multiple_of(j * BLOCK, BLOCK), BLOCK)
+        normed = normed_ref[...]
+        gate = jnp.dot(
+            normed, gate_v[:, :, cols].reshape(width, BLOCK), preferred_element_type=f32
+        )
+        up = jnp.dot(normed, up_v[:, :, cols].reshape(width, BLOCK), preferred_element_type=f32)
+        grad_hidden = contract_last(cots_ref[...], down_v[j])
+        sig = 1.0 / (1.0 + jnp.exp(-gate))
+        silu = gate * sig
+        hidden[:, cols] = (silu * up).astype(bf16)
+        grad_gate[:, cols] = (grad_hidden * up * (sig * (1.0 + gate * (1.0 - sig)))).astype(bf16)
+        grad_up[:, cols] = (grad_hidden * silu).astype(bf16)
+        return carry
+
+    lax.fori_loop(0, blocks, activate, 0)
+
+    theirs = pl.ds(pl.multiple_of((1 - core) * half_units, half_units), half_units)
+    acts = [
+        links.plane(grad_gate.at[:, theirs], other_gate, ACROSS_CORE),
+        links.plane(grad_up.at[:, theirs], other_up, ACROSS_CORE),
+    ]
+    for pair in range(blocks // 2):
+        cols = pl.ds(pl.multiple_of((2 * pair + 1 - core) * BLOCK, BLOCK), BLOCK)
+        acts.append(
+            links.plane(
+                hidden.at[:, cols], other_hidden.at[:, pl.ds(pair * BLOCK, BLOCK)], ACROSS_CORE
+            )
+        )
+    for copy in acts:
+        copy.start()
+
+    piece = 2 * BLOCK
+    group = []
+    for n in range(width // piece):
+        cols = pl.ds(n * piece, piece)
+        some = pl.ds(n * 2, 2)
+        back = contract_last(grad_gate[...], gate_v[some].reshape(piece, hidden_units))
+        back = back + contract_last(grad_up[...], up_v[some].reshape(piece, hidden_units))
+        stage[1, :, :, cols] = back.astype(bf16).reshape(n_fsdp, rows, piece)
+        down = jnp.dot(
+            hidden[...],
+            down_v[:, :, cols].reshape(hidden_units, piece),
+            preferred_element_type=f32,
+        )
+        stage[0, :, :, cols] = down.astype(bf16).reshape(n_fsdp, rows, piece)
+        for which in (1, 0):
+            for flip in (1, 2, 3):
+                target = lax.bitwise_xor(fsdp, flip)
+                copy = links.column(
+                    stage.at[which, target, :, cols], landed.at[which, flip - 1, :, cols], flip
+                )
+                copy.start()
+                group.append(copy)
+
+    for flip in (ACROSS_X, ACROSS_Y):
+        pl.semaphore_signal(
+            free_sem,
+            inc=1,
+            device_id=(lax.bitwise_xor(ctx, flip), fsdp),
+            device_id_type=MESH,
+        )
+
+    def rows_dot(left, right):
+        return lax.dot_general(
+            left, right, (((0,), (0,)), ((), ())), preferred_element_type=f32
+        )
+
+    for copy in swaps + acts:
+        copy.wait_recv()
+    down_rows = 4
+
+    def down_block(step, carry):
+        pair, part = step // 2, lax.rem(step, 2)
+        cols = pl.ds(pl.multiple_of(part * (width // 2), width // 2), width // 2)
+        own = pl.ds(pl.multiple_of((2 * pair + core) * BLOCK, BLOCK), BLOCK)
+        other = pl.ds(pl.multiple_of(pair * BLOCK, BLOCK), BLOCK)
+        total = rows_dot(hidden[:, own], cots_ref[:, cols]) + rows_dot(
+            other_hidden[:, other], other_cots[:, cols]
+        )
+        gate_v[pair, :, cols] = total.astype(bf16)
+        return carry
+
+    lax.fori_loop(0, blocks, down_block, 0)
+    pl.semaphore_wait(free_sem, 2)
+    down_scatter = ChipScatter(
+        links,
+        lambda chip: gate_v.at[chip],
+        [down_v.at[0, pl.ds(0, BLOCK // 2)], down_v.at[0, pl.ds(BLOCK // 2, BLOCK // 2)]],
+        [down_v.at[1], down_v.at[2]],
+    )
+    down_scatter.begin()
+
+    mine = pl.ds(pl.multiple_of(core * half_units, half_units), half_units)
+
+    def gradient_into(own_grad, other_grad, place):
+        def block(b, carry):
+            cols = pl.ds(pl.multiple_of(b * BLOCK, BLOCK), BLOCK)
+            total = rows_dot(normed_ref[:, cols], own_grad[:, mine]) + rows_dot(
+                other_normed[:, cols], other_grad[...]
+            )
+            low = total.astype(bf16)
+            plane, chip = b // 2, 2 * lax.rem(b, 2)
+            at_row = pl.ds(pl.multiple_of((plane // 2) * (BLOCK // 2), BLOCK // 2), BLOCK // 2)
+            at_col = pl.ds(
+                pl.multiple_of(lax.rem(plane, 2) * (width // 2), width // 2), width // 2
+            )
+            place[chip, at_row, at_col] = low[: BLOCK // 2]
+            place[chip + 1, at_row, at_col] = low[BLOCK // 2 :]
+            return carry
+
+        lax.fori_loop(0, blocks, block, 0)
+
+    gate_place = gate_v.at[pl.ds(4, 4)]
+    gradient_into(grad_gate, other_gate, gate_place)
+    gate_scatter = ChipScatter(
+        links,
+        lambda chip: gate_v.at[4 + chip],
+        [down_v.at[3, pl.ds(0, BLOCK // 2)], down_v.at[3, pl.ds(BLOCK // 2, BLOCK // 2)]],
+        [down_v.at[4], down_v.at[5]],
+    )
+    down_scatter.middle()
+    gate_scatter.begin()
+    up_place = up_v.at[pl.ds(0, 4)]
+    gradient_into(grad_up, other_up, up_place)
+    up_copy = links.here(up_place, up_part)
+    up_copy.start()
+    gate_scatter.middle()
+    down_copy = links.here(down_scatter.finish(), down_sum)
+    down_copy.start()
+
+    for copy in group:
+        copy.wait_recv()
+    mid = mid_ref[...]
+    sums = []
+    for which in (0, 1):
+        total = stage[which, fsdp].astype(f32)
+        for slot in range(n_fsdp - 1):
+            total = total + landed[which, slot].astype(f32)
+        sums.append(total)
+    result_ref[...] = (mid + sums[0]).astype(bf16)
+    scale = lax.rsqrt(jnp.mean(mid * mid, axis=-1, keepdims=True) + norm_eps)
+    u = sums[1] * gain_ref[...]
+    inner = jnp.mean(u * mid, axis=-1, keepdims=True)
+    grad_mid = cot_ref[...].astype(f32) + scale * u - mid * (scale * scale * scale * inner)
+    grad_mid_ref[...] = grad_mid
+    grad_proj_ref[...] = grad_mid.astype(bf16)
+
+    gate_copy = links.here(gate_scatter.finish(), gate_sum)
+    gate_copy.start()
+    for copy in swaps + acts + group:
+        copy.wait_send()
+    down_scatter.drain()
+    gate_scatter.drain()
+    for copy in (up_copy, down_copy, gate_copy):
+        copy.wait()
+
+
+def feed_forward(mid, cotangent, gain_ffn, normed_group, cot_group, gate_w, up_w, w_down):
+    f32, bf16 = jnp.float32, jnp.bfloat16
+    n_fsdp = lax.axis_size("fsdp")
+    rows, width = mid.shape
+    group_rows = normed_group.shape[0]
+    units = w_down.shape[0] * BLOCK
+    blocks = units // BLOCK
+    vmem, hbm = pl.BlockSpec(memory_space=pltpu.VMEM), pl.BlockSpec(memory_space=pl.ANY)
+    shape = jax.ShapeDtypeStruct
+    return pl.pallas_call(
+        feed_forward_kernel,
+        name="feed_forward",
+        out_shape=[
+            shape((rows, width), bf16),
+            shape((rows, width), f32),
+            shape((rows, width), bf16),
+            shape((BLOCK, width), bf16),
+            shape((BLOCK, width), bf16),
+            shape((blocks // 2, BLOCK, width), bf16),
         ],
-        axis=-1,
+        in_specs=[vmem] * 5 + [hbm] * 3,
+        out_specs=[vmem] * 3 + [hbm] * 3,
+        scratch_shapes=[
+            pltpu.VMEM((width // BLOCK, BLOCK, units), bf16),
+            pltpu.VMEM((width // BLOCK, BLOCK, units), bf16),
+            pltpu.VMEM((blocks, BLOCK, width), bf16),
+            pltpu.VMEM((group_rows, units), bf16),
+            pltpu.VMEM((group_rows, units), bf16),
+            pltpu.VMEM((group_rows, units), bf16),
+            pltpu.VMEM((group_rows, width), bf16),
+            pltpu.VMEM((group_rows, width), bf16),
+            pltpu.VMEM((group_rows, units // 2), bf16),
+            pltpu.VMEM((group_rows, units // 2), bf16),
+            pltpu.VMEM((group_rows, units // 2), bf16),
+            pltpu.VMEM((2, n_fsdp, rows, width), bf16),
+            pltpu.VMEM((2, n_fsdp - 1, rows, width), bf16),
+            pltpu.SemaphoreType.DMA((48,)),
+            pltpu.SemaphoreType.DMA((48,)),
+            pltpu.SemaphoreType.DMA((8,)),
+            pltpu.SemaphoreType.DMA((3, blocks)),
+            pltpu.SemaphoreType.REGULAR,
+        ],
+        compiler_params=pltpu.CompilerParams(
+            collective_id=2, has_side_effects=True, vmem_limit_bytes=62 * 2**20
+        ),
+    )(mid, cotangent, gain_ffn[None], normed_group, cot_group, gate_w, up_w, w_down)
+
+
+def attention_back_kernel(
+    grad_proj_ref,
+    grad_mid_ref,
+    tokens_ref,
+    gain_ref,
+    w_head_ref,
+    out_head_ref,
+    qkv_ref,
+    attended_ref,
+    cos_ref,
+    sin_ref,
+    pos_col_ref,
+    pos_row_ref,
+    normed_hbm,
+    gate_sum_hbm,
+    up_part_hbm,
+    grad_input_ref,
+    qkv_sum,
+    out_sum,
+    gate_out,
+    up_out,
+    proj,
+    normed,
+    up_part,
+    up_halves,
+    up_sides,
+    grad_att,
+    grads,
+    key_grad,
+    value_grad,
+    part,
+    core_rx,
+    half_rx,
+    side_rx,
+    out_stage,
+    out_landed,
+    head_stage,
+    head_landed,
+    send_sem,
+    recv_sem,
+    local_sem,
+):
+    f32, bf16 = jnp.float32, jnp.bfloat16
+    ctx, fsdp = lax.axis_index("ctx"), lax.axis_index("fsdp")
+    links = Links((send_sem, recv_sem, local_sem), ctx, fsdp)
+    chip, core = ctx // 2, lax.rem(ctx, 2)
+    n_ctx, rows, width = proj.shape
+    n_fsdp = out_landed.shape[0]
+    seq_rows = n_ctx * rows
+    head_columns = out_head_ref.shape[0]
+    strip_rows = out_landed.shape[1]
+    score_scale = 1.0 / math.sqrt(HEAD_SIZE)
+    loads = [links.here(normed_hbm, normed), links.here(up_part_hbm, up_part)]
+    for copy in loads:
+        copy.start()
+
+    flips = [(a, b) for a in range(n_ctx) for b in range(n_fsdp) if a or b]
+    barrier = pltpu.get_barrier_semaphore()
+    for a, b in flips:
+        pl.semaphore_signal(
+            barrier,
+            inc=1,
+            device_id=(lax.bitwise_xor(ctx, a), lax.bitwise_xor(fsdp, b)),
+            device_id_type=MESH,
+        )
+    pl.semaphore_wait(barrier, len(flips))
+
+    proj[ctx] = grad_proj_ref[...]
+    half = rows // 2
+    gather = PlaneGather(
+        links,
+        lambda j: [proj.at[j]],
+        lambda j, which: [proj.at[j, pl.ds(which * half, half)]],
+    )
+    gather.begin()
+
+    def spread(source, dest):
+        half_width = width // 2
+        place = pl.ds(pl.multiple_of((2 * fsdp + core) * half_width, half_width), half_width)
+        copies = []
+        for a in (0, 1):
+            for b in range(n_fsdp):
+                plane = lax.bitwise_xor(fsdp, b)
+                who = lax.bitwise_xor(core, a)
+                at_row = (plane // 2) * (BLOCK // 2) + who * strip_rows
+                block = source.at[
+                    pl.ds(pl.multiple_of(at_row, strip_rows), strip_rows),
+                    pl.ds(pl.multiple_of(lax.rem(plane, 2) * half_width, half_width), half_width),
+                ]
+                target = dest.at[:, place]
+                if a or b:
+                    copies.append(
+                        links.to(block, target, lax.bitwise_xor(ctx, a), plane)
+                    )
+                else:
+                    local = links.here(block, target)
+                    locals_.append(local)
+                    local.start()
+        for copy in copies:
+            copy.start()
+        return copies
+
+    locals_ = []
+    gate_copies = spread(gate_sum_hbm, gate_out)
+    gather.forward()
+    loads[1].wait()
+    up_scatter = ChipScatter(
+        links,
+        lambda q: up_part.at[q],
+        [up_halves.at[0], up_halves.at[1]],
+        [up_sides.at[0], up_sides.at[1]],
+    )
+    up_scatter.begin()
+    gather.finish()
+
+    total = jnp.zeros((head_columns, width), f32)
+    for j in range(0, n_ctx, 2):
+        total = total + lax.dot_general(
+            attended_ref[pl.ds(j * rows, 2 * rows)],
+            proj[pl.ds(j, 2)].reshape(2 * rows, width),
+            (((0,), (0,)), ((), ())),
+            preferred_element_type=f32,
+        )
+    out_stage[...] = total.astype(bf16).reshape(out_stage.shape)
+    half_ctx = n_ctx // 2
+    out_base = links.remote
+    links.remote += n_fsdp
+    out_copies = []
+    plane = out_plane(ctx, fsdp)
+    for j in range(half_ctx):
+        target = half_ctx * core + j
+        away = (target != ctx) | (plane != fsdp)
+        index = links.remote
+        links.remote += 1
+        copy = pltpu.make_async_remote_copy(
+            src_ref=out_stage.at[j],
+            dst_ref=out_landed.at[fsdp],
+            send_sem=send_sem.at[index],
+            recv_sem=recv_sem.at[out_base + fsdp],
+            device_id=(target, plane),
+            device_id_type=MESH,
+        )
+        out_copies.append((away, copy))
+
+        @pl.when(away)
+        def _(copy=copy):
+            copy.start()
+
+    def out_source(source):
+        head = 2 * fsdp + ctx // half_ctx
+        return head_of(head, jnp.int32(source))
+
+    own_out = links.here(out_stage.at[lax.rem(ctx, half_ctx)], out_landed.at[fsdp])
+    own_is_mine = out_source(fsdp) == ctx
+
+    @pl.when(own_is_mine)
+    def _():
+        own_out.start()
+
+    def back(step, carry):
+        at = pl.multiple_of(step * 2 * rows, 2 * rows)
+        tile = proj[pl.ds(2 * step, 2)].reshape(2 * rows, width)
+        grad_att[pl.ds(at, 2 * rows)] = contract_last(tile, out_head_ref[...]).astype(bf16)
+        return carry
+
+    lax.fori_loop(0, n_ctx // 2, back, 0)
+
+    key_grad[...] = jnp.zeros_like(key_grad)
+    value_grad[...] = jnp.zeros_like(value_grad)
+
+    def attend(step, carry):
+        at = pl.ds(pl.multiple_of(step * 2 * rows, 2 * rows), 2 * rows)
+        keys = qkv_ref[:, pl.ds(head_columns, HEAD_SIZE)]
+        values = qkv_ref[:, pl.ds(head_columns + HEAD_SIZE, HEAD_SIZE)]
+        causal = pos_row_ref[...] <= pos_col_ref[at]
+        for column in range(0, head_columns, HEAD_SIZE):
+            cols = pl.ds(column, HEAD_SIZE)
+            query, grad_mixed = qkv_ref[at, cols], grad_att[at, cols]
+            scores = contract_last(query, keys) * score_scale
+            scores = jnp.where(causal, scores, -1e30)
+            shifted = jnp.exp(scores - jnp.max(scores, axis=-1, keepdims=True))
+            probs = shifted * (1.0 / jnp.sum(shifted, axis=-1, keepdims=True))
+            grad_probs = contract_last(grad_mixed, values)
+            delta = jnp.sum(grad_probs * probs, axis=-1, keepdims=True)
+            grad_scores = (probs * (grad_probs - delta)).astype(bf16)
+            value_grad[...] += contract_first(probs.astype(bf16), grad_mixed)
+            key_grad[...] += contract_first(grad_scores, query)
+            grad_query = jnp.dot(grad_scores, keys, preferred_element_type=f32) * score_scale
+            grads[at, cols] = turn(grad_query, cos_ref[at], sin_ref[at], -1.0).astype(bf16)
+        return carry
+
+    lax.fori_loop(0, n_ctx // 2, attend, 0)
+    turned = turn(key_grad[...] * score_scale, cos_ref[...], sin_ref[...], -1.0)
+    grads[:, pl.ds(head_columns, HEAD_SIZE)] = turned.astype(bf16)
+    grads[:, pl.ds(head_columns + HEAD_SIZE, HEAD_SIZE)] = value_grad[...].astype(bf16)
+
+    scatter = PlaneScatter(links, part, core_rx, half_rx, side_rx)
+    for flip, q in scatter.order():
+        at = pl.multiple_of(q * 2 * rows, 2 * rows)
+        out = contract_last(grads[pl.ds(at, 2 * rows)], w_head_ref[...])
+        part[pl.ds(2 * q, 2)] = out.astype(bf16).reshape(2, rows, width)
+        scatter.give(flip, q)
+
+    loads[0].wait()
+    depth = n_ctx * strip_rows
+    head_copies = []
+    for b in (2, 1, 3, 0):
+        plane = lax.bitwise_xor(fsdp, b)
+        cols = pl.ds(pl.multiple_of(plane * depth, depth), depth)
+        total = lax.dot_general(
+            normed[:, :, cols].reshape(seq_rows, depth),
+            grads[...],
+            (((0,), (0,)), ((), ())),
+            preferred_element_type=f32,
+        )
+        head_stage[plane] = total.astype(bf16).reshape(n_ctx, strip_rows, -1)
+        for a in range(n_ctx):
+            target = lax.bitwise_xor(ctx, a)
+            if a or b:
+                copy = links.to(
+                    head_stage.at[plane, target], head_landed.at[ctx, fsdp], target, plane
+                )
+                head_copies.append(copy)
+            else:
+                copy = links.here(head_stage.at[plane, target], head_landed.at[ctx, fsdp])
+                locals_.append(copy)
+            copy.start()
+
+    up_scatter.middle()
+    grad_normed = scatter.run()
+    inputs = tokens_ref[...].astype(f32)
+    scale = lax.rsqrt(jnp.mean(inputs * inputs, axis=-1, keepdims=True) + norm_eps)
+    u = grad_normed * gain_ref[...]
+    inner = jnp.mean(u * inputs, axis=-1, keepdims=True)
+    grad_input_ref[...] = (
+        grad_mid_ref[...] + scale * u - inputs * (scale * scale * scale * inner)
+    )
+    up_copies = spread(up_scatter.finish(), up_out)
+
+    for source in range(n_fsdp):
+        arrival = pltpu.make_async_remote_copy(
+            src_ref=out_stage.at[0],
+            dst_ref=out_landed.at[source],
+            send_sem=send_sem.at[out_base],
+            recv_sem=recv_sem.at[out_base + source],
+            device_id=(lax.bitwise_xor(ctx, 1), fsdp),
+            device_id_type=MESH,
+        )
+        outside = (out_source(source) != ctx) | (fsdp != source)
+
+        @pl.when(outside)
+        def _(arrival=arrival):
+            arrival.wait_recv()
+
+    @pl.when(own_is_mine)
+    def _():
+        own_out.wait()
+
+    total = out_landed[0].astype(f32)
+    for source in range(1, n_fsdp):
+        total = total + out_landed[source].astype(f32)
+    out_sum[...] = total
+    for copy in head_copies:
+        copy.wait_recv()
+    for copy in locals_:
+        copy.wait()
+    query_columns = QUERY_HEADS * HEAD_SIZE
+    key_columns = KEY_VALUE_HEADS * HEAD_SIZE
+    for head in range(KEY_VALUE_HEADS):
+        total = head_landed[head, 0].astype(f32)
+        for source in range(1, n_fsdp):
+            total = total + head_landed[head ^ (4 * (source % 2)), source].astype(f32)
+        qkv_sum[:, pl.ds(head * head_columns, head_columns)] = total[:, :head_columns]
+        qkv_sum[:, pl.ds(query_columns + head * HEAD_SIZE, HEAD_SIZE)] = total[
+            :, head_columns : head_columns + HEAD_SIZE
+        ]
+        qkv_sum[:, pl.ds(query_columns + key_columns + head * HEAD_SIZE, HEAD_SIZE)] = total[
+            :, head_columns + HEAD_SIZE :
+        ]
+    for copy in gate_copies + up_copies:
+        copy.wait_recv()
+    for copy in gate_copies + up_copies + head_copies:
+        copy.wait_send()
+    for away, copy in out_copies:
+
+        @pl.when(away)
+        def _(copy=copy):
+            copy.wait_send()
+
+    gather.drain()
+    scatter.drain()
+    up_scatter.drain()
+
+
+def attention_back(
+    grad_proj,
+    grad_mid,
+    tokens,
+    gain_attn,
+    w_head,
+    out_head,
+    qkv,
+    attended,
+    cos,
+    sin,
+    key_pos,
+    normed,
+    gate_sum,
+    up_part,
+):
+    f32, bf16 = jnp.float32, jnp.bfloat16
+    n_ctx, n_fsdp = lax.axis_size("ctx"), lax.axis_size("fsdp")
+    rows, width = tokens.shape
+    seq_rows = n_ctx * rows
+    strip_rows = width // (n_ctx * n_fsdp)
+    head_columns, all_columns = attended.shape[1], qkv.shape[1]
+    vmem, hbm = pl.BlockSpec(memory_space=pltpu.VMEM), pl.BlockSpec(memory_space=pl.ANY)
+    shape = jax.ShapeDtypeStruct
+    return pl.pallas_call(
+        attention_back_kernel,
+        name="attention_back",
+        out_shape=[
+            shape((rows, width), f32),
+            shape((strip_rows, (QUERY_HEADS + 2 * KEY_VALUE_HEADS) * HEAD_SIZE), f32),
+            shape((strip_rows, width), f32),
+            shape((strip_rows, n_fsdp * width), bf16),
+            shape((strip_rows, n_fsdp * width), bf16),
+        ],
+        in_specs=[vmem] * 12 + [hbm] * 3,
+        out_specs=[vmem] * 3 + [hbm] * 2,
+        scratch_shapes=[
+            pltpu.VMEM((n_ctx, rows, width), bf16),
+            pltpu.VMEM((n_ctx, rows, width), bf16),
+            pltpu.VMEM(up_part.shape, bf16),
+            pltpu.VMEM((2, BLOCK // 2, width), bf16),
+            pltpu.VMEM((2, BLOCK, width), bf16),
+            pltpu.VMEM((seq_rows, head_columns), bf16),
+            pltpu.VMEM((seq_rows, all_columns), bf16),
+            pltpu.VMEM((seq_rows, HEAD_SIZE), f32),
+            pltpu.VMEM((seq_rows, HEAD_SIZE), f32),
+            pltpu.VMEM((n_ctx, rows, width), bf16),
+            pltpu.VMEM((n_ctx // 2, rows, width), bf16),
+            pltpu.VMEM((2, rows // 2, width), bf16),
+            pltpu.VMEM((2, rows, width), bf16),
+            pltpu.VMEM((n_ctx // 2, strip_rows, width), bf16),
+            pltpu.VMEM((n_fsdp, strip_rows, width), bf16),
+            pltpu.VMEM((n_fsdp, n_ctx, strip_rows, all_columns), bf16),
+            pltpu.VMEM((n_ctx, n_fsdp, strip_rows, all_columns), bf16),
+            pltpu.SemaphoreType.DMA((96,)),
+            pltpu.SemaphoreType.DMA((96,)),
+            pltpu.SemaphoreType.DMA((8,)),
+        ],
+        compiler_params=pltpu.CompilerParams(
+            collective_id=3, has_side_effects=True, vmem_limit_bytes=62 * 2**20
+        ),
+    )(
+        grad_proj,
+        grad_mid,
+        tokens,
+        gain_attn[None],
+        w_head,
+        out_head,
+        qkv,
+        attended,
+        cos,
+        sin,
+        key_pos[:, None],
+        key_pos[None],
+        normed,
+        gate_sum,
+        up_part,
     )
 
 
@@ -847,25 +1536,20 @@
     w_down,
     pair_block,
 ):
-    f32, bf16 = jnp.float32, jnp.bfloat16
+    f32 = jnp.float32
     n_ctx, n_fsdp = lax.axis_size("ctx"), lax.axis_size("fsdp")
     ctx, fsdp = lax.axis_index("ctx"), lax.axis_index("fsdp")
     token_rows, width = tokens.shape
-    group_count = QUERY_HEADS // KEY_VALUE_HEADS
-    head_columns = group_count * HEAD_SIZE
-    query_columns = QUERY_HEADS * HEAD_SIZE
-    key_columns = KEY_VALUE_HEADS * HEAD_SIZE
-    score_scale = 1.0 / math.sqrt(HEAD_SIZE)
     depth = query_key_value_weight.shape[0]
-    hidden_cols = w_down.shape[0]
 
     key_pos, own_pos = positions(pair_block, token_rows)
-
     frequency = jnp.exp(
         jnp.arange(HEAD_SIZE // 2, dtype=f32) * (-2.0 * math.log(rope_base) / HEAD_SIZE)
     )
     angles = key_pos.astype(f32)[:, None] * frequency[None, :]
     cosine, sine_val = jnp.cos(angles), jnp.sin(angles)
+    cos = jnp.concatenate([cosine, cosine], axis=1)
+    sin = jnp.concatenate([-sine_val, sine_val], axis=1)
     (
         mid,
         normed_two_group,
@@ -873,7 +1557,7 @@
         gate_w,
         up_w,
         qkv,
-        attended_b,
+        attended,
         normed_one_seq,
         w_head,
         out_head,
@@ -886,122 +1570,38 @@
         w_out,
         w_gate,
         w_up,
-        jnp.concatenate([cosine, cosine], axis=1),
-        jnp.concatenate([-sine_val, sine_val], axis=1),
+        cos,
+        sin,
         key_pos,
     )
-    inputs_f = tokens.astype(f32)
-    normed_one_seq = normed_one_seq.reshape(-1, width)
-    queries = qkv[:, :head_columns].reshape(-1, group_count, HEAD_SIZE).transpose(1, 0, 2)
-    keys = qkv[:, head_columns : head_columns + HEAD_SIZE]
-    values = qkv[:, head_columns + HEAD_SIZE :]
-    causal = key_pos[None, :] <= key_pos[:, None]
-    scores = jnp.einsum("gqd,kd->gqk", queries, keys, preferred_element_type=f32) * score_scale
-    scores = jnp.where(causal, scores, -1e30)
-    shifted = jnp.exp(scores - jnp.max(scores, axis=-1, keepdims=True))
-    probs = shifted / jnp.sum(shifted, axis=-1, keepdims=True)
-    probs_low = probs.astype(bf16)
-
-    mid_scale = lax.rsqrt(jnp.mean(mid * mid, axis=-1, keepdims=True) + norm_eps)
-    gate = jnp.dot(normed_two_group, gate_w, preferred_element_type=f32)
-    up = jnp.dot(normed_two_group, up_w, preferred_element_type=f32)
-    sig = jax.nn.sigmoid(gate)
-    silu = gate * sig
-    hidden_b = (silu * up).astype(bf16)
-    down_part = jnp.dot(hidden_b, w_down, preferred_element_type=f32)
-    grad_hidden = contract_last(cot_group, w_down)
-    grad_gate_b = (grad_hidden * up * sig * (1.0 + gate * (1.0 - sig))).astype(bf16)
-    grad_up_b = (grad_hidden * silu).astype(bf16)
-    normed_part = contract_last(grad_gate_b, gate_w) + contract_last(grad_up_b, up_w)
-    result = (
-        mid
-        + lax.psum_scatter(
-            down_part.astype(bf16), "fsdp", scatter_dimension=0, tiled=True
-        ).astype(f32)
-    ).astype(bf16)
-    grad_normed_two = lax.psum_scatter(
-        normed_part.astype(bf16), "fsdp", scatter_dimension=0, tiled=True
-    ).astype(f32)
-    u = grad_normed_two * gain_ffn
-    grad_mid = (
-        cotangent.astype(f32)
-        + mid_scale * u
-        - mid * mid_scale**3 * jnp.mean(u * mid, axis=-1, keepdims=True)
-    )
-
-    grad_down_part = contract_first(hidden_b, cot_group)
-    grad_gate_part = contract_first(normed_two_group, grad_gate_b)
-    grad_up_part = contract_first(normed_two_group, grad_up_b)
-    grad_down = lax.psum_scatter(
-        grad_down_part.astype(bf16), "ctx", scatter_dimension=0, tiled=True
-    ).astype(f32)
-
-    def spread(part):
-        blocks = part.astype(bf16).reshape(n_fsdp, n_ctx, depth // n_ctx, hidden_cols)
-        blocks = blocks.transpose(1, 0, 2, 3).reshape(width, hidden_cols)
-        mine = lax.psum_scatter(blocks, "ctx", scatter_dimension=0, tiled=True)
-        mine = mine.reshape(n_fsdp, depth // n_ctx, hidden_cols)
-        return lax.all_to_all(mine, "fsdp", split_axis=0, concat_axis=2, tiled=True).reshape(
-            depth // n_ctx, n_fsdp * hidden_cols
-        )
-
-    grad_gate, grad_up = spread(grad_gate_part).astype(f32), spread(grad_up_part).astype(f32)
-
-    grad_proj_b = grad_mid.astype(bf16)
-    grad_proj_seq = lax.all_gather(grad_proj_b, "ctx", axis=0, tiled=True)
-    grad_att = contract_last(grad_proj_seq, out_head).astype(bf16)
-    grad_att = grad_att.reshape(-1, group_count, HEAD_SIZE).transpose(1, 0, 2)
-    grad_out_part = contract_first(attended_b, grad_proj_seq)
-    grad_values = jnp.einsum("gqk,gqd->kd", probs_low, grad_att, preferred_element_type=f32)
-    grad_probs = jnp.einsum("gqd,kd->gqk", grad_att, values, preferred_element_type=f32)
-    delta = jnp.sum(grad_probs * probs, axis=-1, keepdims=True)
-    grad_scores = (probs * (grad_probs - delta)).astype(bf16)
-    grad_queries = score_scale * jnp.einsum(
-        "gqk,kd->gqd", grad_scores, keys, preferred_element_type=f32
-    )
-    grad_keys = score_scale * jnp.einsum(
-        "gqk,gqd->kd", grad_scores, queries, preferred_element_type=f32
-    )
-    grad_projected = jnp.concatenate(
-        [rotate_heads(grad_queries[g], cosine, sine_val, -1.0) for g in range(group_count)]
-        + [rotate_heads(grad_keys, cosine, sine_val, -1.0), grad_values],
-        axis=1,
-    ).astype(bf16)
-    normed_one_part = contract_last(grad_projected, w_head)
-    grad_normed_one = lax.psum_scatter(
-        normed_one_part.astype(bf16), "ctx", scatter_dimension=0, tiled=True
-    ).astype(f32)
-    in_scale = lax.rsqrt(jnp.mean(inputs_f * inputs_f, axis=-1, keepdims=True) + norm_eps)
-    u = grad_normed_one * gain_attn
-    grad_input = (
-        grad_mid
-        + in_scale * u
-        - inputs_f * in_scale**3 * jnp.mean(u * inputs_f, axis=-1, keepdims=True)
-    )
-
-    grad_head_part = contract_first(normed_one_seq, grad_projected).astype(bf16)
-    blocks = grad_head_part.reshape(n_fsdp, n_ctx, depth // n_ctx, -1).transpose(1, 0, 2, 3)
-    blocks = blocks.reshape(n_ctx * n_fsdp, depth // n_ctx, -1)
-    got = lax.all_to_all(blocks, ("ctx", "fsdp"), split_axis=0, concat_axis=0, tiled=True)
-    got = got.astype(f32)
-    sums = [
-        sum(got[(h ^ (4 * (f % 2))) * n_fsdp + f] for f in range(n_fsdp))
-        for h in range(KEY_VALUE_HEADS)
-    ]
-    grad_qkv = jnp.concatenate(
-        [s[:, :head_columns] for s in sums]
-        + [s[:, head_columns : head_columns + HEAD_SIZE] for s in sums]
-        + [s[:, head_columns + HEAD_SIZE :] for s in sums],
-        axis=1,
-    )
-    strip_rows = depth // n_ctx
-    placed = lax.dynamic_update_slice(
-        jnp.zeros((n_ctx, n_fsdp, strip_rows, width), bf16),
-        grad_out_part.astype(bf16).reshape(-1, 1, strip_rows, width),
-        (4 * lax.rem(ctx, 2), out_plane(ctx, fsdp), 0, 0),
-    ).reshape(n_ctx * n_fsdp, strip_rows, width)
-    out_got = lax.all_to_all(placed, ("ctx", "fsdp"), split_axis=0, concat_axis=0, tiled=True)
-    grad_out = jnp.sum(out_got.astype(f32), axis=0)
+    result, grad_mid, grad_proj, down_sum, gate_sum, up_part = feed_forward(
+        mid,
+        cotangent,
+        gain_ffn,
+        normed_two_group,
+        cot_group,
+        gate_w,
+        up_w,
+        w_down.reshape(-1, BLOCK, width),
+    )
+    grad_input, grad_qkv, grad_out, gate_low, up_low = attention_back(
+        grad_proj,
+        grad_mid,
+        tokens,
+        gain_attn,
+        w_head,
+        out_head,
+        qkv,
+        attended,
+        cos,
+        sin,
+        key_pos,
+        normed_one_seq,
+        gate_sum,
+        up_part,
+    )
+    grad_down = down_sum.astype(f32)
+    grad_gate, grad_up = gate_low.astype(f32), up_low.astype(f32)
 
     my_rows = ctx * (depth // n_ctx)
     rows_of = lambda matrix: lax.dynamic_slice_in_dim(

time: 839 us -> 527 us (0.63)
  waiting for transfers between devices: 372 us -> 2.27 us
  Pallas kernels: 221 us -> 490 us
  matrix products: 123 us -> 0 us
  local copies, waits for them, and re-layouts: 45.8 us -> 5.66 us
  other arithmetic: 36.5 us -> 15.1 us
  starting transfers between devices: 20.9 us -> 3.34 us
  between operations: 15.5 us -> 0.98 us
    pallas_call x0 -> x2, Pallas kernels: none -> 268 us  [the longest x1 151 us: attention_back(): pl.pallas_call(attention_back_kernel, name='attention_back', out_shape=[s...]
    ppermute x1, waiting for transfers between devices: 181 us -> 2.27 us  [local_heads(): lax.ppermute(jnp.stack([attn_sum, ffn_sum]), ('ctx', 'fsdp'), gain_pairs)]
    reduce_scatter x6 -> x0, waiting for transfers between devices: 139 us -> none  [the longest x2 95.5 us: spread(): mine = lax.psum_scatter(blocks, 'ctx', scatter_dimension=0, tiled=True)]
    dot_general x17 -> x0, matrix products: 117 us -> none  [the longest x5 39.3 us: contract_last(): lax.dot_general(left, right, (((1,), (1,)), ((), ())), preferred_element_...]
    all_to_all x4 -> x0, waiting for transfers between devices: 53.1 us -> none  [the longest x1 38.9 us: local_heads(): lax.all_to_all(blocks, ('ctx', 'fsdp'), split_axis=0, concat_axis=0, tile...]
    reshape x2 -> x0, local copies, waits for them, and re-layouts: 16.7 us -> none  [spread(): part.astype(bf16).reshape(n_fsdp, n_ctx, depth // n_ctx, hidden_cols)]
    all_to_all x4 -> x0, starting transfers between devices: 16.5 us -> none  [the longest x2 8.85 us: spread(): lax.all_to_all(mine, 'fsdp', split_axis=0, concat_axis=2, tiled=True)]
    unnamed x97 -> x16, local copies, waits for them, and re-layouts: 16 us -> 4.64 us
  transfers between devices with their start and end apart: 12 -> 1, of which waited for: 6 -> 1; matrix products, arithmetic and copies ran while one was open for 16% -> 0% of each run, Pallas kernels for 0% -> 0%
where the time goes in v3:
time: 527 us; the launch traced here: 517 us
  Pallas kernels  490 us (93%)
  other arithmetic  15.1 us (3%)
  local copies, waits for them, and re-layouts  5.66 us (1%)
    pallas_call x1, Pallas kernels, attention_forward(): pl.pallas_call(attention_kernel, name='attention_forward', out_shape=[sha...  221 us
    pallas_call x1, Pallas kernels, attention_back(): pl.pallas_call(attention_back_kernel, name='attention_back', out_shape=[s...  151 us
    pallas_call x1, Pallas kernels, feed_forward(): pl.pallas_call(feed_forward_kernel, name='feed_forward', out_shape=[shape...  117 us
  transfers between devices with their start and end apart: 1, of which 1 were waited for; matrix products, arithmetic and copies ran while one was open for 0% of the time, Pallas kernels for 0%

profile of v3, /device:TPU:5, one launch (start us, length us, event | category | flops | bytes accessed | tf_op | source)
XLA Modules:
  0.0 517.1 jit_solution(1065223004832363157)
XLA Ops:
  0.7 0.7 broadcast_subtract_fusion
  1.3 0.7 multiply_add_fusion
  2.1 1.0 copy.19.pos_col_ref
  3.1 1.9 fusion
  5.0 1.3 pad_maximum_fusion
  6.3 0.0 copy-done.5
  6.3 221.3 %attention_forward.1 = (f32[128,2048]{1,0:T(8,128)}, bf16[512,2048]{1,0:T(8,128)(2,1)}, bf16[512,2048]{1,0:T(8,128)(2,1)}, bf16[8,256,2048]{2,1,0:T(8,128)(2,1)}...) custom-call(bf16[128,2048]{1,0:T(8,128)(2,1)} %tokens_ref.3, ...), custom_call_target="tpu_custom_call" | custom-call | tf_op jit(solution)/shard_map/attention_forward/pallas_call | solution.py:779
  227.7 117.1 %feed_forward.1 = (bf16[128,2048]{1,0:T(8,128)(2,1)}, f32[128,2048]{1,0:T(8,128)}, bf16[128,2048]{1,0:T(8,128)(2,1)}, bf16[256,2048]{1,0:T(8,128)(2,1)}, bf16[25...) custom-call(f32[128,2048]{1,0:T(8,128)} %get-tuple-element.30.mid_ref, bf16[128,2048]{1,0:T(8,128)(2,1)} %cot_ref.3, ...), custom_call_target="tpu_custom_call" | custom-call | tf_op jit(solution)/shard_map/feed_forward/pallas_call | solution.py:1114
  344.7 151.3 %attention_back.1 = (f32[128,2048]{1,0:T(8,128)}, f32[64,4096]{1,0:T(8,128)}, f32[64,2048]{1,0:T(8,128)}, bf16[64,8192]{1,0:T(8,128)(2,1)}, bf16[64,8192]{1,0:T(8,128)(2,1)}) custom-call(bf16[128,2048]{1,0:T(8,128)(2,1)} %get-tuple-element.36.grad_proj_ref, f32[128,2048]{1,0:T(8,128)} %get-tuple-element.37.grad_mid_ref, bf16[128,2048]{1,0:T(8,128)(2,1)} %tokens_ref.3, ...), custom_call_target="tpu_custom_call" | custom-call | tf_op jit(solution)/shard_map/attention_back/pallas_call | solution.py:1471
  496.0 0.0 copy-start.2
  496.1 3.3 multiply_reduce_fusion
  499.4 0.0 copy-done.2
  499.4 3.1 multiply_reduce_fusion.1
  502.5 1.3 multiply_reduce_fusion.2
  503.8 3.3 collective-permute-start
  507.1 0.0 copy-done.1
  507.1 0.0 copy-start.3
  507.1 1.6 convert_element_type.35
  508.7 2.3 collective-permute-done
  511.0 1.3 bitcast_divide_fusion
  512.3 1.9 copy.25
  514.2 1.0 copy.26
  515.1 1.0 copy.27
  516.1 0.8 copy.28
  (12 shorter events, 0.0 us)
Async XLA Ops:
  2.1 4.2 copy-start.5
  496.0 3.3 copy-start.2
  499.4 3.1 copy-start
  499.4 7.7 %copy-start.1 = (bf16[256,2048]{1,0:T(8,128)(2,1)S(1)}, bf16[256,2048]{1,0:T(8,128)(2,1)}, u32[]{:S(2)}) copy-start(bf16[256,2048]{1,0:T(8,128)(2,1)} %get-tuple-element.50) | copy-start | bytes 3145732
  503.8 7.2 %collective-permute-start = (f32[2,64]{1,0:T(2,128)S(1)}, f32[2,64]{1,0:T(2,128)S(1)}, u32[]{:S(2)}, u32[]{:S(2)}) collective-permute-start(f32[2,64]{1,0:T(2,128)S(1)} %pad_maximum_fusion.2), channel_id=1, source_target_pairs={{0,0},{1,8},{2,16},{3,24},{4,1},{5,9},{6,17},{7,25},{8,2},{9,10},{... | collective-permute-start | bytes 1544 | tf_op jit(solution)/shard_map/ppermute | solution.py:1617
  507.1 7.0 %copy-start.3 = (f32[128,2048]{1,0:T(8,128)S(1)}, f32[128,2048]{1,0:T(8,128)}, u32[]{:S(2)}) copy-start(f32[128,2048]{1,0:T(8,128)} %get-tuple-element.74) | copy-start | bytes 3145732
  514.2 1.9 copy-start.4

commit v4 on v3

--- a/solution.py
+++ b/solution.py
@@ -363,24 +363,64 @@
             device_id_type=MESH,
         )
 
+    def flip(self, src, dst, ctx_flip, fsdp_flip):
+        return self.to(
+            src, dst, lax.bitwise_xor(self.ctx, ctx_flip), lax.bitwise_xor(self.fsdp, fsdp_flip)
+        )
+
     def plane(self, src, dst, flip):
-        return self.to(src, dst, lax.bitwise_xor(self.ctx, flip), self.fsdp)
+        return self.flip(src, dst, flip, 0)
 
     def column(self, src, dst, flip):
-        return self.to(src, dst, self.ctx, lax.bitwise_xor(self.fsdp, flip))
+        return self.flip(src, dst, 0, flip)
 
     def here(self, src, dst):
         index, self.locals = self.locals, self.locals + 1
         return pltpu.make_async_copy(src, dst, self.local_sem.at[index])
 
 
-def greet(ctx, fsdp):
+PLANE_FLIPS = [(1, 0), (2, 0), (4, 0)]
+COLUMN_FLIPS = [(0, 1), (0, 2), (0, 3)]
+
+
+def greet(ctx, fsdp, flips):
     barrier = pltpu.get_barrier_semaphore()
-    partners = [(lax.bitwise_xor(ctx, flip), fsdp) for flip in (1, 2, 4)]
-    partners += [(ctx, lax.bitwise_xor(fsdp, flip)) for flip in (1, 2, 3)]
-    for partner in partners:
-        pl.semaphore_signal(barrier, inc=1, device_id=partner, device_id_type=MESH)
-    pl.semaphore_wait(barrier, len(partners))
+    for a, b in flips:
+        pl.semaphore_signal(
+            barrier,
+            inc=1,
+            device_id=(lax.bitwise_xor(ctx, a), lax.bitwise_xor(fsdp, b)),
+            device_id_type=MESH,
+        )
+    pl.semaphore_wait(barrier, len(flips))
+
+
+def start_all(copies):
+    for copy in copies:
+        copy.start()
+
+
+class LineGather:
+    def __init__(self, links, own, group):
+        self.links, self.group = links, group
+        self.home = links.here(own, group.at[0])
+        self.near = links.column(own, group.at[2], 1)
+        self.far = links.column(own, group.at[1], 2)
+        self.relay = links.column(group.at[1], group.at[3], 1)
+
+    def begin(self):
+        start_all([self.far, self.near, self.home])
+
+    def forward(self):
+        self.far.wait_recv()
+        self.relay.start()
+
+    def finish(self):
+        self.near.wait_recv()
+        self.relay.wait_recv()
+        for copy in (self.near, self.far, self.relay):
+            copy.wait_send()
+        self.home.wait()
 
 
 class PlaneGather:
@@ -400,11 +440,12 @@
         refs = self.blocks(index)
         self.cores += self._go([self.links.plane(r, r, ACROSS_CORE) for r in refs])
 
-    def begin(self):
+    def begin(self, sources=None):
         refs = self.blocks(self.ctx)
-        self.from_x = self._go([self.links.plane(r, r, ACROSS_X) for r in refs])
-        self.from_y = self._go([self.links.plane(r, r, ACROSS_Y) for r in refs])
-        self._core(self.ctx)
+        pairs = list(zip(sources or refs, refs))
+        self.from_x = self._go([self.links.plane(s, r, ACROSS_X) for s, r in pairs])
+        self.from_y = self._go([self.links.plane(s, r, ACROSS_Y) for s, r in pairs])
+        self.cores += self._go([self.links.plane(s, r, ACROSS_CORE) for s, r in pairs])
 
     def forward(self):
         index = lax.bitwise_xor(self.ctx, ACROSS_X)
@@ -462,35 +503,33 @@
         total = mine[...].astype(jnp.float32) + self.core_rx[chip].astype(jnp.float32)
         return mine, total
 
-    def run(self):
-        half = self.half_rx.shape[1]
+    def begin(self):
+        half = self.half = self.half_rx.shape[1]
         mine, total = self._summed(3)
         mine[...] = total.astype(jnp.bfloat16)
-        top = self._go(
-            self.links.plane(mine.at[pl.ds(0, half)], self.half_rx.at[0], ACROSS_Y)
-        )
-        bottom = self._go(
-            self.links.plane(mine.at[pl.ds(half, half)], self.half_rx.at[1], ACROSS_X)
-        )
-        sides = []
-        for flip, copy, slot in ((1, top, 0), (2, bottom, 1)):
+        self.corner = [
+            self._go(self.links.plane(mine.at[pl.ds(0, half)], self.half_rx.at[0], ACROSS_Y)),
+            self._go(
+                self.links.plane(mine.at[pl.ds(half, half)], self.half_rx.at[1], ACROSS_X)
+            ),
+        ]
+
+    def middle(self):
+        self.sides = []
+        for flip, across, slot in ((1, ACROSS_X, 0), (2, ACROSS_Y, 1)):
             mine, total = self._summed(flip)
             mine[...] = total.astype(jnp.bfloat16)
-            copy.wait_recv()
-            rows = pl.ds(slot * half, half)
+            self.corner[slot].wait_recv()
+            rows = pl.ds(slot * self.half, self.half)
             mine[rows] = (
-                total[slot * half : (slot + 1) * half]
+                total[slot * self.half : (slot + 1) * self.half]
                 + self.half_rx[slot].astype(jnp.float32)
             ).astype(jnp.bfloat16)
-            sides.append(
-                self._go(
-                    self.links.plane(
-                        mine, self.side_rx.at[slot], ACROSS_X if slot == 0 else ACROSS_Y
-                    )
-                )
-            )
+            self.sides.append(self._go(self.links.plane(mine, self.side_rx.at[slot], across)))
+
+    def finish(self):
         mine, total = self._summed(0)
-        for slot, copy in enumerate(sides):
+        for slot, copy in enumerate(self.sides):
             copy.wait_recv()
             total = total + self.side_rx[slot].astype(jnp.float32)
         return total
@@ -500,12 +539,8 @@
             copy.wait_send()
 
 
-def head_of(ctx, fsdp):
-    return lax.bitwise_xor(ctx, 4 * lax.rem(fsdp, 2))
-
-
-def out_plane(ctx, fsdp):
-    return lax.bitwise_xor(ctx // 2, 2 * lax.rem(fsdp, 2))
+def swap_bits(fsdp):
+    return 2 * lax.rem(fsdp, 2) + fsdp // 2
 
 
 def turn(vectors, cos_rows, sin_rows, sign):
@@ -527,7 +562,8 @@
     pos_row_ref,
     mid_ref,
     normed_two_group,
-    cot_group,
+    cot_near,
+    cot_far,
     gate_w,
     up_w,
     qkv_out,
@@ -538,6 +574,7 @@
     normed,
     w_head,
     out_head,
+    out_relay,
     qkv,
     attended,
     part,
@@ -565,29 +602,74 @@
     score_scale = 1.0 / math.sqrt(HEAD_SIZE)
     finals = []
 
-    greet(ctx, fsdp)
-
-    my_rows = pl.ds(pl.multiple_of(fsdp * depth, depth), depth)
-
-    def head_parts(head):
-        starts = (
-            (head * head_columns, head_columns, 0),
-            (query_columns + head * HEAD_SIZE, HEAD_SIZE, head_columns),
-            (query_columns + key_columns + head * HEAD_SIZE, HEAD_SIZE, head_columns + HEAD_SIZE),
-        )
-        for start, size, place in starts:
-            yield (
+    greet(ctx, fsdp, PLANE_FLIPS + COLUMN_FLIPS + [(6, 0)])
+
+    out_block = out_w_ref.at[
+        pl.ds(pl.multiple_of(lax.rem(ctx, 2) * head_columns, head_columns), head_columns)
+    ]
+    out_target = swap_bits(lax.bitwise_xor(ctx // 2, fsdp))
+    out_away = out_target != fsdp
+    out_copy = links.to(out_block, out_relay, ctx, out_target)
+    out_home = links.here(out_block, out_relay)
+    out_flip = 2 * swap_bits(fsdp)
+    out_moves = fsdp != 0
+    out_last = links.to(out_relay, out_head, lax.bitwise_xor(ctx, out_flip), fsdp)
+    out_stays = links.here(out_relay, out_head)
+
+    @pl.when(out_away)
+    def _():
+        out_copy.start()
+
+    @pl.when(jnp.logical_not(out_away))
+    def _():
+        out_home.start()
+
+    def rows_of(plane):
+        return pl.ds(pl.multiple_of(plane * depth, depth), depth)
+
+    head_parts = []
+    for start, size, place in (
+        (ctx * head_columns, head_columns, 0),
+        (query_columns + ctx * HEAD_SIZE, HEAD_SIZE, head_columns),
+        (query_columns + key_columns + ctx * HEAD_SIZE, HEAD_SIZE, head_columns + HEAD_SIZE),
+    ):
+        head_parts.append(
+            (
                 qkv_w_ref.at[:, pl.ds(pl.multiple_of(start, HEAD_SIZE), size)],
-                w_head.at[my_rows, pl.ds(place, size)],
+                w_head.at[rows_of(fsdp), pl.ds(place, size)],
             )
-
-    head_copies = []
+        )
+    head_far = [links.column(src, dst, 2) for src, dst in head_parts]
+    head_near = [links.column(src, dst, 1) for src, dst in head_parts]
+    own_head = [links.here(src, dst) for src, dst in head_parts]
+    start_all(head_far + head_near + own_head)
+
+    def place_of(j):
+        return pl.ds(pl.multiple_of(j * strip, strip), strip)
+
+    def strips(target):
+        cols = pl.ds(pl.multiple_of(target * hidden + ctx * strip, strip), strip)
+        blocks = pl.ds(fsdp * depth_blocks, depth_blocks)
+        for source, dest in ((gate_ref, gate_w), (up_ref, up_w)):
+            yield source.at[:, :, cols], dest.at[blocks, :, place_of(ctx)]
+
+    strip_copies = [[links.here(src, dst) for src, dst in strips(fsdp)]]
     for flip in (1, 2, 3):
-        for src, dst in head_parts(head_of(ctx, lax.bitwise_xor(fsdp, flip))):
-            head_copies.append(links.column(src, dst, flip))
-    own_head = [links.here(src, dst) for src, dst in head_parts(head_of(ctx, fsdp))]
-    for copy in head_copies + own_head:
-        copy.start()
+        strip_copies.append(
+            [links.column(s, d, flip) for s, d in strips(lax.bitwise_xor(fsdp, flip))]
+        )
+    start_all(strip_copies[0])
+
+    def strip_gather(flip):
+        first = lax.bitwise_xor(fsdp, flip) * depth_blocks
+        blocks = pl.ds(first, depth_blocks)
+        return PlaneGather(
+            links,
+            lambda j: [w.at[blocks, :, place_of(j)] for w in (gate_w, up_w)],
+            lambda j, which: [w.at[first + which, :, place_of(j)] for w in (gate_w, up_w)],
+        )
+
+    weights = [strip_gather(flip) for flip in range(n_fsdp)]
 
     inputs = tokens_ref[...].astype(f32)
     scale = lax.rsqrt(jnp.mean(inputs * inputs, axis=-1, keepdims=True) + norm_eps)
@@ -600,58 +682,39 @@
     )
     gather.begin()
     gather.forward()
+    weights[0].begin([source for source, dest in strips(fsdp)])
     gather.finish()
+
+    @pl.when(out_away)
+    def _():
+        out_copy.wait_recv()
+
+    @pl.when(jnp.logical_not(out_away))
+    def _():
+        out_home.wait()
+
+    @pl.when(out_moves)
+    def _():
+        out_last.start()
+
+    @pl.when(jnp.logical_not(out_moves))
+    def _():
+        out_stays.start()
+
+    weights[0].forward()
+    for copy in head_far:
+        copy.wait_recv()
+    far_rows = w_head.at[rows_of(lax.bitwise_xor(fsdp, 2))]
+    head_relay = links.column(far_rows, far_rows, 1)
+    head_relay.start()
+    weights[0].finish()
     finals.append(links.here(normed, normed_one_out))
     finals[-1].start()
     for copy in own_head:
         copy.wait()
-    for copy in head_copies:
+    for copy in head_near + [head_relay]:
         copy.wait_recv()
-
-    out_block = out_w_ref.at[
-        pl.ds(pl.multiple_of(lax.rem(ctx, 2) * head_columns, head_columns), head_columns)
-    ]
-    out_sends = []
-    slot = links.remote
-    out_slot = links.column(out_block, out_head, 1)
-    out_home = links.here(out_block, out_head)
-    home = out_plane(ctx, fsdp) == fsdp
-    for target in range(n_fsdp):
-        wanted = (out_plane(ctx, jnp.int32(target)) == fsdp) & (fsdp != target)
-        copy = pltpu.make_async_remote_copy(
-            src_ref=out_block,
-            dst_ref=out_head,
-            send_sem=send_sem.at[links.remote],
-            recv_sem=recv_sem.at[slot],
-            device_id=(ctx, jnp.int32(target)),
-            device_id_type=MESH,
-        )
-        links.remote += 1
-        out_sends.append((wanted, copy))
-
-        @pl.when(wanted)
-        def _(copy=copy):
-            copy.start()
-
-    @pl.when(home)
-    def _():
-        out_home.start()
-
-    block_rows_of = pl.ds(fsdp * depth_blocks, depth_blocks)
-
-    def strips(target):
-        cols = pl.ds(pl.multiple_of(target * hidden + ctx * strip, strip), strip)
-        place = pl.ds(pl.multiple_of(ctx * strip, strip), strip)
-        for source, dest in ((gate_ref, gate_w), (up_ref, up_w)):
-            yield source.at[:, :, cols], dest.at[block_rows_of, :, place]
-
-    strip_copies = []
-    for flip in (1, 2, 3):
-        for src, dst in strips(lax.bitwise_xor(fsdp, flip)):
-            strip_copies.append(links.column(src, dst, flip))
-    own_strips = [links.here(src, dst) for src, dst in strips(fsdp)]
-    for copy in strip_copies + own_strips:
-        copy.start()
+    start_all(strip_copies[1] + strip_copies[2] + strip_copies[3])
 
     block_rows = 2 * rows
 
@@ -668,7 +731,6 @@
         return carry
 
     lax.fori_loop(0, seq_rows // block_rows, project, 0)
-
     def attend(step, carry):
         at = pl.multiple_of(step * block_rows, block_rows)
         keys = qkv[:, pl.ds(head_columns, HEAD_SIZE)]
@@ -686,16 +748,15 @@
 
     lax.fori_loop(0, seq_rows // block_rows, attend, 0)
 
-    @pl.when(home)
+    @pl.when(out_moves)
     def _():
-        out_home.wait()
-
-    @pl.when(jnp.logical_not(home))
+        out_last.wait_recv()
+
+    @pl.when(jnp.logical_not(out_moves))
     def _():
-        out_slot.wait_recv()
-
-    for src, dst in (
-        (qkv, qkv_out),
+        out_stays.wait()
+
+    for src, dst in (        (qkv, qkv_out),
         (attended, attended_out),
         (w_head, w_head_out),
         (out_head, out_head_out),
@@ -711,54 +772,55 @@
         )
         part[pl.ds(chip * 2, 2)] = out.astype(bf16).reshape(2, rows, width)
         scatter.give(flip, chip)
-    mid = tokens_ref[...].astype(f32) + scatter.run()
+
+    def arrived(flip):
+        for copy in strip_copies[flip]:
+            copy.wait_recv()
+        weights[flip].begin()
+
+    scatter.begin()
+    scatter.middle()
+    mid = tokens_ref[...].astype(f32) + scatter.finish()
     mid_ref[...] = mid
     mid_scale = lax.rsqrt(jnp.mean(mid * mid, axis=-1, keepdims=True) + norm_eps)
     normed_two[...] = (mid * mid_scale * gain_two_ref[...]).astype(bf16)
 
-    group_rows = pl.ds(pl.multiple_of(fsdp * rows, rows), rows)
-    group_copies = []
-    for source, dest in ((normed_two, normed_two_group), (cot_ref, cot_group)):
-        for flip in (1, 2, 3):
-            group_copies.append(links.column(source, dest.at[group_rows], flip))
-        finals.append(links.here(source, dest.at[group_rows]))
-        finals[-1].start()
-    for copy in group_copies:
-        copy.start()
-
-    for copy in own_strips:
+    group = LineGather(links, normed_two, normed_two_group)
+    cot_copies = [links.column(cot_ref, cot_far, 2), links.column(cot_ref, cot_near, 1)]
+    group.begin()
+    start_all(cot_copies)
+    arrived(1)
+    arrived(2)
+    weights[1].forward()
+    arrived(3)
+    weights[2].forward()
+    weights[1].finish()
+    group.forward()
+    weights[3].forward()
+    weights[2].finish()
+    weights[3].finish()
+    group.finish()
+    for copy in cot_copies:
         copy.wait()
-    for copy in strip_copies:
-        copy.wait_recv()
-
-    def columns_of(j):
-        place = pl.ds(pl.multiple_of(j * strip, strip), strip)
-        return [gate_w.at[:, :, place], up_w.at[:, :, place]]
-
-    def halves_of(j, which):
-        place = pl.ds(pl.multiple_of(j * strip, strip), strip)
-        blocks = gate_w.shape[0] // 2
-        some = pl.ds(which * blocks, blocks)
-        return [gate_w.at[some, :, place], up_w.at[some, :, place]]
-
-    weights = PlaneGather(links, columns_of, halves_of)
-    weights.begin()
-    weights.forward()
-    weights.finish()
-
-    for copy in group_copies:
-        copy.wait_recv()
-    for copy in head_copies + strip_copies + group_copies:
-        copy.wait_send()
-    for wanted, copy in out_sends:
-
-        @pl.when(wanted)
-        def _(copy=copy):
+    for copy in strip_copies[0]:
+        copy.wait()
+
+    for copies in [head_far, head_near, [head_relay]] + strip_copies[1:]:
+        for copy in copies:
             copy.wait_send()
+
+    @pl.when(out_away)
+    def _():
+        out_copy.wait_send()
+
+    @pl.when(out_moves)
+    def _():
+        out_last.wait_send()
 
     gather.drain()
     scatter.drain()
-    weights.drain()
+    for item in weights:
+        item.drain()
     for copy in finals:
         copy.wait()
 
@@ -781,8 +843,9 @@
         name="attention_forward",
         out_shape=[
             shape((rows, width), f32),
-            shape((n_fsdp * rows, width), bf16),
-            shape((n_fsdp * rows, width), bf16),
+            shape((n_fsdp, rows, width), bf16),
+            shape((rows, width), bf16),
+            shape((rows, width), bf16),
             shape((width // BLOCK, BLOCK, hidden), bf16),
             shape((width // BLOCK, BLOCK, hidden), bf16),
             shape((seq_rows, all_columns), bf16),
@@ -792,10 +855,11 @@
             shape((head_columns, width), bf16),
         ],
         in_specs=[vmem] * 4 + [hbm] * 4 + [vmem] * 4,
-        out_specs=[vmem] + [hbm] * 9,
+        out_specs=[vmem] + [hbm] * 10,
         scratch_shapes=[
             pltpu.VMEM((n_ctx, rows, width), bf16),
             pltpu.VMEM((width, all_columns), bf16),
+            pltpu.VMEM((head_columns, width), bf16),
             pltpu.VMEM((head_columns, width), bf16),
             pltpu.VMEM((seq_rows, all_columns), bf16),
             pltpu.VMEM((seq_rows, head_columns), bf16),
@@ -804,9 +868,9 @@
             pltpu.VMEM((2, rows // 2, width), bf16),
             pltpu.VMEM((2, rows, width), bf16),
             pltpu.VMEM((rows, width), bf16),
-            pltpu.SemaphoreType.DMA((80,)),
-            pltpu.SemaphoreType.DMA((80,)),
-            pltpu.SemaphoreType.DMA((24,)),
+            pltpu.SemaphoreType.DMA((112,)),
+            pltpu.SemaphoreType.DMA((112,)),
+            pltpu.SemaphoreType.DMA((16,)),
         ],
         compiler_params=pltpu.CompilerParams(
             collective_id=1, has_side_effects=True, vmem_limit_bytes=58 * 2**20
@@ -838,8 +902,8 @@
         self.sent.append(copy)
         return copy
 
-    def begin(self):
-        corner = self.part(lax.bitwise_xor(self.chip, 3))
+    def begin(self, source=None):
+        corner = (source or self.part)(lax.bitwise_xor(self.chip, 3))
         half = corner.shape[0] // 2
         self.half = half
         self.corner = [
@@ -879,7 +943,8 @@
     cot_ref,
     gain_ref,
     normed_ref,
-    cots_ref,
+    cot_near_ref,
+    cot_far_ref,
     gate_hbm,
     up_hbm,
     down_hbm,
@@ -892,6 +957,7 @@
     gate_v,
     up_v,
     down_v,
+    cots,
     hidden,
     grad_gate,
     grad_up,
@@ -906,18 +972,19 @@
     recv_sem,
     local_sem,
     load_sem,
-    free_sem,
+    down_free,
+    gate_free,
 ):
     f32, bf16 = jnp.float32, jnp.bfloat16
     ctx, fsdp = lax.axis_index("ctx"), lax.axis_index("fsdp")
     links = Links((send_sem, recv_sem, local_sem), ctx, fsdp)
     core = lax.rem(ctx, 2)
     rows, width = mid_ref.shape
-    group_rows = normed_ref.shape[0]
     blocks = gate_v.shape[0]
     hidden_units = blocks * BLOCK
     half_units = hidden_units // 2
-    n_fsdp = group_rows // rows
+    n_fsdp = normed_ref.shape[0]
+    group_rows = n_fsdp * rows
 
     def loads(j):
         cols = pl.ds(pl.multiple_of(j * BLOCK, BLOCK), BLOCK)
@@ -933,157 +1000,215 @@
         for copy in loads(j):
             copy.start()
 
-    greet(ctx, fsdp)
-
-    swaps = [
-        links.plane(normed_ref, other_normed, ACROSS_CORE),
-        links.plane(cots_ref, other_cots, ACROSS_CORE),
-    ]
-    for copy in swaps:
-        copy.start()
+    greet(ctx, fsdp, PLANE_FLIPS + COLUMN_FLIPS[:2])
+
+    cot_relay = links.column(cot_far_ref, cots.at[3], 1)
+    cot_relay.start()
+    cots[0] = cot_ref[...]
+    cots[1] = cot_far_ref[...]
+    cots[2] = cot_near_ref[...]
+
+    swaps = [links.plane(normed_ref, other_normed, ACROSS_CORE)]
+    cot_swaps = [links.plane(cots.at[s], other_cots.at[s], ACROSS_CORE) for s in range(n_fsdp)]
+    start_all(swaps + cot_swaps[:3])
+
+    half_slots, half_rows = n_fsdp // 2, group_rows // 2
 
     def activate(j, carry):
         for copy in loads(j):
             copy.wait()
         cols = pl.ds(pl.multiple_of(j * BLOCK, BLOCK), BLOCK)
-        normed = normed_ref[...]
+        normed = normed_ref[...].reshape(group_rows, width)
         gate = jnp.dot(
             normed, gate_v[:, :, cols].reshape(width, BLOCK), preferred_element_type=f32
         )
         up = jnp.dot(normed, up_v[:, :, cols].reshape(width, BLOCK), preferred_element_type=f32)
-        grad_hidden = contract_last(cots_ref[...], down_v[j])
-        sig = 1.0 / (1.0 + jnp.exp(-gate))
+        sig = jax.nn.sigmoid(gate)
         silu = gate * sig
         hidden[:, cols] = (silu * up).astype(bf16)
-        grad_gate[:, cols] = (grad_hidden * up * (sig * (1.0 + gate * (1.0 - sig)))).astype(bf16)
-        grad_up[:, cols] = (grad_hidden * silu).astype(bf16)
+        grad_gate[:, cols] = (up * (sig * (1.0 + gate * (1.0 - sig)))).astype(bf16)
+        grad_up[:, cols] = silu.astype(bf16)
         return carry
 
     lax.fori_loop(0, blocks, activate, 0)
 
+    piece = 2 * BLOCK
+    pieces = width // piece
+
+    def spot(n):
+        return pl.ds(n * piece, piece)
+
+    def put(which, first, n, value):
+        stage[which, pl.ds(first, half_slots), :, spot(n)] = value.astype(bf16).reshape(
+            half_slots, rows, piece
+        )
+
+    def down_out(first, n):
+        value = jnp.dot(
+            hidden[pl.ds(first * rows, half_rows)],
+            down_v[:, :, spot(n)].reshape(hidden_units, piece),
+            preferred_element_type=f32,
+        )
+        put(0, first, n, value)
+
+    def back_out(first, n):
+        at, some = pl.ds(first * rows, half_rows), pl.ds(n * 2, 2)
+        value = contract_last(grad_gate[at], gate_v[some].reshape(piece, hidden_units))
+        value = value + contract_last(grad_up[at], up_v[some].reshape(piece, hidden_units))
+        put(1, first, n, value)
+
+    near, far = {}, []
+
+    def send_near(which, n):
+        near[which, n] = [
+            links.column(stage.at[which, 3, :, spot(n)], landed.at[which, 1, :, spot(n)], 1),
+            links.column(stage.at[which, 2, :, spot(n)], landed.at[which, 0, :, spot(n)], 1),
+        ]
+        start_all(near[which, n])
+
+    def relay(which, n):
+        near[which, n][0].wait_recv()
+        stage[which, 1, :, spot(n)] = (
+            stage[which, 1, :, spot(n)].astype(f32) + landed[which, 1, :, spot(n)].astype(f32)
+        ).astype(bf16)
+        copy = links.column(stage.at[which, 1, :, spot(n)], landed.at[which, 2, :, spot(n)], 2)
+        copy.start()
+        far.append(copy)
+
+    for n in range(pieces):
+        down_out(half_slots, n)
+        send_near(0, n)
+        down_out(0, n)
+
+    def activation_grads(first):
+        at = pl.ds(first * rows, half_rows)
+
+        def step(j, carry):
+            cols = pl.ds(pl.multiple_of(j * BLOCK, BLOCK), BLOCK)
+            cot_rows = cots[pl.ds(first, half_slots)].reshape(half_rows, width)
+            grad_hidden = contract_last(cot_rows, down_v[j])
+            grad_gate[at, cols] = (grad_gate[at, cols].astype(f32) * grad_hidden).astype(bf16)
+            grad_up[at, cols] = (grad_up[at, cols].astype(f32) * grad_hidden).astype(bf16)
+            return carry
+
+        lax.fori_loop(0, blocks, step, 0)
+
+    hidden_acts = []
+    for pair in range(blocks // 2):
+        cols = pl.ds(pl.multiple_of((2 * pair + 1 - core) * BLOCK, BLOCK), BLOCK)
+        hidden_acts.append(
+            links.plane(
+                hidden.at[:, cols], other_hidden.at[:, pl.ds(pair * BLOCK, BLOCK)], ACROSS_CORE
+            )
+        )
+    start_all(hidden_acts)
+    activation_grads(0)
+    cot_relay.wait_recv()
+    cot_swaps[3].start()
+    activation_grads(half_slots)
     theirs = pl.ds(pl.multiple_of((1 - core) * half_units, half_units), half_units)
     acts = [
         links.plane(grad_gate.at[:, theirs], other_gate, ACROSS_CORE),
         links.plane(grad_up.at[:, theirs], other_up, ACROSS_CORE),
     ]
-    for pair in range(blocks // 2):
-        cols = pl.ds(pl.multiple_of((2 * pair + 1 - core) * BLOCK, BLOCK), BLOCK)
-        acts.append(
-            links.plane(
-                hidden.at[:, cols], other_hidden.at[:, pl.ds(pair * BLOCK, BLOCK)], ACROSS_CORE
+    start_all(acts)
+
+    def free(sem):
+        for flip in (ACROSS_X, ACROSS_Y):
+            pl.semaphore_signal(
+                sem,
+                inc=1,
+                device_id=(lax.bitwise_xor(ctx, flip), fsdp),
+                device_id_type=MESH,
             )
-        )
-    for copy in acts:
-        copy.start()
-
-    piece = 2 * BLOCK
-    group = []
-    for n in range(width // piece):
-        cols = pl.ds(n * piece, piece)
-        some = pl.ds(n * 2, 2)
-        back = contract_last(grad_gate[...], gate_v[some].reshape(piece, hidden_units))
-        back = back + contract_last(grad_up[...], up_v[some].reshape(piece, hidden_units))
-        stage[1, :, :, cols] = back.astype(bf16).reshape(n_fsdp, rows, piece)
-        down = jnp.dot(
-            hidden[...],
-            down_v[:, :, cols].reshape(hidden_units, piece),
-            preferred_element_type=f32,
-        )
-        stage[0, :, :, cols] = down.astype(bf16).reshape(n_fsdp, rows, piece)
-        for which in (1, 0):
-            for flip in (1, 2, 3):
-                target = lax.bitwise_xor(fsdp, flip)
-                copy = links.column(
-                    stage.at[which, target, :, cols], landed.at[which, flip - 1, :, cols], flip
-                )
-                copy.start()
-                group.append(copy)
-
-    for flip in (ACROSS_X, ACROSS_Y):
-        pl.semaphore_signal(
-            free_sem,
-            inc=1,
-            device_id=(lax.bitwise_xor(ctx, flip), fsdp),
-            device_id_type=MESH,
-        )
-
-    def rows_dot(left, right):
-        return lax.dot_general(
-            left, right, (((0,), (0,)), ((), ())), preferred_element_type=f32
-        )
+
+    free(down_free)
+
+    def flat(ref, cols):
+        return ref[:, :, cols].reshape(group_rows, -1)
+
+    for copy in cot_swaps + hidden_acts:
+        copy.wait_recv()
+
+    def down_block(pair, carry):
+        own = pl.ds(pl.multiple_of((2 * pair + core) * BLOCK, BLOCK), BLOCK)
+        other = pl.ds(pl.multiple_of(pair * BLOCK, BLOCK), BLOCK)
+        left, right = hidden[:, own].T, other_hidden[:, other].T
+        for cols in (pl.ds(0, width // 2), pl.ds(width // 2, width // 2)):
+            total = jnp.dot(left, flat(cots, cols), preferred_element_type=f32)
+            total = total + jnp.dot(right, flat(other_cots, cols), preferred_element_type=f32)
+            down_v[pair, :, cols] = total.astype(bf16)
+        return carry
+
+    lax.fori_loop(0, blocks // 2, down_block, 0)
+    pl.semaphore_wait(down_free, 2)
+
+    def scatter_in(place):
+        corner = place.at[4]
+        return ChipScatter(
+            links,
+            lambda chip: place.at[chip],
+            [corner.at[pl.ds(0, BLOCK // 2)], corner.at[pl.ds(BLOCK // 2, BLOCK // 2)]],
+            [place.at[5], place.at[6]],
+        )
+
+    down_scatter = scatter_in(down_v)
+    down_scatter.begin()
+    for n in range(pieces):
+        back_out(half_slots, n)
+        send_near(1, n)
+    for n in range(pieces):
+        back_out(0, n)
+    free(gate_free)
+    relay(0, 0)
+    relay(0, 1)
+
+    mine = pl.ds(pl.multiple_of(core * half_units, half_units), half_units)
+
+    def weight_block(b, carry):
+        cols = pl.ds(pl.multiple_of(b * BLOCK, BLOCK), BLOCK)
+        left, right = flat(normed_ref, cols).T, flat(other_normed, cols).T
+        plane, chip = b // 2, 2 * lax.rem(b, 2)
+        at_row = pl.ds(pl.multiple_of((plane // 2) * (BLOCK // 2), BLOCK // 2), BLOCK // 2)
+        at_col = pl.ds(pl.multiple_of(lax.rem(plane, 2) * (width // 2), width // 2), width // 2)
+        for own_grad, other_grad, place in (
+            (grad_gate, other_gate, gate_v),
+            (grad_up, other_up, up_v),
+        ):
+            total = jnp.dot(left, own_grad[:, mine], preferred_element_type=f32)
+            total = total + jnp.dot(right, other_grad[...], preferred_element_type=f32)
+            low = total.astype(bf16)
+            place[chip, at_row, at_col] = low[: BLOCK // 2]
+            place[chip + 1, at_row, at_col] = low[BLOCK // 2 :]
+        return carry
 
     for copy in swaps + acts:
         copy.wait_recv()
-    down_rows = 4
-
-    def down_block(step, carry):
-        pair, part = step // 2, lax.rem(step, 2)
-        cols = pl.ds(pl.multiple_of(part * (width // 2), width // 2), width // 2)
-        own = pl.ds(pl.multiple_of((2 * pair + core) * BLOCK, BLOCK), BLOCK)
-        other = pl.ds(pl.multiple_of(pair * BLOCK, BLOCK), BLOCK)
-        total = rows_dot(hidden[:, own], cots_ref[:, cols]) + rows_dot(
-            other_hidden[:, other], other_cots[:, cols]
-        )
-        gate_v[pair, :, cols] = total.astype(bf16)
-        return carry
-
-    lax.fori_loop(0, blocks, down_block, 0)
-    pl.semaphore_wait(free_sem, 2)
-    down_scatter = ChipScatter(
-        links,
-        lambda chip: gate_v.at[chip],
-        [down_v.at[0, pl.ds(0, BLOCK // 2)], down_v.at[0, pl.ds(BLOCK // 2, BLOCK // 2)]],
-        [down_v.at[1], down_v.at[2]],
-    )
-    down_scatter.begin()
-
-    mine = pl.ds(pl.multiple_of(core * half_units, half_units), half_units)
-
-    def gradient_into(own_grad, other_grad, place):
-        def block(b, carry):
-            cols = pl.ds(pl.multiple_of(b * BLOCK, BLOCK), BLOCK)
-            total = rows_dot(normed_ref[:, cols], own_grad[:, mine]) + rows_dot(
-                other_normed[:, cols], other_grad[...]
-            )
-            low = total.astype(bf16)
-            plane, chip = b // 2, 2 * lax.rem(b, 2)
-            at_row = pl.ds(pl.multiple_of((plane // 2) * (BLOCK // 2), BLOCK // 2), BLOCK // 2)
-            at_col = pl.ds(
-                pl.multiple_of(lax.rem(plane, 2) * (width // 2), width // 2), width // 2
-            )
-            place[chip, at_row, at_col] = low[: BLOCK // 2]
-            place[chip + 1, at_row, at_col] = low[BLOCK // 2 :]
-            return carry
-
-        lax.fori_loop(0, blocks, block, 0)
-
-    gate_place = gate_v.at[pl.ds(4, 4)]
-    gradient_into(grad_gate, other_gate, gate_place)
-    gate_scatter = ChipScatter(
-        links,
-        lambda chip: gate_v.at[4 + chip],
-        [down_v.at[3, pl.ds(0, BLOCK // 2)], down_v.at[3, pl.ds(BLOCK // 2, BLOCK // 2)]],
-        [down_v.at[4], down_v.at[5]],
-    )
+    lax.fori_loop(0, blocks // 2, weight_block, 0)
+    relay(0, 2)
     down_scatter.middle()
+    lax.fori_loop(blocks // 2, blocks, weight_block, 0)
+    pl.semaphore_wait(gate_free, 2)
+    gate_scatter = scatter_in(gate_v)
     gate_scatter.begin()
-    up_place = up_v.at[pl.ds(0, 4)]
-    gradient_into(grad_up, other_up, up_place)
-    up_copy = links.here(up_place, up_part)
+    up_copy = links.here(up_v.at[pl.ds(0, 4)], up_part)
     up_copy.start()
+    relay(0, 3)
+    relay(1, 0)
+    relay(1, 1)
+    relay(1, 2)
+    relay(1, 3)
     gate_scatter.middle()
     down_copy = links.here(down_scatter.finish(), down_sum)
     down_copy.start()
 
-    for copy in group:
+    for copy in [pair[1] for pair in near.values()] + far:
         copy.wait_recv()
     mid = mid_ref[...]
     sums = []
     for which in (0, 1):
-        total = stage[which, fsdp].astype(f32)
-        for slot in range(n_fsdp - 1):
-            total = total + landed[which, slot].astype(f32)
-        sums.append(total)
+        total = stage[which, 0].astype(f32) + landed[which, 0].astype(f32)
+        sums.append(total + landed[which, 2].astype(f32))
     result_ref[...] = (mid + sums[0]).astype(bf16)
     scale = lax.rsqrt(jnp.mean(mid * mid, axis=-1, keepdims=True) + norm_eps)
     u = sums[1] * gain_ref[...]
@@ -1094,7 +1219,8 @@
 
     gate_copy = links.here(gate_scatter.finish(), gate_sum)
     gate_copy.start()
-    for copy in swaps + acts + group:
+    sent = [copy for pair in near.values() for copy in pair] + far + swaps + cot_swaps
+    for copy in sent + hidden_acts + acts + [cot_relay]:
         copy.wait_send()
     down_scatter.drain()
     gate_scatter.drain()
@@ -1102,11 +1228,13 @@
         copy.wait()
 
 
-def feed_forward(mid, cotangent, gain_ffn, normed_group, cot_group, gate_w, up_w, w_down):
+def feed_forward(
+    mid, cotangent, gain_ffn, normed_group, cot_near, cot_far, gate_w, up_w, w_down
+):
     f32, bf16 = jnp.float32, jnp.bfloat16
     n_fsdp = lax.axis_size("fsdp")
     rows, width = mid.shape
-    group_rows = normed_group.shape[0]
+    group_rows = n_fsdp * rows
     units = w_down.shape[0] * BLOCK
     blocks = units // BLOCK
     vmem, hbm = pl.BlockSpec(memory_space=pltpu.VMEM), pl.BlockSpec(memory_space=pl.ANY)
@@ -1122,17 +1250,18 @@
             shape((BLOCK, width), bf16),
             shape((blocks // 2, BLOCK, width), bf16),
         ],
-        in_specs=[vmem] * 5 + [hbm] * 3,
+        in_specs=[vmem] * 6 + [hbm] * 3,
         out_specs=[vmem] * 3 + [hbm] * 3,
         scratch_shapes=[
             pltpu.VMEM((width // BLOCK, BLOCK, units), bf16),
             pltpu.VMEM((width // BLOCK, BLOCK, units), bf16),
             pltpu.VMEM((blocks, BLOCK, width), bf16),
+            pltpu.VMEM((n_fsdp, rows, width), bf16),
             pltpu.VMEM((group_rows, units), bf16),
             pltpu.VMEM((group_rows, units), bf16),
             pltpu.VMEM((group_rows, units), bf16),
-            pltpu.VMEM((group_rows, width), bf16),
-            pltpu.VMEM((group_rows, width), bf16),
+            pltpu.VMEM((n_fsdp, rows, width), bf16),
+            pltpu.VMEM((n_fsdp, rows, width), bf16),
             pltpu.VMEM((group_rows, units // 2), bf16),
             pltpu.VMEM((group_rows, units // 2), bf16),
             pltpu.VMEM((group_rows, units // 2), bf16),
@@ -1143,11 +1272,12 @@
             pltpu.SemaphoreType.DMA((8,)),
             pltpu.SemaphoreType.DMA((3, blocks)),
             pltpu.SemaphoreType.REGULAR,
+            pltpu.SemaphoreType.REGULAR,
         ],
         compiler_params=pltpu.CompilerParams(
             collective_id=2, has_side_effects=True, vmem_limit_bytes=62 * 2**20
         ),
-    )(mid, cotangent, gain_ffn[None], normed_group, cot_group, gate_w, up_w, w_down)
+    )(mid, cotangent, gain_ffn[None], normed_group, cot_near, cot_far, gate_w, up_w, w_down)
 
 
 def attention_back_kernel(
@@ -1186,7 +1316,9 @@
     side_rx,
     out_stage,
     out_landed,
+    out_summed,
     head_stage,
+    head_summed,
     head_landed,
     send_sem,
     recv_sem,
@@ -1206,16 +1338,8 @@
     for copy in loads:
         copy.start()
 
-    flips = [(a, b) for a in range(n_ctx) for b in range(n_fsdp) if a or b]
-    barrier = pltpu.get_barrier_semaphore()
-    for a, b in flips:
-        pl.semaphore_signal(
-            barrier,
-            inc=1,
-            device_id=(lax.bitwise_xor(ctx, a), lax.bitwise_xor(fsdp, b)),
-            device_id_type=MESH,
-        )
-    pl.semaphore_wait(barrier, len(flips))
+    flips = [(a, 0) for a in range(1, n_ctx)] + COLUMN_FLIPS + [(1, b) for b in (1, 2, 3)]
+    greet(ctx, fsdp, flips)
 
     proj[ctx] = grad_proj_ref[...]
     half = rows // 2
@@ -1253,16 +1377,15 @@
         return copies
 
     locals_ = []
-    gate_copies = spread(gate_sum_hbm, gate_out)
-    gather.forward()
-    loads[1].wait()
     up_scatter = ChipScatter(
         links,
         lambda q: up_part.at[q],
         [up_halves.at[0], up_halves.at[1]],
         [up_sides.at[0], up_sides.at[1]],
     )
-    up_scatter.begin()
+    gate_copies = spread(gate_sum_hbm, gate_out)
+    gather.forward()
+    up_scatter.begin(lambda q: up_part_hbm.at[q])
     gather.finish()
 
     total = jnp.zeros((head_columns, width), f32)
@@ -1276,38 +1399,70 @@
     out_stage[...] = total.astype(bf16).reshape(out_stage.shape)
     half_ctx = n_ctx // 2
     out_base = links.remote
-    links.remote += n_fsdp
+    links.remote += half_ctx
     out_copies = []
-    plane = out_plane(ctx, fsdp)
     for j in range(half_ctx):
         target = half_ctx * core + j
-        away = (target != ctx) | (plane != fsdp)
-        index = links.remote
-        links.remote += 1
         copy = pltpu.make_async_remote_copy(
             src_ref=out_stage.at[j],
-            dst_ref=out_landed.at[fsdp],
-            send_sem=send_sem.at[index],
-            recv_sem=recv_sem.at[out_base + fsdp],
-            device_id=(target, plane),
+            dst_ref=out_landed.at[chip],
+            send_sem=send_sem.at[out_base + j],
+            recv_sem=recv_sem.at[out_base + chip],
+            device_id=(target, fsdp),
             device_id_type=MESH,
         )
-        out_copies.append((away, copy))
-
-        @pl.when(away)
+        out_copies.append((target != ctx, copy))
+
+        @pl.when(target != ctx)
         def _(copy=copy):
             copy.start()
 
-    def out_source(source):
-        head = 2 * fsdp + ctx // half_ctx
-        return head_of(head, jnp.int32(source))
-
-    own_out = links.here(out_stage.at[lax.rem(ctx, half_ctx)], out_landed.at[fsdp])
-    own_is_mine = out_source(fsdp) == ctx
-
-    @pl.when(own_is_mine)
+    own_out = links.here(out_stage.at[lax.rem(ctx, half_ctx)], out_landed.at[chip])
+    out_own_chip = lax.rem(ctx, 2) == ctx // half_ctx
+
+    @pl.when(out_own_chip)
     def _():
         own_out.start()
+
+    def out_arrivals():
+        for source in range(half_ctx):
+            arrival = pltpu.make_async_remote_copy(
+                src_ref=out_stage.at[0],
+                dst_ref=out_landed.at[source],
+                send_sem=send_sem.at[out_base],
+                recv_sem=recv_sem.at[out_base + source],
+                device_id=(lax.bitwise_xor(ctx, 1), fsdp),
+                device_id_type=MESH,
+            )
+
+            @pl.when(2 * source + ctx // half_ctx != ctx)
+            def _(arrival=arrival):
+                arrival.wait_recv()
+
+        @pl.when(out_own_chip)
+        def _():
+            own_out.wait()
+
+    def out_begin():
+        out_arrivals()
+        copies = [
+            links.column(
+                out_landed.at[lax.bitwise_xor(fsdp, flip)], out_summed.at[slot], 1
+            )
+            for flip, slot in ((3, 1), (1, 0))
+        ]
+        start_all(copies)
+        return copies
+
+    def out_relay(copies):
+        copies[0].wait_recv()
+        across = lax.bitwise_xor(fsdp, 2)
+        out_landed[across] = (
+            out_landed[across].astype(f32) + out_summed[1].astype(f32)
+        ).astype(bf16)
+        copy = links.column(out_landed.at[across], out_summed.at[2], 2)
+        copy.start()
+        return copy
 
     def back(step, carry):
         at = pl.multiple_of(step * 2 * rows, 2 * rows)
@@ -1320,13 +1475,14 @@
     key_grad[...] = jnp.zeros_like(key_grad)
     value_grad[...] = jnp.zeros_like(value_grad)
 
-    def attend(step, carry):
-        at = pl.ds(pl.multiple_of(step * 2 * rows, 2 * rows), 2 * rows)
-        keys = qkv_ref[:, pl.ds(head_columns, HEAD_SIZE)]
-        values = qkv_ref[:, pl.ds(head_columns + HEAD_SIZE, HEAD_SIZE)]
-        causal = pos_row_ref[...] <= pos_col_ref[at]
-        for column in range(0, head_columns, HEAD_SIZE):
-            cols = pl.ds(column, HEAD_SIZE)
+    def attend_head(column):
+        cols = pl.ds(column, HEAD_SIZE)
+
+        def step(index, carry):
+            at = pl.ds(pl.multiple_of(index * 2 * rows, 2 * rows), 2 * rows)
+            keys = qkv_ref[:, pl.ds(head_columns, HEAD_SIZE)]
+            values = qkv_ref[:, pl.ds(head_columns + HEAD_SIZE, HEAD_SIZE)]
+            causal = pos_row_ref[...] <= pos_col_ref[at]
             query, grad_mixed = qkv_ref[at, cols], grad_att[at, cols]
             scores = contract_last(query, keys) * score_scale
             scores = jnp.where(causal, scores, -1e30)
@@ -1339,12 +1495,61 @@
             key_grad[...] += contract_first(grad_scores, query)
             grad_query = jnp.dot(grad_scores, keys, preferred_element_type=f32) * score_scale
             grads[at, cols] = turn(grad_query, cos_ref[at], sin_ref[at], -1.0).astype(bf16)
-        return carry
-
-    lax.fori_loop(0, n_ctx // 2, attend, 0)
+            return carry
+
+        lax.fori_loop(0, n_ctx // 2, step, 0)
+
+    depth = n_ctx * strip_rows
+    head_near, head_far = [], []
+
+    def head_part(cols, slot):
+        flip = (0, 2, 1, 3)[slot]
+        places = pl.ds(pl.multiple_of(lax.bitwise_xor(fsdp, flip) * depth, depth), depth)
+        total = contract_first(normed[:, :, places].reshape(seq_rows, depth), grads[:, cols])
+        head_stage[slot, :, :, cols] = total.astype(bf16).reshape(n_ctx, strip_rows, -1)
+
+    def head_begin(cols):
+        copies = []
+        for slot in (3, 2):
+            head_part(cols, slot)
+            copy = links.flip(
+                head_stage.at[slot, :, :, cols],
+                head_summed.at[slot - 2, :, :, cols],
+                0,
+                1,
+            )
+            copy.start()
+            copies.append(copy)
+        head_near.append(copies)
+        for slot in (1, 0):
+            head_part(cols, slot)
+
+    def head_relay(index, cols):
+        head_near[index][0].wait_recv()
+        head_stage[1, :, :, cols] = (
+            head_stage[1, :, :, cols].astype(f32) + head_summed[1, :, :, cols].astype(f32)
+        ).astype(bf16)
+        copy = links.flip(
+            head_stage.at[1, :, :, cols], head_summed.at[2, :, :, cols], 0, 2
+        )
+        copy.start()
+        head_far.append(copy)
+
+    first_cols = pl.ds(0, HEAD_SIZE)
+    rest_cols = pl.ds(HEAD_SIZE, grads.shape[1] - HEAD_SIZE)
+    attend_head(0)
+    loads[1].wait()
+    up_scatter.middle()
+    out_near = out_begin()
+    loads[0].wait()
+    head_begin(first_cols)
+    for column in range(HEAD_SIZE, head_columns, HEAD_SIZE):
+        attend_head(column)
+    out_far = out_relay(out_near)
     turned = turn(key_grad[...] * score_scale, cos_ref[...], sin_ref[...], -1.0)
     grads[:, pl.ds(head_columns, HEAD_SIZE)] = turned.astype(bf16)
     grads[:, pl.ds(head_columns + HEAD_SIZE, HEAD_SIZE)] = value_grad[...].astype(bf16)
+    head_begin(rest_cols)
 
     scatter = PlaneScatter(links, part, core_rx, half_rx, side_rx)
     for flip, q in scatter.order():
@@ -1353,33 +1558,12 @@
         part[pl.ds(2 * q, 2)] = out.astype(bf16).reshape(2, rows, width)
         scatter.give(flip, q)
 
-    loads[0].wait()
-    depth = n_ctx * strip_rows
-    head_copies = []
-    for b in (2, 1, 3, 0):
-        plane = lax.bitwise_xor(fsdp, b)
-        cols = pl.ds(pl.multiple_of(plane * depth, depth), depth)
-        total = lax.dot_general(
-            normed[:, :, cols].reshape(seq_rows, depth),
-            grads[...],
-            (((0,), (0,)), ((), ())),
-            preferred_element_type=f32,
-        )
-        head_stage[plane] = total.astype(bf16).reshape(n_ctx, strip_rows, -1)
-        for a in range(n_ctx):
-            target = lax.bitwise_xor(ctx, a)
-            if a or b:
-                copy = links.to(
-                    head_stage.at[plane, target], head_landed.at[ctx, fsdp], target, plane
-                )
-                head_copies.append(copy)
-            else:
-                copy = links.here(head_stage.at[plane, target], head_landed.at[ctx, fsdp])
-                locals_.append(copy)
-            copy.start()
-
-    up_scatter.middle()
-    grad_normed = scatter.run()
+    scatter.begin()
+    head_relay(0, first_cols)
+    scatter.middle()
+    head_relay(1, rest_cols)
+    up_copies = spread(up_scatter.finish(), up_out)
+    grad_normed = scatter.finish()
     inputs = tokens_ref[...].astype(f32)
     scale = lax.rsqrt(jnp.mean(inputs * inputs, axis=-1, keepdims=True) + norm_eps)
     u = grad_normed * gain_ref[...]
@@ -1387,31 +1571,25 @@
     grad_input_ref[...] = (
         grad_mid_ref[...] + scale * u - inputs * (scale * scale * scale * inner)
     )
-    up_copies = spread(up_scatter.finish(), up_out)
-
-    for source in range(n_fsdp):
-        arrival = pltpu.make_async_remote_copy(
-            src_ref=out_stage.at[0],
-            dst_ref=out_landed.at[source],
-            send_sem=send_sem.at[out_base],
-            recv_sem=recv_sem.at[out_base + source],
-            device_id=(lax.bitwise_xor(ctx, 1), fsdp),
-            device_id_type=MESH,
-        )
-        outside = (out_source(source) != ctx) | (fsdp != source)
-
-        @pl.when(outside)
-        def _(arrival=arrival):
-            arrival.wait_recv()
-
-    @pl.when(own_is_mine)
-    def _():
-        own_out.wait()
-
-    total = out_landed[0].astype(f32)
-    for source in range(1, n_fsdp):
-        total = total + out_landed[source].astype(f32)
-    out_sum[...] = total
+    for copy in [pair[1] for pair in head_near] + head_far:
+        copy.wait_recv()
+    head_stage[0] = (
+        head_stage[0].astype(f32) + head_summed[0].astype(f32) + head_summed[2].astype(f32)
+    ).astype(bf16)
+    head_copies = [
+        links.plane(
+            head_stage.at[0, lax.bitwise_xor(ctx, a)], head_landed.at[ctx], a
+        )
+        for a in range(1, n_ctx)
+    ]
+    start_all(head_copies)
+    head_landed[ctx] = head_stage[0, ctx]
+
+    for copy in (out_near[1], out_far):
+        copy.wait_recv()
+    out_sum[...] = (
+        out_landed[fsdp].astype(f32) + out_summed[0].astype(f32) + out_summed[2].astype(f32)
+    )
     for copy in head_copies:
         copy.wait_recv()
     for copy in locals_:
@@ -1419,9 +1597,7 @@
     query_columns = QUERY_HEADS * HEAD_SIZE
     key_columns = KEY_VALUE_HEADS * HEAD_SIZE
     for head in range(KEY_VALUE_HEADS):
-        total = head_landed[head, 0].astype(f32)
-        for source in range(1, n_fsdp):
-            total = total + head_landed[head ^ (4 * (source % 2)), source].astype(f32)
+        total = head_landed[head].astype(f32)
         qkv_sum[:, pl.ds(head * head_columns, head_columns)] = total[:, :head_columns]
         qkv_sum[:, pl.ds(query_columns + head * HEAD_SIZE, HEAD_SIZE)] = total[
             :, head_columns : head_columns + HEAD_SIZE
@@ -1431,7 +1607,9 @@
         ]
     for copy in gate_copies + up_copies:
         copy.wait_recv()
-    for copy in gate_copies + up_copies + head_copies:
+    for copy in gate_copies + up_copies + head_copies + head_far + head_near[0] + head_near[1]:
+        copy.wait_send()
+    for copy in out_near + [out_far]:
         copy.wait_send()
     for away, copy in out_copies:
 
@@ -1496,8 +1674,10 @@
             pltpu.VMEM((2, rows, width), bf16),
             pltpu.VMEM((n_ctx // 2, strip_rows, width), bf16),
             pltpu.VMEM((n_fsdp, strip_rows, width), bf16),
+            pltpu.VMEM((n_fsdp - 1, strip_rows, width), bf16),
             pltpu.VMEM((n_fsdp, n_ctx, strip_rows, all_columns), bf16),
-            pltpu.VMEM((n_ctx, n_fsdp, strip_rows, all_columns), bf16),
+            pltpu.VMEM((n_fsdp - 1, n_ctx, strip_rows, all_columns), bf16),
+            pltpu.VMEM((n_ctx, strip_rows, all_columns), bf16),
             pltpu.SemaphoreType.DMA((96,)),
             pltpu.SemaphoreType.DMA((96,)),
             pltpu.SemaphoreType.DMA((8,)),
@@ -1553,7 +1733,8 @@
     (
         mid,
         normed_two_group,
-        cot_group,
+        cot_near,
+        cot_far,
         gate_w,
         up_w,
         qkv,
@@ -1579,7 +1760,8 @@
         cotangent,
         gain_ffn,
         normed_two_group,
-        cot_group,
+        cot_near,
+        cot_far,
         gate_w,
         up_w,
         w_down.reshape(-1, BLOCK, width),
@@ -1632,7 +1814,8 @@
 
 
 def solution(mesh):
-    local = local_heads if mesh.shape["ctx"] == KEY_VALUE_HEADS else local_general
+    fits = mesh.shape["ctx"] == KEY_VALUE_HEADS and mesh.shape["fsdp"] == KEY_VALUE_HEADS // 2
+    local = local_heads if fits else local_general
     return jax.shard_map(
         local,
         mesh=mesh,

time: 527 us -> 443 us (0.84); the launches traced: 517 us -> 438 us
  Pallas kernels: 490 us -> 409 us
    pallas_call x1, Pallas kernels: 221 us -> 171 us  [attention_forward(): pl.pallas_call(attention_kernel, name='attention_forward', out_shape=[sha...]
    pallas_call x1, Pallas kernels: 151 us -> 121 us  [attention_back(): pl.pallas_call(attention_back_kernel, name='attention_back', out_shape=[s...]
where the time goes in v4:
time: 443 us; the launch traced here: 438 us
  Pallas kernels  409 us (92%)
  other arithmetic  15.1 us (3%)
  local copies, waits for them, and re-layouts  5.66 us (1%)
  starting transfers between devices  5.48 us (1%)
    pallas_call x1, Pallas kernels, attention_forward(): pl.pallas_call(attention_kernel, name='attention_forward', out_shape=[sha...  171 us
    pallas_call x1, Pallas kernels, attention_back(): pl.pallas_call(attention_back_kernel, name='attention_back', out_shape=[s...  121 us
    pallas_call x1, Pallas kernels, feed_forward(): pl.pallas_call(feed_forward_kernel, name='feed_forward', out_shape=[shape...  116 us
  transfers between devices with their start and end apart: 1, of which 1 were waited for; matrix products, arithmetic and copies ran while one was open for 0% of the time, Pallas kernels for 0%

profile of v4, /device:TPU:5, one launch (start us, length us, event | category | flops | bytes accessed | tf_op | source)
XLA Modules:
  0.0 438.5 jit_solution(13183068153357023905)
XLA Ops:
  0.7 0.7 broadcast_subtract_fusion
  1.3 0.7 multiply_add_fusion
  2.1 1.0 copy.19.pos_col_ref
  3.1 1.9 fusion
  5.0 1.3 pad_maximum_fusion
  6.3 0.0 copy-done.5
  6.3 171.4 %attention_forward.1 = (f32[128,2048]{1,0:T(8,128)}, bf16[4,128,2048]{2,1,0:T(8,128)(2,1)}, bf16[128,2048]{1,0:T(8,128)(2,1)}, bf16[128,2048]{1,0:T(8,128)(2,1)}...) custom-call(bf16[128,2048]{1,0:T(8,128)(2,1)} %tokens_ref.3, ...), custom_call_target="tpu_custom_call" | custom-call | tf_op jit(solution)/shard_map/attention_forward/pallas_call | solution.py:841
  177.7 116.4 %feed_forward.1 = (bf16[128,2048]{1,0:T(8,128)(2,1)}, f32[128,2048]{1,0:T(8,128)}, bf16[128,2048]{1,0:T(8,128)(2,1)}, bf16[256,2048]{1,0:T(8,128)(2,1)}, bf16[25...) custom-call(f32[128,2048]{1,0:T(8,128)} %get-tuple-element.31.mid_ref, bf16[128,2048]{1,0:T(8,128)(2,1)} %cot_ref.3, ...), custom_call_target="tpu_custom_call" | custom-call | tf_op jit(solution)/shard_map/feed_forward/pallas_call | solution.py:1242
  294.1 120.8 %attention_back.1 = (f32[128,2048]{1,0:T(8,128)}, f32[64,4096]{1,0:T(8,128)}, f32[64,2048]{1,0:T(8,128)}, bf16[64,8192]{1,0:T(8,128)(2,1)}, bf16[64,8192]{1,0:T(8,128)(2,1)}) custom-call(bf16[128,2048]{1,0:T(8,128)(2,1)} %get-tuple-element.38.grad_proj_ref, f32[128,2048]{1,0:T(8,128)} %get-tuple-element.39.grad_mid_ref, bf16[128,2048]{1,0:T(8,128)(2,1)} %tokens_ref.3, ...), custom_call_target="tpu_custom_call" | custom-call | tf_op jit(solution)/shard_map/attention_back/pallas_call | solution.py:1649
  414.9 0.0 copy-start.2
  414.9 3.3 multiply_reduce_fusion
  418.3 0.0 copy-done.2
  418.3 0.0 copy-start
  418.3 0.0 copy-start.1
  418.3 3.1 multiply_reduce_fusion.1
  421.4 1.3 multiply_reduce_fusion.2
  422.7 5.5 %collective-permute-start = (f32[2,64]{1,0:T(2,128)S(1)}, f32[2,64]{1,0:T(2,128)S(1)}, u32[]{:S(2)}, u32[]{:S(2)}) collective-permute-start(f32[2,64]{1,0:T(2,128)S(1)} %pad_maximum_fusion.2), channel_id=1, source_target_pairs={{0,0},{1,8},{2,16},{3,24},{4,1},{5,9},{6,17},{7,25},{8,2},{9,10},{... | collective-permute-start | bytes 1544 | tf_op jit(solution)/shard_map/ppermute | solution.py:1799
  428.2 1.6 convert_element_type.35
  429.7 2.6 collective-permute-done
  432.3 1.3 bitcast_divide_fusion
  433.6 1.9 copy.25
  435.5 1.0 copy.26
  436.5 1.0 copy.27
  437.4 0.8 copy.28
  (12 shorter events, 0.0 us)
Async XLA Ops:
  2.1 4.2 copy-start.5
  414.9 3.3 copy-start.2
  418.3 3.1 copy-start
  418.3 9.9 %copy-start.1 = (bf16[256,2048]{1,0:T(8,128)(2,1)S(1)}, bf16[256,2048]{1,0:T(8,128)(2,1)}, u32[]{:S(2)}) copy-start(bf16[256,2048]{1,0:T(8,128)(2,1)} %get-tuple-element.52) | copy-start | bytes 3145732
  422.7 9.6 %collective-permute-start = (f32[2,64]{1,0:T(2,128)S(1)}, f32[2,64]{1,0:T(2,128)S(1)}, u32[]{:S(2)}, u32[]{:S(2)}) collective-permute-start(f32[2,64]{1,0:T(2,128)S(1)} %pad_maximum_fusion.2), channel_id=1, source_target_pairs={{0,0},{1,8},{2,16},{3,24},{4,1},{5,9},{6,17},{7,25},{8,2},{9,10},{... | collective-permute-start | bytes 1544 | tf_op jit(solution)/shard_map/ppermute | solution.py:1799
  428.2 7.3 %copy-start.3 = (f32[128,2048]{1,0:T(8,128)S(1)}, f32[128,2048]{1,0:T(8,128)}, u32[]{:S(2)}) copy-start(f32[128,2048]{1,0:T(8,128)} %get-tuple-element.76) | copy-start | bytes 3145732
  435.5 1.9 copy-start.4
